TPU v7x, 32 devices: a whole 2x2x4 slice. The times are simulated.
32 devices in a mesh: ep: 16 (over z, x, core), dp: 2 (over y).
Axes of the slice: x: 2, y: 2, z: 4, core: 2. Of those that a mesh axis runs over, the one named last changes fastest.
Arguments:
- tokens: bfloat16 [4096, 2048], P(('dp', 'ep')), parts along dimension 0, may hold values from -6 to 6
- expert_ids: int32 [4096, 8], P(('dp', 'ep')), parts along dimension 0, may hold values from 0 to 15, all different within a row; in each aligned block of 128 rows (0 to 127, 128 to 255, ...) at most 72 rows name the same one
- gate_scores: float32 [4096, 8], P(('dp', 'ep')), parts along dimension 0, may hold values from 0.05 to 1
- gate_weight: bfloat16 [32, 2048, 768], P(('dp', 'ep')), parts along dimension 0, may hold values from -0.125 to 0.125
- up_weight: bfloat16 [32, 2048, 768], P(('dp', 'ep')), parts along dimension 0, may hold values from -0.125 to 0.125
- down_weight: bfloat16 [32, 768, 2048], P(('dp', 'ep')), parts along dimension 0, may hold values from -0.21875 to 0.21875
- partner: int32 [16], replicated, may hold values from 0 to 15, as said below
Outputs:
- mixed: bfloat16 [4096, 2048], P(('dp', 'ep')), parts along dimension 0
There are 2 independent parts, one for each index of `dp`. A program takes and returns all parts, laid end to end along the dimension named above; an argument that names none is the same for every part. Nothing has to cross between parts.
Inputs may be any that keep to these rules, and one draw needn't show every extreme that they name: `expert_ids`: each row names 8 different experts; among the 128 rows of one device no expert is named more than 72 times, a bound that some block reaches. A perfect matching: partner[partner[e]] = e and partner[e] != e for every expert e.
All inputs are finite; a program needn't handle non-finite values.
Results may differ from a plain program's by a relative error of at most 0.0059.
Values may be sent and summed in bfloat16 or wider, within the bound.
No kernel may reach another device: no remote copies, remote signals or barrier semaphores. Data moves between devices by JAX's collectives and lax.ppermute only.
A program may use at most 128 MiB of HBM per device.

v0:
```python
import jax
import jax.numpy as jnp
from jax import lax
from jax.sharding import PartitionSpec as P


def expert_rows(inputs, w_gate, w_up, w_down):
    gate_proj = jnp.dot(inputs, w_gate, preferred_element_type=jnp.float32)
    up_proj = jnp.dot(inputs, w_up, preferred_element_type=jnp.float32)
    hidden = (jax.nn.silu(gate_proj) * up_proj).astype(jnp.bfloat16)
    return jnp.dot(hidden, w_down, preferred_element_type=jnp.float32).astype(jnp.bfloat16)


def to_pieces(weights, n_dev):
    return weights.reshape(n_dev, weights.shape[1] // n_dev, weights.shape[2])


def on_device(tokens, expert_ids, gate_scores, gate_weight, up_weight, down_weight, partner):
    n_dev = lax.axis_size("ep")
    experts = partner.shape[0]
    tok_rows, top_k = expert_ids.shape
    model_width = tokens.shape[1]
    mean_rows = tok_rows * top_k // experts
    capacity = min(tok_rows, max(2, mean_rows + mean_rows // 8))
    flat_ids = expert_ids.reshape(-1)
    one_hot = (flat_ids[:, None] == jnp.arange(experts, dtype=jnp.int32)[None, :]).astype(jnp.int32)
    slot_index = jnp.sum(jnp.cumsum(one_hot, 0) * one_hot, 1) - 1
    spread = (
        lax.all_to_all(
            to_pieces(gate_weight, n_dev), "ep", split_axis=0, concat_axis=0, tiled=True
        ),
        lax.all_to_all(to_pieces(up_weight, n_dev), "ep", split_axis=0, concat_axis=0, tiled=True),
        lax.all_to_all(
            to_pieces(down_weight, n_dev), "ep", split_axis=0, concat_axis=0, tiled=True
        ),
    )
    moved = (
        jnp.take(spread[0], partner, axis=0),
        jnp.take(spread[1], partner, axis=0),
        jnp.take(spread[2], partner, axis=0),
    )
    weights_back = (
        lax.all_to_all(moved[0], "ep", split_axis=0, concat_axis=0, tiled=True),
        lax.all_to_all(moved[1], "ep", split_axis=0, concat_axis=0, tiled=True),
        lax.all_to_all(moved[2], "ep", split_axis=0, concat_axis=0, tiled=True),
    )
    used_gate = weights_back[0].reshape(gate_weight.shape)[0]
    used_up = weights_back[1].reshape(up_weight.shape)[0]
    used_down = weights_back[2].reshape(down_weight.shape)[0]
    buffer_index = flat_ids * capacity + slot_index
    row_source = jnp.arange(tok_rows * top_k, dtype=jnp.int32) // top_k
    send_buffer = jnp.zeros((n_dev * capacity, model_width), jnp.bfloat16)
    send_buffer = send_buffer.at[buffer_index].set(tokens[row_source])
    send_buffer = send_buffer.reshape(n_dev, capacity, model_width)
    items = lax.all_to_all(send_buffer, "ep", split_axis=0, concat_axis=0, tiled=True)
    flat_rows = items.reshape(-1, model_width)
    result_rows = expert_rows(flat_rows, used_gate, used_up, used_down).reshape(items.shape)
    returned = lax.all_to_all(result_rows, "ep", split_axis=0, concat_axis=0, tiled=True)
    gathered = returned.reshape(-1, model_width)[buffer_index]
    weighted = (
        gathered.reshape(tok_rows, top_k, model_width).astype(jnp.float32) * gate_scores[:, :, None]
    )
    return jnp.sum(weighted, 1).astype(jnp.bfloat16)


def solution(mesh):
    in_specs = (
        P(("dp", "ep"), None),
        P(("dp", "ep"), None),
        P(("dp", "ep"), None),
        P(("dp", "ep"), None, None),
        P(("dp", "ep"), None, None),
        P(("dp", "ep"), None, None),
        P(),
    )
    out_specs = P(("dp", "ep"), None)
    return jax.shard_map(
        on_device, mesh=mesh, in_specs=in_specs, out_specs=out_specs, check_vma=False
    )
```

profile of v0, /device:TPU:15, one launch (start us, length us, event | category | flops | bytes accessed | tf_op | source)
XLA Modules:
  0.0 702.7 jit_solution(7301698861957219577)
XLA Ops:
  0.0 0.0 copy-start
  0.0 0.0 copy-start.2
  0.0 76.7 %all_to_all.40 = bf16[16,128,768]{2,1,0:T(8,128)(2,1)} all-to-all(bf16[16,128,768]{2,1,0:T(8,128)(2,1)} %bitcast.37), channel_id=1, replica_groups=mesh['ep'=16,'dp'=2] {'ep'}, dimensions={0} | all-to-all | bytes 6291456 | tf_op jit(solution)/shard_map/all_to_all | solution.py:29
  76.7 0.0 copy-done.2
  76.7 74.9 %all_to_all.41 = bf16[16,128,768]{2,1,0:T(8,128)(2,1)} all-to-all(bf16[16,128,768]{2,1,0:T(8,128)(2,1)S(1)} %bitcast.38), channel_id=1, replica_groups=mesh['ep'=16,'dp'=2] {'ep'}, dimensions={0} | all-to-all | bytes 6291456 | tf_op jit(solution)/shard_map/all_to_all | solution.py:32
  151.6 0.0 copy-start.3
  151.6 5.3 all-to-all-start.5
  156.9 0.0 copy-done.3
  156.9 0.1 copy.12
  157.0 0.1 eq.29
  157.1 0.1 eq.25
  157.2 4.5 reduce-window.6
  161.7 0.1 slice.18
  161.8 0.1 copy.14
  162.0 0.1 copy.15
  162.1 0.1 copy.11
  162.2 0.1 mul.36
  162.3 0.1 broadcast_add_fusion
  162.4 0.0 copy-done
  162.4 22.9 %scatter_custom_fusion = bf16[1152,2048]{1,0:T(8,128)(2,1)} fusion(s32[1024]{0:T(1024)S(1)} %bitcast.43, bf16[128,2048]{1,0:T(8,128)(2,1)S(1)} %copy-done, s32[1024]{0:T(1024)S(1)} %broadcast_clamp_fusion.1, bf16[]{:T(256)} %constant.50.clone.1), kind=kCustom, calls=%fused_computation.9 | custom fusion | bytes 4718594 | tf_op jit(solution)/shard_map/scatter | solution.py:53
  185.3 41.6 %all-to-all-done.5 = bf16[16,48,2048]{2,1,0:T(8,128)(2,1)} async-done(((bf16[16,48,2048]{2,1,0:T(8,128)(2,1)}), bf16[16,48,2048]{2,1,0:T(8,128)(2,1)}, u32[]{:S(2)}, u32[]{:S(2)}) %all-to-all-start.5) | async-done | bytes 3145760 | tf_op jit(solution)/shard_map/all_to_all | solution.py:33
  226.9 0.0 copy-start.5
  226.9 5.0 all-to-all-start
  231.9 0.0 copy-done.5
  232.0 4.3 gather_fusion.2
  236.3 4.4 gather_fusion.3
  240.7 6.2 broadcast_select_fusion.1
  246.8 88.8 %all-to-all-done = bf16[16,72,2048]{2,1,0:T(8,128)(2,1)} async-done(((bf16[16,72,2048]{2,1,0:T(8,128)(2,1)}), bf16[16,72,2048]{2,1,0:T(8,128)(2,1)}, u32[]{:S(2)}, u32[]{:S(2)}) %all-to-all-start) | async-done | bytes 4718624 | tf_op jit(solution)/shard_map/all_to_all | solution.py:55
  335.6 74.8 %all_to_all.42 = bf16[16,128,768]{2,1,0:T(8,128)(2,1)} all-to-all(bf16[16,128,768]{2,1,0:T(8,128)(2,1)} %get-tuple-element.6), channel_id=1, replica_groups=mesh['ep'=16,'dp'=2] {'ep'}, dimensions={0} | all-to-all | bytes 6291456 | tf_op jit(solution)/shard_map/all_to_all | solution.py:43
  410.4 5.2 all-to-all-start.4
  415.6 4.2 gather_fusion
  419.9 3.9 broadcast_select_fusion.2
  423.8 61.9 %all-to-all-done.4 = bf16[16,128,768]{2,1,0:T(8,128)(2,1)} async-done(((bf16[16,128,768]{2,1,0:T(8,128)(2,1)}), bf16[16,128,768]{2,1,0:T(8,128)(2,1)}, u32[]{:S(2)}, u32[]{:S(2)}) %all-to-all-start.4) | async-done | bytes 3145760 | tf_op jit(solution)/shard_map/all_to_all | solution.py:44
  485.6 4.9 all-to-all-start.6
  490.5 8.9 %fusion.9 = f32[1152,768]{1,0:T(8,128)} fusion(bf16[1152,2048]{1,0:T(8,128)(2,1)} %bitcast.6, bf16[2048,768]{1,0:T(8,128)(2,1)} %bitcast.40), kind=kOutput, calls=%fused_computation.38 | convolution fusion | flops 3623878656 | bytes 11403264 | tf_op jit(solution)/shard_map/dot_general | solution.py:8
  499.5 61.1 %all-to-all-done.6 = bf16[16,48,2048]{2,1,0:T(8,128)(2,1)} async-done(((bf16[16,48,2048]{2,1,0:T(8,128)(2,1)}), bf16[16,48,2048]{2,1,0:T(8,128)(2,1)}, u32[]{:S(2)}, u32[]{:S(2)}) %all-to-all-start.6) | async-done | bytes 3145760 | tf_op jit(solution)/shard_map/all_to_all | solution.py:45
  560.5 14.3 %convolution_convert_fusion = bf16[1152,2048]{1,0:T(8,128)(2,1)} fusion(bf16[768,2048]{1,0:T(8,128)(2,1)} %bitcast.12, bf16[1152,2048]{1,0:T(8,128)(2,1)} %bitcast.6, bf16[2048,768]{1,0:T(8,128)(2,1)} %bitcast.10, f32[1152,768]{1,0:T(8,128)} %fusion.9), kind=kOutput, calls=%fused_computation.8 | convolution fusion | flops 7255425024 | bytes 19267584 | tf_op jit(solution)/shard_map/dot_general | solution.py:11
  574.8 0.0 copy-start.4
  574.8 5.0 all-to-all-start.7
  579.9 0.0 copy-done.4
  579.9 0.1 copy.16
  580.0 103.6 %all-to-all-done.7 = bf16[16,72,2048]{2,1,0:T(8,128)(2,1)} async-done(((bf16[16,72,2048]{2,1,0:T(8,128)(2,1)}), bf16[16,72,2048]{2,1,0:T(8,128)(2,1)}, u32[]{:S(2)}, u32[]{:S(2)}) %all-to-all-start.7) | async-done | bytes 4718624 | tf_op jit(solution)/shard_map/all_to_all | solution.py:58
  683.6 0.0 copy-start.1
  683.6 11.9 %gather_fusion.1 = bf16[1024,2048]{1,0:T(8,128)(2,1)} fusion(bf16[1152,2048]{1,0:T(8,128)(2,1)} %bitcast.14, s32[1024]{0:T(1024)S(1)} %broadcast_clamp_fusion), kind=kCustom, calls=%fused_computation.4 | custom fusion | bytes 8392704 | tf_op jit(solution)/shard_map/gather | solution.py:59
  695.4 7.3 %fusion = bf16[128,2048]{1,0:T(8,128)(2,1)} fusion(bf16[1024,2048]{1,0:T(8,128)(2,1)} %gather_fusion.1, f32[128,8]{1,0:T(8,128)S(1)} %copy.16), kind=kLoop, calls=%fused_computation.7 | loop fusion | flops 6029312 | bytes 4722688 | tf_op jit(solution)/shard_map/reduce_sum | solution.py:63
  702.7 0.0 copy-done.1
  (13 shorter events, 0.1 us)
Async XLA Ops:
  0.0 162.4 %copy-start = (bf16[128,2048]{1,0:T(8,128)(2,1)S(1)}, bf16[128,2048]{1,0:T(8,128)(2,1)}, u32[]{:S(2)}) copy-start(bf16[128,2048]{1,0:T(8,128)(2,1)} %param.9) | copy-start | bytes 1572868
  0.0 76.7 %copy-start.2 = (bf16[1,2048,768]{2,1,0:T(8,128)(2,1)S(1)}, bf16[1,2048,768]{2,1,0:T(8,128)(2,1)}, u32[]{:S(2)}) copy-start(bf16[1,2048,768]{2,1,0:T(8,128)(2,1)} %param.13) | copy-start | bytes 9437188
  151.6 5.3 copy-start.3
  151.6 75.3 %all-to-all-start.5 = ((bf16[16,48,2048]{2,1,0:T(8,128)(2,1)}), bf16[16,48,2048]{2,1,0:T(8,128)(2,1)}, u32[]{:S(2)}, u32[]{:S(2)}) async-start(bf16[16,48,2048]{2,1,0:T(8,128)(2,1)} %bitcast.39), calls=%async_computation.5 | async-start | bytes 6291456 | tf_op jit(solution)/shard_map/all_to_all | solution.py:33
  226.9 5.0 copy-start.5
  226.9 108.7 %all-to-all-start = ((bf16[16,72,2048]{2,1,0:T(8,128)(2,1)}), bf16[16,72,2048]{2,1,0:T(8,128)(2,1)}, u32[]{:S(2)}, u32[]{:S(2)}) async-start(bf16[16,72,2048]{2,1,0:T(8,128)(2,1)} %bitcast.35), calls=%async_computation | async-start | bytes 9437184 | tf_op jit(solution)/shard_map/all_to_all | solution.py:55
  410.4 75.2 %all-to-all-start.4 = ((bf16[16,128,768]{2,1,0:T(8,128)(2,1)}), bf16[16,128,768]{2,1,0:T(8,128)(2,1)}, u32[]{:S(2)}, u32[]{:S(2)}) async-start(bf16[16,128,768]{2,1,0:T(8,128)(2,1)} %get-tuple-element.7), calls=%async_computation.4 | async-start | bytes 6291456 | tf_op jit(solution)/shard_map/all_to_all | solution.py:44
  485.6 74.9 %all-to-all-start.6 = ((bf16[16,48,2048]{2,1,0:T(8,128)(2,1)}), bf16[16,48,2048]{2,1,0:T(8,128)(2,1)}, u32[]{:S(2)}, u32[]{:S(2)}) async-start(bf16[16,48,2048]{2,1,0:T(8,128)(2,1)} %broadcast_select_fusion.2), calls=%async_computation.6 | async-start | bytes 6291456 | tf_op jit(solution)/shard_map/all_to_all | solution.py:45
  574.8 5.0 copy-start.4
  574.8 108.7 %all-to-all-start.7 = ((bf16[16,72,2048]{2,1,0:T(8,128)(2,1)}), bf16[16,72,2048]{2,1,0:T(8,128)(2,1)}, u32[]{:S(2)}, u32[]{:S(2)}) async-start(bf16[16,72,2048]{2,1,0:T(8,128)(2,1)} %bitcast.36), calls=%async_computation.7 | async-start | bytes 9437184 | tf_op jit(solution)/shard_map/all_to_all | solution.py:58
  683.6 19.2 %copy-start.1 = (bf16[128,2048]{1,0:T(8,128)(2,1)S(1)}, bf16[128,2048]{1,0:T(8,128)(2,1)}, u32[]{:S(2)}) copy-start(bf16[128,2048]{1,0:T(8,128)(2,1)} %param.9) | copy-start | bytes 1572868
where the time goes:
time: 704 us; the launch traced here: 703 us
  waiting for transfers between devices  357 us (51%)
  blocking collectives  226 us (32%)
  local copies, waits for them, and re-layouts  48.5 us (7%)
  starting transfers between devices  25.5 us (4%)
  matrix products  23.2 us (3%)
  other arithmetic  22.1 us (3%)
    all_to_all x1, waiting for transfers between devices, on_device(): lax.all_to_all(result_rows, 'ep', split_axis=0, concat_axis=0, tiled=True)  104 us
    all_to_all x1, waiting for transfers between devices, on_device(): lax.all_to_all(send_buffer, 'ep', split_axis=0, concat_axis=0, tiled=True)  88.8 us
    all_to_all x1, blocking collectives, on_device(): lax.all_to_all(to_pieces(gate_weight, n_dev), 'ep', split_axis=0, concat_...  76.7 us
    all_to_all x1, blocking collectives, on_device(): lax.all_to_all(to_pieces(up_weight, n_dev), 'ep', split_axis=0, concat_ax...  74.9 us
    all_to_all x1, blocking collectives, on_device(): lax.all_to_all(moved[0], 'ep', split_axis=0, concat_axis=0, tiled=True)  74.8 us
    all_to_all x1, waiting for transfers between devices, on_device(): lax.all_to_all(moved[1], 'ep', split_axis=0, concat_axis=0, tiled=True)  61.9 us
    all_to_all x1, waiting for transfers between devices, on_device(): lax.all_to_all(moved[2], 'ep', split_axis=0, concat_axis=0, tiled=True)  61.1 us
    all_to_all x1, waiting for transfers between devices, on_device(): lax.all_to_all(to_pieces(down_weight, n_dev), 'ep', split_axis=0, concat_...  41.6 us
  transfers between devices with their start and end apart: 5, of which 5 were waited for; matrix products, arithmetic and copies ran while one was open for 9% of the time, Pallas kernels for 0%

commit v1 on v0

v1 whole, which is shorter than its diff:
```python
import functools

import jax
import jax.numpy as jnp
from jax import lax
from jax.experimental import pallas as pl
from jax.experimental.pallas import tpu as pltpu
from jax.sharding import PartitionSpec as P


def ffn_kernel(n_in, tiles, *refs):
    x_refs, refs = refs[:n_in], refs[n_in:]
    w_ref, weights, refs = refs[0], refs[1:7], refs[7:]
    out_refs, (rows, total) = refs[:n_in], refs[n_in:]
    step = pl.program_id(0)
    half = x_refs[0].shape[0]

    @pl.when(step == 0)
    def _():
        for i, x_ref in enumerate(x_refs):
            rows[pl.ds(i * half, half), :] = x_ref[...]
        total[...] = jnp.zeros_like(total)

    def add_tile(expert, gate_ref, up_ref, down_ref):
        x = rows[...]
        gate = jnp.dot(x, gate_ref[0], preferred_element_type=jnp.float32)
        up = jnp.dot(x, up_ref[0], preferred_element_type=jnp.float32)
        hidden = (gate / (1.0 + jnp.exp(-gate)) * up).astype(jnp.bfloat16)
        out = jnp.dot(hidden, down_ref[0], preferred_element_type=jnp.float32)
        total[...] += out * w_ref[:, expert : expert + 1]

    @pl.when(step < tiles)
    def _():
        add_tile(0, *weights[:3])

    @pl.when(step >= tiles)
    def _():
        add_tile(1, *weights[3:])

    @pl.when(step == 2 * tiles - 1)
    def _():
        for i, out_ref in enumerate(out_refs):
            out_ref[...] = total[pl.ds(i * half, half), :].astype(out_ref.dtype)


def ffn(blocks, kinds, scores, own, other):
    half, width = blocks[0].shape
    ff = own[0].shape[2]
    tile = 256
    tiles = ff // tile
    n_in = len(blocks)
    m = n_in * half
    whole = pl.BlockSpec((half, width), lambda i: (0, 0))

    def spec(first):
        at = (lambda i: jnp.minimum(i, tiles - 1)) if first else (lambda i: jnp.maximum(i - tiles, 0))
        return [
            pl.BlockSpec((1, width, tile), lambda i: (0, 0, at(i))),
            pl.BlockSpec((1, width, tile), lambda i: (0, 0, at(i))),
            pl.BlockSpec((1, tile, width), lambda i: (0, at(i), 0)),
        ]

    return pl.pallas_call(
        functools.partial(ffn_kernel, n_in, tiles),
        grid=(2 * tiles,),
        in_specs=[whole] * n_in + [pl.BlockSpec((m, 2), lambda i: (0, 0))] + spec(True) + spec(False),
        out_specs=[whole] * n_in,
        out_shape=[jax.ShapeDtypeStruct((half, width), kind) for kind in kinds],
        scratch_shapes=[pltpu.VMEM((m, width), jnp.bfloat16), pltpu.VMEM((m, width), jnp.float32)],
        compiler_params=pltpu.CompilerParams(vmem_limit_bytes=40 * 2**20),
        cost_estimate=pl.CostEstimate(
            flops=12 * m * width * ff, bytes_accessed=12 * width * ff + 6 * m * width, transcendentals=2 * m * ff
        ),
    )(*blocks, scores, *own, *other)


def ring_order(chips):
    return list(range(0, chips, 2)) + list(range(1, chips, 2))[::-1]


def on_device(tokens, expert_ids, gate_scores, gate_weight, up_weight, down_weight, partner):
    n_dev = lax.axis_size("ep")
    chips = n_dev // 2
    far = chips // 2
    rows, width = tokens.shape
    half = rows // 2
    order = ring_order(chips)
    forward = [(order[i] * 2 + k, order[(i + 1) % chips] * 2 + k) for i in range(chips) for k in range(2)]
    backward = [(b, a) for a, b in forward]
    swap = [(i, i ^ 1) for i in range(n_dev)]
    perm = (forward, backward)

    other = tuple(lax.ppermute(w, "ep", swap) for w in (gate_weight, up_weight, down_weight))
    own = (gate_weight, up_weight, down_weight)

    slot_scores = jnp.sum(
        jnp.where(expert_ids.T[None] == partner[:, None, None], gate_scores.T[None], 0.0), axis=1
    )
    all_scores = lax.all_gather(slot_scores, "ep", axis=0).reshape(chips, 2, n_dev, rows)
    me = lax.axis_index("ep")
    core = me % 2
    chip = me // 2
    mine = lax.dynamic_index_in_dim(all_scores, core, 1, keepdims=False)
    mine = jnp.stack(
        [
            lax.dynamic_index_in_dim(mine, me, 1, keepdims=False),
            lax.dynamic_index_in_dim(mine, chip * 2 + 1 - core, 1, keepdims=False),
        ],
        axis=-1,
    )
    place = jnp.where(chip % 2 == 0, chip // 2, chips - 1 - chip // 2)
    mine = mine[jnp.asarray(order, jnp.int32)]
    mine = jnp.concatenate([mine, mine], axis=0)

    def scores_of(distance, h):
        block = lax.dynamic_index_in_dim(mine, (place + distance) % chips, 0, keepdims=False)
        return block[h * half : (h + 1) * half]

    halves = (tokens[:half], tokens[half:])
    held = [[[halves[h]] for h in range(2)] for _ in range(2)]
    last = [[far if d == h else far - 1 for h in range(2)] for d in range(2)]
    for s in range(1, far + 1):
        for h in range(2):
            for d in range(2):
                if s <= last[d][h]:
                    held[d][h].append(lax.ppermute(held[d][h][-1], "ep", perm[d]))

    done = {}

    def compute(keys):
        blocks = [held[d][h][s] for d, h, s in keys]
        kinds = [jnp.bfloat16 if s == last[d][h] else jnp.float32 for d, h, s in keys]
        scores = jnp.concatenate([scores_of(-s if d == 0 else s, h) for d, h, s in keys], axis=0)
        for key, out in zip(keys, ffn(blocks, kinds, scores, own, other)):
            done[key] = out

    compute([(0, 0, 0), (0, 1, 0)] + [(d, h, 1) for d in range(2) for h in range(2)])
    for s in range(2, far + 1):
        compute([(d, h, s) for d in range(2) for h in range(2) if s <= last[d][h]])

    back = {}
    for s in range(far, 0, -1):
        for h in range(2):
            for d in range(2):
                if s > last[d][h]:
                    continue
                part = done[d, h, s]
                if (d, h) in back:
                    part = (back[d, h].astype(jnp.float32) + part).astype(jnp.bfloat16)
                back[d, h] = lax.ppermute(part, "ep", perm[1 - d])
    out = [
        (done[0, h, 0] + back[0, h].astype(jnp.float32) + back[1, h].astype(jnp.float32)).astype(jnp.bfloat16)
        for h in range(2)
    ]
    return jnp.concatenate(out, axis=0)


def solution(mesh):
    rows = P(("dp", "ep"), None)
    stacks = P(("dp", "ep"), None, None)
    return jax.shard_map(
        on_device,
        mesh=mesh,
        in_specs=(rows, rows, rows, stacks, stacks, stacks, P()),
        out_specs=rows,
        check_vma=False,
    )
```

time: 704 us -> 163 us (0.23)
  the two profiles are of different devices: /device:TPU:15 before, /device:TPU:0 now
where the time goes in v1:
time: 163 us
  waiting for transfers between devices  51.2 us (31%)
  Pallas kernels  42 us (26%)
  starting transfers between devices  26.6 us (16%)
  blocking collectives  25.7 us (16%)
  local copies, waits for them, and re-layouts  14 us (9%)
  other arithmetic  3.22 us (2%)
    pallas_call x4, Pallas kernels, ffn(): pl.pallas_call(functools.partial(ffn_kernel, n_in, tiles), grid=(2 * tile...  42 us
    ppermute x14, waiting for transfers between devices, on_device(): held[d][h].append(lax.ppermute(held[d][h][-1], 'ep', perm[d]))  32.4 us
    all_gather x1, blocking collectives, on_device(): lax.all_gather(slot_scores, 'ep', axis=0).reshape(chips, 2, n_dev, rows)  25.7 us
    ppermute x14, waiting for transfers between devices, on_device(): back[d, h] = lax.ppermute(part, 'ep', perm[1 - d])  18.8 us
    ppermute x14, starting transfers between devices, on_device(): back[d, h] = lax.ppermute(part, 'ep', perm[1 - d])  14.5 us
    ppermute x14, starting transfers between devices, on_device(): held[d][h].append(lax.ppermute(held[d][h][-1], 'ep', perm[d]))  11.2 us
    unnamed x39, local copies, waits for them, and re-layouts  9.94 us
  transfers between devices with their start and end apart: 31, of which 14 were waited for; matrix products, arithmetic and copies ran while one was open for 4% of the time, Pallas kernels for 26%

profile of v1, /device:TPU:0, one launch (start us, length us, event | category | flops | bytes accessed | tf_op | source)
XLA Modules:
  0.0 163.1 jit_solution(867806681010181791)
XLA Ops:
  0.0 0.5 collective-permute-start.4
  0.5 0.4 collective-permute-start.6
  1.0 1.8 %fusion = (bf16[64,2048]{1,0:T(8,128)(2,1)S(1)}, bf16[64,2048]{1,0:T(8,128)(2,1)}) fusion(bf16[128,2048]{1,0:T(8,128)(2,1)} %param.8), kind=kLoop, calls=%fused_computation.49 | loop fusion | bytes 1048576 | tf_op jit(solution)/shard_map/slice | solution.py:119
  2.7 2.9 %collective-permute-start = (bf16[64,2048]{1,0:T(8,128)(2,1)}, bf16[64,2048]{1,0:T(8,128)(2,1)}, u32[]{:S(2)}, u32[]{:S(2)}) collective-permute-start(bf16[64,2048]{1,0:T(8,128)(2,1)} %get-tuple-element.38.refs_0_), channel_id=1, source_target_pairs={{0,8},{2,10},{8,16},{10,18},{16,24},{18,26},{24,28},{26,30},{28,20... | collective-permute-start | bytes 786440 | tf_op jit(solution)/shard_map/ppermute | solution.py:126
  5.7 1.6 collective-permute-start.1
  7.2 0.8 select_reduce_fusion
  8.0 25.7 %all-gather = f32[256,128]{1,0:T(8,128)S(1)} all-gather(f32[16,128]{1,0:T(8,128)S(1)} %select_reduce_fusion), channel_id=2, replica_groups=mesh['ep'=16,'dp'=2] {'ep'}, dimensions={0}, use_global_device_ids=true | all-gather | bytes 139264 | tf_op jit(solution)/shard_map/all_gather | solution.py:99
  33.8 0.2 collective-permute-start.2
  34.1 0.7 pad_clamp_fusion
  34.7 0.6 gather_fusion
  35.4 7.9 %collective-permute-done.2.refs_4_ = bf16[64,2048]{1,0:T(8,128)(2,1)} collective-permute-done((bf16[64,2048]{1,0:T(8,128)(2,1)}, bf16[64,2048]{1,0:T(8,128)(2,1)}, u32[]{:S(2)}, u32[]{:S(2)}) %collective-permute-start.2) | collective-permute-done | bytes 262176 | tf_op jit(solution)/shard_map/ppermute | solution.py:126
  43.3 5.0 %collective-permute-done.3.refs_5_ = bf16[64,2048]{1,0:T(8,128)(2,1)} collective-permute-done((bf16[64,2048]{1,0:T(8,128)(2,1)S(1)}, bf16[64,2048]{1,0:T(8,128)(2,1)}, u32[]{:S(2)}, u32[]{:S(2)}) %collective-permute-start.3) | collective-permute-done | bytes 262176 | tf_op jit(solution)/shard_map/ppermute | solution.py:126
  48.4 2.3 %collective-permute-done.7.refs_0_ = bf16[64,2048]{1,0:T(8,128)(2,1)S(1)} collective-permute-done((bf16[64,2048]{1,0:T(8,128)(2,1)}, bf16[64,2048]{1,0:T(8,128)(2,1)S(1)}, u32[]{:S(2)}, u32[]{:S(2)}) %collective-permute-start.7) | collective-permute-done | bytes 262176 | tf_op jit(solution)/shard_map/ppermute | solution.py:126
  50.6 0.4 collective-permute-start.16
  51.1 5.3 %collective-permute-done.14.refs_1_ = bf16[64,2048]{1,0:T(8,128)(2,1)} collective-permute-done((bf16[64,2048]{1,0:T(8,128)(2,1)}, bf16[64,2048]{1,0:T(8,128)(2,1)}, u32[]{:S(2)}, u32[]{:S(2)}) %collective-permute-start.14) | collective-permute-done | bytes 262176 | tf_op jit(solution)/shard_map/ppermute | solution.py:126
  56.4 0.4 collective-permute-start.10
  56.9 0.4 collective-permute-done.16.refs_2_
  57.3 1.2 collective-permute-start.8
  58.5 0.7 copy-done.4
  59.2 4.2 %collective-permute-done.10.refs_3_ = bf16[64,2048]{1,0:T(8,128)(2,1)S(1)} collective-permute-done((bf16[64,2048]{1,0:T(8,128)(2,1)}, bf16[64,2048]{1,0:T(8,128)(2,1)S(1)}, u32[]{:S(2)}, u32[]{:S(2)}) %collective-permute-start.10) | collective-permute-done | bytes 262176 | tf_op jit(solution)/shard_map/ppermute | solution.py:126
  63.4 0.6 collective-permute-start.11
  64.0 0.7 copy-done.6
  64.9 1.4 collective-permute-start.9
  66.3 0.7 copy-done.8
  67.0 3.6 %collective-permute-done.11.refs_3_ = bf16[64,2048]{1,0:T(8,128)(2,1)S(1)} collective-permute-done((bf16[64,2048]{1,0:T(8,128)(2,1)S(1)}, bf16[64,2048]{1,0:T(8,128)(2,1)S(1)}, u32[]{:S(2)}, u32[]{:S(2)}) %collective-permute-start.11) | collective-permute-done | bytes 262176 | tf_op jit(solution)/shard_map/ppermute | solution.py:126
  70.6 0.4 collective-permute-start.12
  71.0 0.7 copy-done.10
  71.9 0.7 copy-done.12
  72.6 1.6 collective-permute-start.15
  74.2 3.7 %collective-permute-done.12.refs_1_ = bf16[64,2048]{1,0:T(8,128)(2,1)S(1)} collective-permute-done((bf16[64,2048]{1,0:T(8,128)(2,1)S(1)}, bf16[64,2048]{1,0:T(8,128)(2,1)S(1)}, u32[]{:S(2)}, u32[]{:S(2)}) %collective-permute-start.12) | collective-permute-done | bytes 262176 | tf_op jit(solution)/shard_map/ppermute | solution.py:126
  77.9 0.7 copy-done.14
  78.6 0.3 collective-permute-start.17
  79.0 0.8 copy.61.refs_6_
  79.8 0.1 copy.64.refs_4_
  80.0 0.1 copy.63.refs_4_
  80.3 1.9 %copy-done.1 = bf16[1,2048,768]{2,1,0:T(8,128)(2,1)S(1)} copy-done((bf16[1,2048,768]{2,1,0:T(8,128)(2,1)S(1)}, bf16[1,2048,768]{2,1,0:T(8,128)(2,1)}, u32[]{:S(2)}) %copy-start.1) | copy-done | bytes 3145752
  82.2 1.9 %copy-done.3 = bf16[1,768,2048]{2,1,0:T(8,128)(2,1)S(1)} copy-done((bf16[1,768,2048]{2,1,0:T(8,128)(2,1)S(1)}, bf16[1,768,2048]{2,1,0:T(8,128)(2,1)}, u32[]{:S(2)}) %copy-start.3) | copy-done | bytes 3145752
  84.1 0.9 copy-done.13
  85.0 0.9 copy-done.15
  86.0 8.4 %shard_map.83 = (bf16[64,2048]{1,0:T(8,128)(2,1)S(1)}, bf16[64,2048]{1,0:T(8,128)(2,1)S(1)}) custom-call(bf16[64,2048]{1,0:T(8,128)(2,1)S(1)} %copy-done.13, bf16[64,2048]{1,0:T(8,128)(2,1)S(1)} %copy-done.15, f32[128,2]{1,0:T(8,128)S(1)} %copy.62.refs_2_, bf16[1,2048,768]{2,1,0:T(8,128)(2,1)S(1)} %copy-done, bf16[1,2048,768]{2,1,0:T(8,128)(2,1)S(1)} %copy-done.1, ...), custom_call_target="tpu_custom_call" | custom-call | flops 2415919104 | bytes 20447232 | tf_op jit(solution)/shard_map/pallas_call | solution.py:63
  94.5 1.8 %collective-permute-start.27 = (bf16[64,2048]{1,0:T(8,128)(2,1)S(1)}, bf16[64,2048]{1,0:T(8,128)(2,1)S(1)}, u32[]{:S(2)}, u32[]{:S(2)}) collective-permute-start(bf16[64,2048]{1,0:T(8,128)(2,1)S(1)} %get-tuple-element.33), channel_id=1, source_target_pairs={{0,8},{2,10},{8,16},{10,18},{16,24},{18,26},{24,28},{26,30},{28,20... | collective-permute-start | bytes 786440 | tf_op jit(solution)/shard_map/ppermute | solution.py:150
  96.3 10.5 %shard_map.84 = (f32[64,2048]{1,0:T(8,128)S(1)}, bf16[64,2048]{1,0:T(8,128)(2,1)S(1)}, bf16[64,2048]{1,0:T(8,128)(2,1)S(1)}, f32[64,2048]{1,0:T(8,128)S(1)}) custom-call(bf16[64,2048]{1,0:T(8,128)(2,1)S(1)} %copy-done.9, bf16[64,2048]{1,0:T(8,128)(2,1)} %collective-permute-done.15.refs_1_, bf16[64,2048]{1,0:T(8,128)(2,1)} %collective-permute-done.17.refs_2_, ...), custom_call_target="tpu_custom_call" | custom-call | flops 4831838208 | bytes 22020096 | tf_op jit(solution)/shard_map/pallas_call | solution.py:63
  106.8 0.3 collective-permute-start.24
  107.1 1.8 %collective-permute-start.21 = (bf16[64,2048]{1,0:T(8,128)(2,1)S(1)}, bf16[64,2048]{1,0:T(8,128)(2,1)S(1)}, u32[]{:S(2)}, u32[]{:S(2)}) collective-permute-start(bf16[64,2048]{1,0:T(8,128)(2,1)S(1)} %get-tuple-element.26), channel_id=1, source_target_pairs={{0,8},{2,10},{8,16},{10,18},{16,24},{18,26},{24,28},{26,30},{28,20... | collective-permute-start | bytes 786440 | tf_op jit(solution)/shard_map/ppermute | solution.py:150
  108.8 0.3 collective-permute-start.13
  109.1 12.7 %shard_map.82 = (f32[64,2048]{1,0:T(8,128)S(1)}, f32[64,2048]{1,0:T(8,128)S(1)}, f32[64,2048]{1,0:T(8,128)S(1)}, f32[64,2048]{1,0:T(8,128)S(1)}, f32[64,2048]{1,0:T(8,128)S(1)}, /*index=5*/f32[64,2048]{1,0:T(8,128)S(1)}) custom-call(bf16[64,2048]{1,0:T(8,128)(2,1)} %get-tuple-element.38.refs_0_, bf16[64,2048]{1,0:T(8,128)(2,1)S(1)} %copy-done.17, ...), custom_call_target="tpu_custom_call" | custom-call | flops 7247757312 | bytes 23592960 | tf_op jit(solution)/shard_map/pallas_call | solution.py:63
  121.8 10.5 %shard_map.85 = (f32[64,2048]{1,0:T(8,128)S(1)}, f32[64,2048]{1,0:T(8,128)S(1)}, f32[64,2048]{1,0:T(8,128)S(1)}, f32[64,2048]{1,0:T(8,128)S(1)}) custom-call(bf16[64,2048]{1,0:T(8,128)(2,1)S(1)} %copy-done.5, bf16[64,2048]{1,0:T(8,128)(2,1)} %collective-permute-done.14.refs_1_, bf16[64,2048]{1,0:T(8,128)(2,1)} %collective-permute-done.16.refs_2_, ...), custom_call_target="tpu_custom_call" | custom-call | flops 4831838208 | bytes 22020096 | tf_op jit(solution)/shard_map/pallas_call | solution.py:63
  132.4 1.8 %collective-permute-start.28 = (bf16[64,2048]{1,0:T(8,128)(2,1)S(1)}, bf16[64,2048]{1,0:T(8,128)(2,1)S(1)}, u32[]{:S(2)}, u32[]{:S(2)}) collective-permute-start(bf16[64,2048]{1,0:T(8,128)(2,1)S(1)} %add_convert_fusion.3), channel_id=1, source_target_pairs={{0,8},{2,10},{8,16},{10,18},{16,24},{18,26},{24,28},{26,30},{28,20... | collective-permute-start | bytes 786440 | tf_op jit(solution)/shard_map/ppermute | solution.py:150
  134.2 0.3 collective-permute-start.25
  134.6 1.8 %collective-permute-start.22 = (bf16[64,2048]{1,0:T(8,128)(2,1)S(1)}, bf16[64,2048]{1,0:T(8,128)(2,1)S(1)}, u32[]{:S(2)}, u32[]{:S(2)}) collective-permute-start(bf16[64,2048]{1,0:T(8,128)(2,1)S(1)} %add_convert_fusion.8), channel_id=1, source_target_pairs={{0,8},{2,10},{8,16},{10,18},{16,24},{18,26},{24,28},{26,30},{28,20... | collective-permute-start | bytes 786440 | tf_op jit(solution)/shard_map/ppermute | solution.py:150
  136.5 0.3 collective-permute-start.18
  136.8 4.9 %collective-permute-done.28 = bf16[64,2048]{1,0:T(8,128)(2,1)S(1)} collective-permute-done((bf16[64,2048]{1,0:T(8,128)(2,1)S(1)}, bf16[64,2048]{1,0:T(8,128)(2,1)S(1)}, u32[]{:S(2)}, u32[]{:S(2)}) %collective-permute-start.28) | collective-permute-done | bytes 262176 | tf_op jit(solution)/shard_map/ppermute | solution.py:150
  141.7 1.8 %collective-permute-start.29 = (bf16[64,2048]{1,0:T(8,128)(2,1)S(1)}, bf16[64,2048]{1,0:T(8,128)(2,1)S(1)}, u32[]{:S(2)}, u32[]{:S(2)}) collective-permute-start(bf16[64,2048]{1,0:T(8,128)(2,1)S(1)} %add_convert_fusion.2), channel_id=1, source_target_pairs={{0,8},{2,10},{8,16},{10,18},{16,24},{18,26},{24,28},{26,30},{28,20... | collective-permute-start | bytes 786440 | tf_op jit(solution)/shard_map/ppermute | solution.py:150
  143.6 0.3 collective-permute-start.26
  143.9 3.4 %collective-permute-done.22 = bf16[64,2048]{1,0:T(8,128)(2,1)S(1)} collective-permute-done((bf16[64,2048]{1,0:T(8,128)(2,1)S(1)}, bf16[64,2048]{1,0:T(8,128)(2,1)S(1)}, u32[]{:S(2)}, u32[]{:S(2)}) %collective-permute-start.22) | collective-permute-done | bytes 262176 | tf_op jit(solution)/shard_map/ppermute | solution.py:150
  147.3 1.8 %collective-permute-start.23 = (bf16[64,2048]{1,0:T(8,128)(2,1)S(1)}, bf16[64,2048]{1,0:T(8,128)(2,1)S(1)}, u32[]{:S(2)}, u32[]{:S(2)}) collective-permute-start(bf16[64,2048]{1,0:T(8,128)(2,1)S(1)} %add_convert_fusion.7), channel_id=1, source_target_pairs={{0,8},{2,10},{8,16},{10,18},{16,24},{18,26},{24,28},{26,30},{28,20... | collective-permute-start | bytes 786440 | tf_op jit(solution)/shard_map/ppermute | solution.py:150
  149.2 0.3 collective-permute-start.19
  149.5 1.4 collective-permute-done.29
  151.0 1.5 collective-permute-start.30
  152.5 3.2 %collective-permute-done.19 = bf16[64,2048]{1,0:T(8,128)(2,1)S(1)} collective-permute-done((bf16[64,2048]{1,0:T(8,128)(2,1)S(1)}, bf16[64,2048]{1,0:T(8,128)(2,1)S(1)}, u32[]{:S(2)}, u32[]{:S(2)}) %collective-permute-start.19) | collective-permute-done | bytes 262176 | tf_op jit(solution)/shard_map/ppermute | solution.py:150
  155.7 0.3 collective-permute-start.20
  156.0 1.4 collective-permute-done.30
  157.5 4.6 %collective-permute-done.20 = bf16[64,2048]{1,0:T(8,128)(2,1)S(1)} collective-permute-done((bf16[64,2048]{1,0:T(8,128)(2,1)S(1)}, bf16[64,2048]{1,0:T(8,128)(2,1)S(1)}, u32[]{:S(2)}, u32[]{:S(2)}) %collective-permute-start.20) | collective-permute-done | bytes 262176 | tf_op jit(solution)/shard_map/ppermute | solution.py:150
  162.2 0.8 pad_maximum_fusion
  (76 shorter events, 1.8 us)
Async XLA Ops:
  0.0 80.3 %copy-start = (bf16[1,2048,768]{2,1,0:T(8,128)(2,1)S(1)}, bf16[1,2048,768]{2,1,0:T(8,128)(2,1)}, u32[]{:S(2)}) copy-start(bf16[1,2048,768]{2,1,0:T(8,128)(2,1)} %refs_5_.5) | copy-start | bytes 9437188
  0.0 80.2 %collective-permute-start.4 = (bf16[1,2048,768]{2,1,0:T(8,128)(2,1)}, bf16[1,2048,768]{2,1,0:T(8,128)(2,1)}, u32[]{:S(2)}, u32[]{:S(2)}) collective-permute-start(bf16[1,2048,768]{2,1,0:T(8,128)(2,1)} %refs_5_.5), channel_id=1, source_target_pairs={{0,2},{2,0},{4,6},{6,4},{8,10},{10,8},{12,14},{14,12},{16,18},{18,... | collective-permute-start | bytes 9437192 | tf_op jit(solution)/shard_map/ppermute | solution.py:93
  0.5 79.8 %collective-permute-start.5 = (bf16[1,2048,768]{2,1,0:T(8,128)(2,1)}, bf16[1,2048,768]{2,1,0:T(8,128)(2,1)}, u32[]{:S(2)}, u32[]{:S(2)}) collective-permute-start(bf16[1,2048,768]{2,1,0:T(8,128)(2,1)} %refs_6_.3), channel_id=1, source_target_pairs={{0,2},{2,0},{4,6},{6,4},{8,10},{10,8},{12,14},{14,12},{16,18},{18,... | collective-permute-start | bytes 9437192 | tf_op jit(solution)/shard_map/ppermute | solution.py:93
  0.5 79.8 %collective-permute-start.6 = (bf16[1,768,2048]{2,1,0:T(8,128)(2,1)}, bf16[1,768,2048]{2,1,0:T(8,128)(2,1)}, u32[]{:S(2)}, u32[]{:S(2)}) collective-permute-start(bf16[1,768,2048]{2,1,0:T(8,128)(2,1)} %refs_7_.5), channel_id=1, source_target_pairs={{0,2},{2,0},{4,6},{6,4},{8,10},{10,8},{12,14},{14,12},{16,18},{18,... | collective-permute-start | bytes 9437192 | tf_op jit(solution)/shard_map/ppermute | solution.py:93
  2.7 76.3 %copy-start.16 = (bf16[64,2048]{1,0:T(8,128)(2,1)}, bf16[64,2048]{1,0:T(8,128)(2,1)S(1)}, u32[]{:S(2)}) copy-start(bf16[64,2048]{1,0:T(8,128)(2,1)S(1)} %get-tuple-element.37.refs_1_) | copy-start | bytes 786436
  2.7 31.0 %collective-permute-start = (bf16[64,2048]{1,0:T(8,128)(2,1)}, bf16[64,2048]{1,0:T(8,128)(2,1)}, u32[]{:S(2)}, u32[]{:S(2)}) collective-permute-start(bf16[64,2048]{1,0:T(8,128)(2,1)} %get-tuple-element.38.refs_0_), channel_id=1, source_target_pairs={{0,8},{2,10},{8,16},{10,18},{16,24},{18,26},{24,28},{26,30},{28,20... | collective-permute-start | bytes 786440 | tf_op jit(solution)/shard_map/ppermute | solution.py:126
  5.7 28.3 %collective-permute-start.1 = (bf16[64,2048]{1,0:T(8,128)(2,1)S(1)}, bf16[64,2048]{1,0:T(8,128)(2,1)}, u32[]{:S(2)}, u32[]{:S(2)}) collective-permute-start(bf16[64,2048]{1,0:T(8,128)(2,1)S(1)} %get-tuple-element.37.refs_1_), channel_id=1, source_target_pairs={{0,8},{2,10},{8,16},{10,18},{16,24},{18,26},{24,28},{26,30},{28,20... | collective-permute-start | bytes 786440 | tf_op jit(solution)/shard_map/ppermute | solution.py:126
  33.8 9.5 %collective-permute-start.2 = (bf16[64,2048]{1,0:T(8,128)(2,1)}, bf16[64,2048]{1,0:T(8,128)(2,1)}, u32[]{:S(2)}, u32[]{:S(2)}) collective-permute-start(bf16[64,2048]{1,0:T(8,128)(2,1)} %get-tuple-element.38.refs_0_), channel_id=1, source_target_pairs={{8,0},{10,2},{16,8},{18,10},{24,16},{26,18},{28,24},{30,26},{20,28... | collective-permute-start | bytes 786440 | tf_op jit(solution)/shard_map/ppermute | solution.py:126
  34.0 14.3 %collective-permute-start.3 = (bf16[64,2048]{1,0:T(8,128)(2,1)S(1)}, bf16[64,2048]{1,0:T(8,128)(2,1)}, u32[]{:S(2)}, u32[]{:S(2)}) collective-permute-start(bf16[64,2048]{1,0:T(8,128)(2,1)S(1)} %get-tuple-element.37.refs_1_), channel_id=1, source_target_pairs={{8,0},{10,2},{16,8},{18,10},{24,16},{26,18},{28,24},{30,26},{20,28... | collective-permute-start | bytes 786440 | tf_op jit(solution)/shard_map/ppermute | solution.py:126
  43.3 7.4 %collective-permute-start.7 = (bf16[64,2048]{1,0:T(8,128)(2,1)}, bf16[64,2048]{1,0:T(8,128)(2,1)S(1)}, u32[]{:S(2)}, u32[]{:S(2)}) collective-permute-start(bf16[64,2048]{1,0:T(8,128)(2,1)} %collective-permute-done.refs_2_), channel_id=1, source_target_pairs={{0,8},{2,10},{8,16},{10,18},{16,24},{18,26},{24,28},{26,30},{28,20... | collective-permute-start | bytes 786440 | tf_op jit(solution)/shard_map/ppermute | solution.py:126
  48.3 8.1 %collective-permute-start.14 = (bf16[64,2048]{1,0:T(8,128)(2,1)}, bf16[64,2048]{1,0:T(8,128)(2,1)}, u32[]{:S(2)}, u32[]{:S(2)}) collective-permute-start(bf16[64,2048]{1,0:T(8,128)(2,1)} %collective-permute-done.1.refs_3_), channel_id=1, source_target_pairs={{0,8},{2,10},{8,16},{10,18},{16,24},{18,26},{24,28},{26,30},{28,20... | collective-permute-start | bytes 786440 | tf_op jit(solution)/shard_map/ppermute | solution.py:126
  50.6 6.7 %collective-permute-start.16 = (bf16[64,2048]{1,0:T(8,128)(2,1)}, bf16[64,2048]{1,0:T(8,128)(2,1)}, u32[]{:S(2)}, u32[]{:S(2)}) collective-permute-start(bf16[64,2048]{1,0:T(8,128)(2,1)} %collective-permute-done.2.refs_4_), channel_id=1, source_target_pairs={{8,0},{10,2},{16,8},{18,10},{24,16},{26,18},{28,24},{30,26},{20,28... | collective-permute-start | bytes 786440 | tf_op jit(solution)/shard_map/ppermute | solution.py:126
  56.4 7.0 %collective-permute-start.10 = (bf16[64,2048]{1,0:T(8,128)(2,1)}, bf16[64,2048]{1,0:T(8,128)(2,1)S(1)}, u32[]{:S(2)}, u32[]{:S(2)}) collective-permute-start(bf16[64,2048]{1,0:T(8,128)(2,1)} %collective-permute-done.3.refs_5_), channel_id=1, source_target_pairs={{8,0},{10,2},{16,8},{18,10},{24,16},{26,18},{28,24},{30,26},{20,28... | collective-permute-start | bytes 786440 | tf_op jit(solution)/shard_map/ppermute | solution.py:126
  57.3 7.5 %collective-permute-start.8 = (bf16[64,2048]{1,0:T(8,128)(2,1)S(1)}, bf16[64,2048]{1,0:T(8,128)(2,1)S(1)}, u32[]{:S(2)}, u32[]{:S(2)}) collective-permute-start(bf16[64,2048]{1,0:T(8,128)(2,1)S(1)} %collective-permute-done.7.refs_0_), channel_id=1, source_target_pairs={{0,8},{2,10},{8,16},{10,18},{16,24},{18,26},{24,28},{26,30},{28,20... | collective-permute-start | bytes 786440 | tf_op jit(solution)/shard_map/ppermute | solution.py:126
  58.5 0.7 copy-start.4
  63.4 7.2 %collective-permute-start.11 = (bf16[64,2048]{1,0:T(8,128)(2,1)S(1)}, bf16[64,2048]{1,0:T(8,128)(2,1)S(1)}, u32[]{:S(2)}, u32[]{:S(2)}) collective-permute-start(bf16[64,2048]{1,0:T(8,128)(2,1)S(1)} %collective-permute-done.10.refs_3_), channel_id=1, source_target_pairs={{8,0},{10,2},{16,8},{18,10},{24,16},{26,18},{28,24},{30,26},{20,28... | collective-permute-start | bytes 786440 | tf_op jit(solution)/shard_map/ppermute | solution.py:126
  64.0 0.7 copy-start.6
  64.9 7.0 %collective-permute-start.9 = (bf16[64,2048]{1,0:T(8,128)(2,1)S(1)}, bf16[64,2048]{1,0:T(8,128)(2,1)S(1)}, u32[]{:S(2)}, u32[]{:S(2)}) collective-permute-start(bf16[64,2048]{1,0:T(8,128)(2,1)S(1)} %collective-permute-done.8.refs_0_), channel_id=1, source_target_pairs={{0,8},{2,10},{8,16},{10,18},{16,24},{18,26},{24,28},{26,30},{28,20... | collective-permute-start | bytes 786440 | tf_op jit(solution)/shard_map/ppermute | solution.py:126
  66.3 0.7 copy-start.8
  70.6 7.3 %collective-permute-start.12 = (bf16[64,2048]{1,0:T(8,128)(2,1)S(1)}, bf16[64,2048]{1,0:T(8,128)(2,1)S(1)}, u32[]{:S(2)}, u32[]{:S(2)}) collective-permute-start(bf16[64,2048]{1,0:T(8,128)(2,1)S(1)} %collective-permute-done.11.refs_3_), channel_id=1, source_target_pairs={{8,0},{10,2},{16,8},{18,10},{24,16},{26,18},{28,24},{30,26},{20,28... | collective-permute-start | bytes 786440 | tf_op jit(solution)/shard_map/ppermute | solution.py:126
  71.0 0.7 copy-start.10
  71.9 0.7 copy-start.12
  72.6 23.7 %collective-permute-start.15 = (bf16[64,2048]{1,0:T(8,128)(2,1)}, bf16[64,2048]{1,0:T(8,128)(2,1)}, u32[]{:S(2)}, u32[]{:S(2)}) collective-permute-start(bf16[64,2048]{1,0:T(8,128)(2,1)} %collective-permute-done.14.refs_1_), channel_id=1, source_target_pairs={{0,8},{2,10},{8,16},{10,18},{16,24},{18,26},{24,28},{26,30},{28,20... | collective-permute-start | bytes 786440 | tf_op jit(solution)/shard_map/ppermute | solution.py:126
  77.9 0.7 copy-start.14
  78.6 17.7 %collective-permute-start.17 = (bf16[64,2048]{1,0:T(8,128)(2,1)}, bf16[64,2048]{1,0:T(8,128)(2,1)}, u32[]{:S(2)}, u32[]{:S(2)}) collective-permute-start(bf16[64,2048]{1,0:T(8,128)(2,1)} %collective-permute-done.16.refs_2_), channel_id=1, source_target_pairs={{8,0},{10,2},{16,8},{18,10},{24,16},{26,18},{28,24},{30,26},{20,28... | collective-permute-start | bytes 786440 | tf_op jit(solution)/shard_map/ppermute | solution.py:126
  80.3 1.9 %copy-start.1 = (bf16[1,2048,768]{2,1,0:T(8,128)(2,1)S(1)}, bf16[1,2048,768]{2,1,0:T(8,128)(2,1)}, u32[]{:S(2)}) copy-start(bf16[1,2048,768]{2,1,0:T(8,128)(2,1)} %refs_6_.3) | copy-start | bytes 9437188
  82.2 1.9 %copy-start.3 = (bf16[1,768,2048]{2,1,0:T(8,128)(2,1)S(1)}, bf16[1,768,2048]{2,1,0:T(8,128)(2,1)}, u32[]{:S(2)}) copy-start(bf16[1,768,2048]{2,1,0:T(8,128)(2,1)} %refs_7_.5) | copy-start | bytes 9437188
  84.1 0.9 copy-start.13
  85.0 0.9 copy-start.15
  86.0 10.3 %copy-start.9 = (bf16[64,2048]{1,0:T(8,128)(2,1)S(1)}, bf16[64,2048]{1,0:T(8,128)(2,1)}, u32[]{:S(2)}) copy-start(bf16[64,2048]{1,0:T(8,128)(2,1)} %copy-done.8) | copy-start | bytes 786436
  86.0 10.3 %copy-start.11 = (bf16[64,2048]{1,0:T(8,128)(2,1)S(1)}, bf16[64,2048]{1,0:T(8,128)(2,1)}, u32[]{:S(2)}) copy-start(bf16[64,2048]{1,0:T(8,128)(2,1)} %copy-done.10) | copy-start | bytes 786436
  94.4 14.7 %copy-start.2 = (bf16[1,2048,768]{2,1,0:T(8,128)(2,1)S(1)}, bf16[1,2048,768]{2,1,0:T(8,128)(2,1)}, u32[]{:S(2)}) copy-start(bf16[1,2048,768]{2,1,0:T(8,128)(2,1)} %refs_6_.3) | copy-start | bytes 9437188
  94.4 14.7 %copy-start.17 = (bf16[64,2048]{1,0:T(8,128)(2,1)S(1)}, bf16[64,2048]{1,0:T(8,128)(2,1)}, u32[]{:S(2)}) copy-start(bf16[64,2048]{1,0:T(8,128)(2,1)} %copy-done.16) | copy-start | bytes 786436
  94.5 14.7 %copy-start.18 = (f32[384,2]{1,0:T(8,128)S(1)}, f32[384,2]{1,0:T(8,128)}, u32[]{:S(2)}) copy-start(f32[384,2]{1,0:T(8,128)} %copy.61.refs_6_) | copy-start | bytes 9220
  94.5 37.8 %collective-permute-start.27 = (bf16[64,2048]{1,0:T(8,128)(2,1)S(1)}, bf16[64,2048]{1,0:T(8,128)(2,1)S(1)}, u32[]{:S(2)}, u32[]{:S(2)}) collective-permute-start(bf16[64,2048]{1,0:T(8,128)(2,1)S(1)} %get-tuple-element.33), channel_id=1, source_target_pairs={{0,8},{2,10},{8,16},{10,18},{16,24},{18,26},{24,28},{26,30},{28,20... | collective-permute-start | bytes 786440 | tf_op jit(solution)/shard_map/ppermute | solution.py:150
  106.8 27.4 %collective-permute-start.24 = (bf16[64,2048]{1,0:T(8,128)(2,1)S(1)}, bf16[64,2048]{1,0:T(8,128)(2,1)S(1)}, u32[]{:S(2)}, u32[]{:S(2)}) collective-permute-start(bf16[64,2048]{1,0:T(8,128)(2,1)S(1)} %get-tuple-element.30), channel_id=1, source_target_pairs={{8,0},{10,2},{16,8},{18,10},{24,16},{26,18},{28,24},{30,26},{20,28... | collective-permute-start | bytes 786440 | tf_op jit(solution)/shard_map/ppermute | solution.py:150
  107.1 27.5 %collective-permute-start.21 = (bf16[64,2048]{1,0:T(8,128)(2,1)S(1)}, bf16[64,2048]{1,0:T(8,128)(2,1)S(1)}, u32[]{:S(2)}, u32[]{:S(2)}) collective-permute-start(bf16[64,2048]{1,0:T(8,128)(2,1)S(1)} %get-tuple-element.26), channel_id=1, source_target_pairs={{0,8},{2,10},{8,16},{10,18},{16,24},{18,26},{24,28},{26,30},{28,20... | collective-permute-start | bytes 786440 | tf_op jit(solution)/shard_map/ppermute | solution.py:150
  108.8 12.9 %copy-start.5 = (bf16[64,2048]{1,0:T(8,128)(2,1)S(1)}, bf16[64,2048]{1,0:T(8,128)(2,1)}, u32[]{:S(2)}) copy-start(bf16[64,2048]{1,0:T(8,128)(2,1)} %copy-done.4) | copy-start | bytes 786436
  108.8 12.9 %copy-start.7 = (bf16[64,2048]{1,0:T(8,128)(2,1)S(1)}, bf16[64,2048]{1,0:T(8,128)(2,1)}, u32[]{:S(2)}) copy-start(bf16[64,2048]{1,0:T(8,128)(2,1)} %copy-done.6) | copy-start | bytes 786436
  108.8 27.6 %collective-permute-start.13 = (bf16[64,2048]{1,0:T(8,128)(2,1)S(1)}, bf16[64,2048]{1,0:T(8,128)(2,1)S(1)}, u32[]{:S(2)}, u32[]{:S(2)}) collective-permute-start(bf16[64,2048]{1,0:T(8,128)(2,1)S(1)} %get-tuple-element.22), channel_id=1, source_target_pairs={{8,0},{10,2},{16,8},{18,10},{24,16},{26,18},{28,24},{30,26},{20,28... | collective-permute-start | bytes 786440 | tf_op jit(solution)/shard_map/ppermute | solution.py:150
  132.4 9.3 %collective-permute-start.28 = (bf16[64,2048]{1,0:T(8,128)(2,1)S(1)}, bf16[64,2048]{1,0:T(8,128)(2,1)S(1)}, u32[]{:S(2)}, u32[]{:S(2)}) collective-permute-start(bf16[64,2048]{1,0:T(8,128)(2,1)S(1)} %add_convert_fusion.3), channel_id=1, source_target_pairs={{0,8},{2,10},{8,16},{10,18},{16,24},{18,26},{24,28},{26,30},{28,20... | collective-permute-start | bytes 786440 | tf_op jit(solution)/shard_map/ppermute | solution.py:150
  134.2 9.3 %collective-permute-start.25 = (bf16[64,2048]{1,0:T(8,128)(2,1)S(1)}, bf16[64,2048]{1,0:T(8,128)(2,1)S(1)}, u32[]{:S(2)}, u32[]{:S(2)}) collective-permute-start(bf16[64,2048]{1,0:T(8,128)(2,1)S(1)} %add_convert_fusion.5), channel_id=1, source_target_pairs={{8,0},{10,2},{16,8},{18,10},{24,16},{26,18},{28,24},{30,26},{20,28... | collective-permute-start | bytes 786440 | tf_op jit(solution)/shard_map/ppermute | solution.py:150
  134.6 12.7 %collective-permute-start.22 = (bf16[64,2048]{1,0:T(8,128)(2,1)S(1)}, bf16[64,2048]{1,0:T(8,128)(2,1)S(1)}, u32[]{:S(2)}, u32[]{:S(2)}) collective-permute-start(bf16[64,2048]{1,0:T(8,128)(2,1)S(1)} %add_convert_fusion.8), channel_id=1, source_target_pairs={{0,8},{2,10},{8,16},{10,18},{16,24},{18,26},{24,28},{26,30},{28,20... | collective-permute-start | bytes 786440 | tf_op jit(solution)/shard_map/ppermute | solution.py:150
  136.5 12.7 %collective-permute-start.18 = (bf16[64,2048]{1,0:T(8,128)(2,1)S(1)}, bf16[64,2048]{1,0:T(8,128)(2,1)S(1)}, u32[]{:S(2)}, u32[]{:S(2)}) collective-permute-start(bf16[64,2048]{1,0:T(8,128)(2,1)S(1)} %add_convert_fusion.11), channel_id=1, source_target_pairs={{8,0},{10,2},{16,8},{18,10},{24,16},{26,18},{28,24},{30,26},{20,28... | collective-permute-start | bytes 786440 | tf_op jit(solution)/shard_map/ppermute | solution.py:150
  141.7 9.2 %collective-permute-start.29 = (bf16[64,2048]{1,0:T(8,128)(2,1)S(1)}, bf16[64,2048]{1,0:T(8,128)(2,1)S(1)}, u32[]{:S(2)}, u32[]{:S(2)}) collective-permute-start(bf16[64,2048]{1,0:T(8,128)(2,1)S(1)} %add_convert_fusion.2), channel_id=1, source_target_pairs={{0,8},{2,10},{8,16},{10,18},{16,24},{18,26},{24,28},{26,30},{28,20... | collective-permute-start | bytes 786440 | tf_op jit(solution)/shard_map/ppermute | solution.py:150
  143.6 12.4 %collective-permute-start.26 = (bf16[64,2048]{1,0:T(8,128)(2,1)S(1)}, bf16[64,2048]{1,0:T(8,128)(2,1)S(1)}, u32[]{:S(2)}, u32[]{:S(2)}) collective-permute-start(bf16[64,2048]{1,0:T(8,128)(2,1)S(1)} %add_convert_fusion.4), channel_id=1, source_target_pairs={{8,0},{10,2},{16,8},{18,10},{24,16},{26,18},{28,24},{30,26},{20,28... | collective-permute-start | bytes 786440 | tf_op jit(solution)/shard_map/ppermute | solution.py:150
  147.3 10.2 %collective-permute-start.23 = (bf16[64,2048]{1,0:T(8,128)(2,1)S(1)}, bf16[64,2048]{1,0:T(8,128)(2,1)S(1)}, u32[]{:S(2)}, u32[]{:S(2)}) collective-permute-start(bf16[64,2048]{1,0:T(8,128)(2,1)S(1)} %add_convert_fusion.7), channel_id=1, source_target_pairs={{0,8},{2,10},{8,16},{10,18},{16,24},{18,26},{24,28},{26,30},{28,20... | collective-permute-start | bytes 786440 | tf_op jit(solution)/shard_map/ppermute | solution.py:150
  149.2 6.4 %collective-permute-start.19 = (bf16[64,2048]{1,0:T(8,128)(2,1)S(1)}, bf16[64,2048]{1,0:T(8,128)(2,1)S(1)}, u32[]{:S(2)}, u32[]{:S(2)}) collective-permute-start(bf16[64,2048]{1,0:T(8,128)(2,1)S(1)} %add_convert_fusion.10), channel_id=1, source_target_pairs={{8,0},{10,2},{16,8},{18,10},{24,16},{26,18},{28,24},{30,26},{20,28... | collective-permute-start | bytes 786440 | tf_op jit(solution)/shard_map/ppermute | solution.py:150
  151.0 6.4 %collective-permute-start.30 = (bf16[64,2048]{1,0:T(8,128)(2,1)S(1)}, bf16[64,2048]{1,0:T(8,128)(2,1)S(1)}, u32[]{:S(2)}, u32[]{:S(2)}) collective-permute-start(bf16[64,2048]{1,0:T(8,128)(2,1)S(1)} %add_convert_fusion.1), channel_id=1, source_target_pairs={{0,8},{2,10},{8,16},{10,18},{16,24},{18,26},{24,28},{26,30},{28,20... | collective-permute-start | bytes 786440 | tf_op jit(solution)/shard_map/ppermute | solution.py:150
  155.7 6.4 %collective-permute-start.20 = (bf16[64,2048]{1,0:T(8,128)(2,1)S(1)}, bf16[64,2048]{1,0:T(8,128)(2,1)S(1)}, u32[]{:S(2)}, u32[]{:S(2)}) collective-permute-start(bf16[64,2048]{1,0:T(8,128)(2,1)S(1)} %add_convert_fusion.9), channel_id=1, source_target_pairs={{8,0},{10,2},{16,8},{18,10},{24,16},{26,18},{28,24},{30,26},{20,28... | collective-permute-start | bytes 786440 | tf_op jit(solution)/shard_map/ppermute | solution.py:150

commit v2 on v1

v2 whole, which is shorter than its diff:
```python
import functools

import jax
import jax.numpy as jnp
from jax import lax
from jax.experimental import pallas as pl
from jax.experimental.pallas import tpu as pltpu
from jax.sharding import PartitionSpec as P

LANES = 128


def pack_kernel(n_dev, tokens_ref, ids_ref, scores_ref, partner_ref, out_ref):
    rows, width = tokens_ref.shape
    extra = out_ref.shape[1] - width
    lane = lax.broadcasted_iota(jnp.int32, (extra, 1), 0)
    served = jnp.full((extra, 1), -1, jnp.int32)
    for slot in range(n_dev):
        hit = (lane == slot) | (lane == slot + n_dev)
        served = jnp.where(hit, partner_ref[slot], served)
    total = jnp.zeros((extra, rows), jnp.float32)
    for k in range(ids_ref.shape[0]):
        total += jnp.where(ids_ref[k : k + 1, :] == served, scores_ref[k : k + 1, :], 0.0)
    high = total.astype(jnp.bfloat16).astype(jnp.float32)
    tail = jnp.where(lane < n_dev, high, total - high).T.astype(jnp.bfloat16)
    out_ref[:, :width] = tokens_ref[...]
    out_ref[:, width:] = tail


def pack(tokens, expert_ids, gate_scores, partner, n_dev):
    rows, width = tokens.shape
    extra = -(-2 * n_dev // LANES) * LANES
    near = pl.BlockSpec(memory_space=pltpu.VMEM)
    return pl.pallas_call(
        functools.partial(pack_kernel, n_dev),
        in_specs=[near, near, near, pl.BlockSpec(memory_space=pltpu.SMEM)],
        out_specs=near,
        out_shape=jax.ShapeDtypeStruct((rows, width + extra), jnp.bfloat16),
        compiler_params=pltpu.CompilerParams(vmem_limit_bytes=6 * 2**20),
    )(tokens, expert_ids.T, gate_scores.T, partner)


def ffn_kernel(n_in, n_out, n_dev, *refs):
    x_refs, weights, refs = refs[:n_in], refs[n_in : n_in + 6], refs[n_in + 6 :]
    out_refs, (rows, total) = refs[:n_out], refs[n_out:]
    half = out_refs[0].shape[0]
    width = total.shape[1]
    me = lax.axis_index("ep")
    slots = (me, me + 1 - 2 * (me % 2))
    tails = []
    at = 0
    for x_ref in x_refs:
        rows[pl.ds(at, x_ref.shape[0]), :] = x_ref[:, :width]
        tails.append(x_ref[:, width:].astype(jnp.float32))
        at += x_ref.shape[0]
    tails = jnp.concatenate(tails, axis=0)
    lane = lax.broadcasted_iota(jnp.int32, tails.shape, 1)
    for expert, slot in enumerate(slots):
        hit = (lane == slot) | (lane == slot + n_dev)
        score = jnp.sum(jnp.where(hit, tails, 0.0), axis=1, keepdims=True)
        gate_ref, up_ref, down_ref = weights[3 * expert : 3 * expert + 3]
        x = rows[...]
        gate = jnp.dot(x, gate_ref[0], preferred_element_type=jnp.float32)
        up = jnp.dot(x, up_ref[0], preferred_element_type=jnp.float32)
        hidden = (gate / (1.0 + jnp.exp(-gate)) * up).astype(jnp.bfloat16)
        out = jnp.dot(hidden, down_ref[0], preferred_element_type=jnp.float32) * score
        if expert == 0:
            total[...] = out
        else:
            out = total[...] + out
            for i, out_ref in enumerate(out_refs):
                out_ref[...] = out[i * half : (i + 1) * half].astype(out_ref.dtype)


def ffn(blocks, half, kinds, own, other, n_dev):
    _, width, ff = own[0].shape
    m = sum(block.shape[0] for block in blocks)
    n_in, n_out = len(blocks), len(kinds)
    near = pl.BlockSpec(memory_space=pltpu.VMEM)
    return pl.pallas_call(
        functools.partial(ffn_kernel, n_in, n_out, n_dev),
        in_specs=[near] * (n_in + 6),
        out_specs=[near] * n_out,
        out_shape=[jax.ShapeDtypeStruct((half, width), kind) for kind in kinds],
        scratch_shapes=[pltpu.VMEM((m, width), jnp.bfloat16), pltpu.VMEM((m, width), jnp.float32)],
        compiler_params=pltpu.CompilerParams(vmem_limit_bytes=16 * 2**20),
        cost_estimate=pl.CostEstimate(
            flops=12 * m * width * ff, bytes_accessed=12 * width * ff + 6 * m * width, transcendentals=2 * m * ff
        ),
    )(*blocks, *own, *other)


def ring_order(chips):
    return list(range(0, chips, 2)) + list(range(1, chips, 2))[::-1]


def on_device(tokens, expert_ids, gate_scores, gate_weight, up_weight, down_weight, partner):
    n_dev = lax.axis_size("ep")
    chips = n_dev // 2
    far = chips // 2
    order = ring_order(chips)

    def shift(by):
        return [(order[i] * 2 + k, order[(i + by) % chips] * 2 + k) for i in range(chips) for k in range(2)]

    perm = (shift(1), shift(-1))
    swap = [(i, i ^ 1) for i in range(n_dev)]
    own = (gate_weight, up_weight, down_weight)

    def tie(value, *deps):
        return lax.optimization_barrier((value, deps))[0]

    packed = pack(tokens, expert_ids, gate_scores, partner, n_dev)
    half = tokens.shape[0] // 2
    other = [lax.ppermute(w, "ep", swap) for w in own]
    first = [lax.ppermute(packed, "ep", perm[d]) for d in range(2)]
    held = {(d, h, 1): block[h * half : (h + 1) * half] for d, block in enumerate(first) for h in range(2)}
    last = {(d, h): far if d == h else far - 1 for d in range(2) for h in range(2)}

    def keys(s):
        if s == 0:
            return [(0, 0, 0), (0, 1, 0)]
        return [(d, h, s) for h in range(2) for d in range(2) if s <= last[d, h]]

    done = {}

    def compute(s, blocks):
        names = [(d, h, 1) for d in range(2) for h in range(2)] if s == 1 else keys(s)
        kinds = [jnp.bfloat16 if n[2] and n[2] == last[n[:2]] else jnp.float32 for n in names]
        done.update(zip(names, ffn(blocks, half, kinds, own, other, n_dev)))

    for s in range(1, far + 1):
        if s > 1:
            for d, h, _ in keys(s):
                deps = other if s == 2 else [done[keys(s - 2)[0]]]
                if s == 3:
                    deps = deps + [done[keys(0)[0]]]
                if s == far:
                    deps = deps + [held[d, 1 - h, s - 1]]
                held[d, h, s] = lax.ppermute(tie(held[d, h, s - 1], *deps), "ep", perm[d])
        blocks = first if s == 1 else [held[k] for k in keys(s)]
        compute(s, blocks if s == 1 else tie(blocks, done[keys(s - 1)[0]]))
        if s == 1:
            compute(0, [packed])
    for k in keys(far - 1):
        done[k] = tie(done[k], *[held[k] for k in keys(far)])

    back = {}
    for s in range(far, 0, -1):
        for d, h, _ in keys(s):
            part = done[d, h, s]
            if (d, h) in back:
                part = (back[d, h].astype(jnp.float32) + part).astype(jnp.bfloat16)
            back[d, h] = lax.ppermute(part, "ep", perm[1 - d])
    out = [
        (done[0, h, 0] + back[0, h].astype(jnp.float32) + back[1, h].astype(jnp.float32)).astype(jnp.bfloat16)
        for h in range(2)
    ]
    return jnp.concatenate(out, axis=0)


def solution(mesh):
    rows = P(("dp", "ep"), None)
    stacks = P(("dp", "ep"), None, None)
    return jax.shard_map(
        on_device,
        mesh=mesh,
        in_specs=(rows, rows, rows, stacks, stacks, stacks, P()),
        out_specs=rows,
        check_vma=False,
    )
```

time: 163 us -> 107 us (0.66)
  blocking collectives: 25.7 us -> 0 us
  Pallas kernels: 42 us -> 21.5 us
  local copies, waits for them, and re-layouts: 14 us -> 6.93 us
  waiting for transfers between devices: 51.2 us -> 47.6 us
  starting transfers between devices: 26.6 us -> 28.9 us
  other arithmetic: 3.22 us -> 1.55 us
    all_gather x1 -> x0, blocking collectives: 25.7 us -> none  [on_device(): lax.all_gather(slot_scores, 'ep', axis=0).reshape(chips, 2, n_dev, rows)]
    pallas_call x4 -> x6, Pallas kernels: 42 us -> 21.5 us  [the longest x5 20.8 us: ffn(): pl.pallas_call(functools.partial(ffn_kernel, n_in, n_out, n_dev), in_spec...]
    ppermute x17 -> x15, waiting for transfers between devices: 32.4 us -> 20 us  [the longest x2 14.4 us: on_device(): first = [lax.ppermute(packed, 'ep', perm[d]) for d in range(2)]]
    ppermute x14, waiting for transfers between devices: 18.8 us -> 27.6 us  [on_device(): back[d, h] = lax.ppermute(part, 'ep', perm[1 - d])]
    unnamed x39 -> x14, local copies, waits for them, and re-layouts: 9.94 us -> 6.85 us
    slice x6 -> x2, local copies, waits for them, and re-layouts: 2.13 us -> 0.08 us  [on_device(): block[h * half:(h + 1) * half]]
    ppermute x17 -> x15, starting transfers between devices: 12.1 us -> 14.2 us  [the longest x10 10.2 us: on_device(): held[d, h, s] = lax.ppermute(tie(held[d, h, s - 1], *deps), 'ep', perm[d])]
  transfers between devices with their start and end apart: 31 -> 29, of which waited for: 14 -> 14; matrix products, arithmetic and copies ran while one was open for 4% -> 1% of each run, Pallas kernels for 26% -> 17%
where the time goes in v2:
time: 107 us
  waiting for transfers between devices  47.6 us (44%)
  starting transfers between devices  28.9 us (27%)
  Pallas kernels  21.5 us (20%)
  local copies, waits for them, and re-layouts  6.93 us (6%)
  other arithmetic  1.55 us (1%)
    ppermute x14, waiting for transfers between devices, on_device(): back[d, h] = lax.ppermute(part, 'ep', perm[1 - d])  27.6 us
    pallas_call x5, Pallas kernels, ffn(): pl.pallas_call(functools.partial(ffn_kernel, n_in, n_out, n_dev), in_spec...  20.8 us
    ppermute x14, starting transfers between devices, on_device(): back[d, h] = lax.ppermute(part, 'ep', perm[1 - d])  14.8 us
    ppermute x2, waiting for transfers between devices, on_device(): first = [lax.ppermute(packed, 'ep', perm[d]) for d in range(2)]  14.4 us
    ppermute x10, starting transfers between devices, on_device(): held[d, h, s] = lax.ppermute(tie(held[d, h, s - 1], *deps), 'ep', perm[d])  10.2 us
    unnamed x14, local copies, waits for them, and re-layouts  6.85 us
    ppermute x10, waiting for transfers between devices, on_device(): held[d, h, s] = lax.ppermute(tie(held[d, h, s - 1], *deps), 'ep', perm[d])  5.61 us
    ppermute x2, starting transfers between devices, on_device(): first = [lax.ppermute(packed, 'ep', perm[d]) for d in range(2)]  2.97 us
  transfers between devices with their start and end apart: 29, of which 14 were waited for; matrix products, arithmetic and copies ran while one was open for 1% of the time, Pallas kernels for 17%

profile of v2, /device:TPU:0, one launch (start us, length us, event | category | flops | bytes accessed | tf_op | source)
XLA Modules:
  0.0 106.7 jit_solution(3899904773382201486)
XLA Ops:
  0.0 0.5 collective-permute-start
  0.5 0.1 collective-permute-start.1
  0.5 0.4 collective-permute-start.2
  1.0 1.0 copy-done.3
  2.0 0.7 copy-done.4
  2.7 0.7 copy-done.5
  3.4 0.7 copy-done.6
  4.0 0.7 shard_map.73.refs_0_
  4.7 3.0 %collective-permute-start.3 = (bf16[128,2176]{1,0:T(8,128)(2,1)S(1)}, bf16[128,2176]{1,0:T(8,128)(2,1)S(1)}, u32[]{:S(2)}, u32[]{:S(2)}) collective-permute-start(bf16[128,2176]{1,0:T(8,128)(2,1)S(1)} %shard_map.73.refs_0_), channel_id=1, source_target_pairs={{0,8},{2,10},{8,16},{10,18},{16,24},{18,26},{24,28},{26,30},{28,20... | collective-permute-start | bytes 1671176 | tf_op jit(solution)/shard_map/ppermute | solution.py:116
  7.7 12.9 %collective-permute-done.3.refs_0_ = bf16[128,2176]{1,0:T(8,128)(2,1)S(1)} collective-permute-done((bf16[128,2176]{1,0:T(8,128)(2,1)S(1)}, bf16[128,2176]{1,0:T(8,128)(2,1)S(1)}, u32[]{:S(2)}, u32[]{:S(2)}) %collective-permute-start.3) | collective-permute-done | bytes 557088 | tf_op jit(solution)/shard_map/ppermute | solution.py:116
  20.6 1.5 %collective-permute-done.5.refs_1_ = bf16[128,2176]{1,0:T(8,128)(2,1)S(1)} collective-permute-done((bf16[128,2176]{1,0:T(8,128)(2,1)S(1)}, bf16[128,2176]{1,0:T(8,128)(2,1)S(1)}, u32[]{:S(2)}, u32[]{:S(2)}) %collective-permute-start.5) | collective-permute-done | bytes 557088 | tf_op jit(solution)/shard_map/ppermute | solution.py:116
  22.1 0.0 collective-permute-done.1.refs_5_.refs_6_.refs_8_
  22.2 0.0 collective-permute-done.2.refs_6_.refs_7_.refs_9_
  22.2 1.6 %collective-permute-start.4 = (bf16[64,2176]{1,0:T(8,128)(2,1)S(1)}, bf16[64,2176]{1,0:T(8,128)(2,1)S(1)}, u32[]{:S(2)}, u32[]{:S(2)}) collective-permute-start(bf16[64,2176]{1,0:T(8,128)(2,1)S(1)} %get-tuple-element.46), channel_id=1, source_target_pairs={{0,8},{2,10},{8,16},{10,18},{16,24},{18,26},{24,28},{26,30},{28,20... | collective-permute-start | bytes 835592 | tf_op jit(solution)/shard_map/ppermute | solution.py:140
  23.8 0.4 collective-permute-start.7
  24.2 1.6 %collective-permute-start.8 = (bf16[64,2176]{1,0:T(8,128)(2,1)S(1)}, bf16[64,2176]{1,0:T(8,128)(2,1)S(1)}, u32[]{:S(2)}, u32[]{:S(2)}) collective-permute-start(bf16[64,2176]{1,0:T(8,128)(2,1)S(1)} %get-tuple-element.50), channel_id=1, source_target_pairs={{0,8},{2,10},{8,16},{10,18},{16,24},{18,26},{24,28},{26,30},{28,20... | collective-permute-start | bytes 835592 | tf_op jit(solution)/shard_map/ppermute | solution.py:140
  25.8 0.4 collective-permute-start.9
  26.3 1.9 %copy-done.1 = bf16[1,2048,768]{2,1,0:T(8,128)(2,1)S(1)} copy-done((bf16[1,2048,768]{2,1,0:T(8,128)(2,1)S(1)}, bf16[1,2048,768]{2,1,0:T(8,128)(2,1)}, u32[]{:S(2)}) %copy-start.1) | copy-done | bytes 3145752
  28.2 1.9 %copy-done.2 = bf16[1,768,2048]{2,1,0:T(8,128)(2,1)S(1)} copy-done((bf16[1,768,2048]{2,1,0:T(8,128)(2,1)S(1)}, bf16[1,768,2048]{2,1,0:T(8,128)(2,1)}, u32[]{:S(2)}) %copy-start.2) | copy-done | bytes 3145752
  30.1 5.1 %shard_map.75 = (f32[64,2048]{1,0:T(8,128)S(1)}, f32[64,2048]{1,0:T(8,128)S(1)}, f32[64,2048]{1,0:T(8,128)S(1)}, f32[64,2048]{1,0:T(8,128)S(1)}) custom-call(bf16[128,2176]{1,0:T(8,128)(2,1)S(1)} %collective-permute-done.3.refs_0_, bf16[128,2176]{1,0:T(8,128)(2,1)S(1)} %collective-permute-done.5.refs_1_, bf16[1,2048,768]{2,1,0:T(8,128)(2,1)S(1)} %copy-done, ...), custom_call_target="tpu_custom_call" | custom-call | flops 4831838208 | bytes 22020096 | tf_op jit(solution)/shard_map/pallas_call | solution.py:80
  35.1 2.8 %shard_map.74 = (f32[64,2048]{1,0:T(8,128)S(1)}, f32[64,2048]{1,0:T(8,128)S(1)}) custom-call(bf16[128,2176]{1,0:T(8,128)(2,1)S(1)} %shard_map.73.refs_0_, bf16[1,2048,768]{2,1,0:T(8,128)(2,1)S(1)} %copy-done, bf16[1,2048,768]{2,1,0:T(8,128)(2,1)S(1)} %copy-done.1, bf16[1,768,2048]{2,1,0:T(8,128)(2,1)S(1)} %copy-done.2, ...), custom_call_target="tpu_custom_call" | custom-call | flops 2415919104 | bytes 20447232 | tf_op jit(solution)/shard_map/pallas_call | solution.py:80
  37.9 0.0 collective-permute-done.4.refs_0_
  37.9 0.0 collective-permute-done.7.refs_1_
  38.0 1.6 %collective-permute-start.6 = (bf16[64,2176]{1,0:T(8,128)(2,1)S(1)}, bf16[64,2176]{1,0:T(8,128)(2,1)S(1)}, u32[]{:S(2)}, u32[]{:S(2)}) collective-permute-start(bf16[64,2176]{1,0:T(8,128)(2,1)S(1)} %collective-permute-done.4.refs_0_), channel_id=1, source_target_pairs={{0,8},{2,10},{8,16},{10,18},{16,24},{18,26},{24,28},{26,30},{28,20... | collective-permute-start | bytes 835592 | tf_op jit(solution)/shard_map/ppermute | solution.py:140
  39.6 0.4 collective-permute-start.13
  40.1 1.6 %collective-permute-start.10 = (bf16[64,2176]{1,0:T(8,128)(2,1)S(1)}, bf16[64,2176]{1,0:T(8,128)(2,1)S(1)}, u32[]{:S(2)}, u32[]{:S(2)}) collective-permute-start(bf16[64,2176]{1,0:T(8,128)(2,1)S(1)} %collective-permute-done.8.refs_2_), channel_id=1, source_target_pairs={{0,8},{2,10},{8,16},{10,18},{16,24},{18,26},{24,28},{26,30},{28,20... | collective-permute-start | bytes 835592 | tf_op jit(solution)/shard_map/ppermute | solution.py:140
  41.6 0.4 collective-permute-start.12
  42.1 5.1 %shard_map.76 = (f32[64,2048]{1,0:T(8,128)S(1)}, f32[64,2048]{1,0:T(8,128)S(1)}, f32[64,2048]{1,0:T(8,128)S(1)}, f32[64,2048]{1,0:T(8,128)S(1)}) custom-call(bf16[64,2176]{1,0:T(8,128)(2,1)S(1)} %collective-permute-done.4.refs_0_, bf16[64,2176]{1,0:T(8,128)(2,1)S(1)} %collective-permute-done.7.refs_1_, bf16[64,2176]{1,0:T(8,128)(2,1)S(1)} %collective-permute-done.8.refs_2_, ...), custom_call_target="tpu_custom_call" | custom-call | flops 4831838208 | bytes 22020096 | tf_op jit(solution)/shard_map/pallas_call | solution.py:80
  47.2 0.3 collective-permute-done.6.refs_0_
  47.5 1.3 %collective-permute-done.13.refs_1_ = bf16[64,2176]{1,0:T(8,128)(2,1)S(1)} collective-permute-done((bf16[64,2176]{1,0:T(8,128)(2,1)S(1)}, bf16[64,2176]{1,0:T(8,128)(2,1)S(1)}, u32[]{:S(2)}, u32[]{:S(2)}) %collective-permute-start.13) | collective-permute-done | bytes 278560 | tf_op jit(solution)/shard_map/ppermute | solution.py:140
  48.8 1.7 %collective-permute-done.10.refs_2_ = bf16[64,2176]{1,0:T(8,128)(2,1)S(1)} collective-permute-done((bf16[64,2176]{1,0:T(8,128)(2,1)S(1)}, bf16[64,2176]{1,0:T(8,128)(2,1)S(1)}, u32[]{:S(2)}, u32[]{:S(2)}) %collective-permute-start.10) | collective-permute-done | bytes 278560 | tf_op jit(solution)/shard_map/ppermute | solution.py:140
  50.5 1.3 %collective-permute-done.12.refs_3_ = bf16[64,2176]{1,0:T(8,128)(2,1)S(1)} collective-permute-done((bf16[64,2176]{1,0:T(8,128)(2,1)S(1)}, bf16[64,2176]{1,0:T(8,128)(2,1)S(1)}, u32[]{:S(2)}, u32[]{:S(2)}) %collective-permute-start.12) | collective-permute-done | bytes 278560 | tf_op jit(solution)/shard_map/ppermute | solution.py:140
  51.8 1.6 %collective-permute-start.11 = (bf16[64,2176]{1,0:T(8,128)(2,1)S(1)}, bf16[64,2176]{1,0:T(8,128)(2,1)S(1)}, u32[]{:S(2)}, u32[]{:S(2)}) collective-permute-start(bf16[64,2176]{1,0:T(8,128)(2,1)S(1)} %collective-permute-done.6.refs_0_), channel_id=1, source_target_pairs={{0,8},{2,10},{8,16},{10,18},{16,24},{18,26},{24,28},{26,30},{28,20... | collective-permute-start | bytes 835592 | tf_op jit(solution)/shard_map/ppermute | solution.py:140
  53.3 0.4 collective-permute-start.14
  53.8 5.1 %shard_map.77 = (f32[64,2048]{1,0:T(8,128)S(1)}, bf16[64,2048]{1,0:T(8,128)(2,1)S(1)}, bf16[64,2048]{1,0:T(8,128)(2,1)S(1)}, f32[64,2048]{1,0:T(8,128)S(1)}) custom-call(bf16[64,2176]{1,0:T(8,128)(2,1)S(1)} %collective-permute-done.6.refs_0_, bf16[64,2176]{1,0:T(8,128)(2,1)S(1)} %collective-permute-done.13.refs_1_, ...), custom_call_target="tpu_custom_call" | custom-call | flops 4831838208 | bytes 22020096 | tf_op jit(solution)/shard_map/pallas_call | solution.py:80
  58.9 1.0 collective-permute-done.14.refs_1_
  59.9 2.8 %shard_map.78 = (bf16[64,2048]{1,0:T(8,128)(2,1)S(1)}, bf16[64,2048]{1,0:T(8,128)(2,1)S(1)}) custom-call(bf16[64,2176]{1,0:T(8,128)(2,1)S(1)} %collective-permute-done.11.refs_0_, bf16[64,2176]{1,0:T(8,128)(2,1)S(1)} %collective-permute-done.14.refs_1_, bf16[1,2048,768]{2,1,0:T(8,128)(2,1)S(1)} %copy-done, bf16[1,2048,768]{2,1,0:T(8,128)(2,1)S(1)} %copy-done.1, ...), custom_call_target="tpu_custom_call" | custom-call | flops 2415919104 | bytes 20447232 | tf_op jit(solution)/shard_map/pallas_call | solution.py:80
  62.7 1.6 %collective-permute-start.25 = (bf16[64,2048]{1,0:T(8,128)(2,1)S(1)}, bf16[64,2048]{1,0:T(8,128)(2,1)S(1)}, u32[]{:S(2)}, u32[]{:S(2)}) collective-permute-start(bf16[64,2048]{1,0:T(8,128)(2,1)S(1)} %get-tuple-element.80), channel_id=1, source_target_pairs={{0,8},{2,10},{8,16},{10,18},{16,24},{18,26},{24,28},{26,30},{28,20... | collective-permute-start | bytes 786440 | tf_op jit(solution)/shard_map/ppermute | solution.py:154
  64.2 0.5 collective-permute-start.22
  64.8 1.5 %collective-permute-start.19 = (bf16[64,2048]{1,0:T(8,128)(2,1)S(1)}, bf16[64,2048]{1,0:T(8,128)(2,1)S(1)}, u32[]{:S(2)}, u32[]{:S(2)}) collective-permute-start(bf16[64,2048]{1,0:T(8,128)(2,1)S(1)} %get-tuple-element.72), channel_id=1, source_target_pairs={{0,8},{2,10},{8,16},{10,18},{16,24},{18,26},{24,28},{26,30},{28,20... | collective-permute-start | bytes 786440 | tf_op jit(solution)/shard_map/ppermute | solution.py:154
  66.3 0.5 collective-permute-start.15
  66.8 5.2 %collective-permute-done.25 = bf16[64,2048]{1,0:T(8,128)(2,1)S(1)} collective-permute-done((bf16[64,2048]{1,0:T(8,128)(2,1)S(1)}, bf16[64,2048]{1,0:T(8,128)(2,1)S(1)}, u32[]{:S(2)}, u32[]{:S(2)}) %collective-permute-start.25) | collective-permute-done | bytes 262176 | tf_op jit(solution)/shard_map/ppermute | solution.py:154
  72.0 1.6 %collective-permute-start.26 = (bf16[64,2048]{1,0:T(8,128)(2,1)S(1)}, bf16[64,2048]{1,0:T(8,128)(2,1)S(1)}, u32[]{:S(2)}, u32[]{:S(2)}) collective-permute-start(bf16[64,2048]{1,0:T(8,128)(2,1)S(1)} %add_convert_fusion.3), channel_id=1, source_target_pairs={{0,8},{2,10},{8,16},{10,18},{16,24},{18,26},{24,28},{26,30},{28,20... | collective-permute-start | bytes 786440 | tf_op jit(solution)/shard_map/ppermute | solution.py:154
  73.6 0.6 collective-permute-start.23
  74.2 3.4 %collective-permute-done.19 = bf16[64,2048]{1,0:T(8,128)(2,1)S(1)} collective-permute-done((bf16[64,2048]{1,0:T(8,128)(2,1)S(1)}, bf16[64,2048]{1,0:T(8,128)(2,1)S(1)}, u32[]{:S(2)}, u32[]{:S(2)}) %collective-permute-start.19) | collective-permute-done | bytes 262176 | tf_op jit(solution)/shard_map/ppermute | solution.py:154
  77.6 1.6 %collective-permute-start.20 = (bf16[64,2048]{1,0:T(8,128)(2,1)S(1)}, bf16[64,2048]{1,0:T(8,128)(2,1)S(1)}, u32[]{:S(2)}, u32[]{:S(2)}) collective-permute-start(bf16[64,2048]{1,0:T(8,128)(2,1)S(1)} %add_convert_fusion.8), channel_id=1, source_target_pairs={{0,8},{2,10},{8,16},{10,18},{16,24},{18,26},{24,28},{26,30},{28,20... | collective-permute-start | bytes 786440 | tf_op jit(solution)/shard_map/ppermute | solution.py:154
  79.3 0.6 collective-permute-start.16
  79.8 3.4 %collective-permute-done.26 = bf16[64,2048]{1,0:T(8,128)(2,1)S(1)} collective-permute-done((bf16[64,2048]{1,0:T(8,128)(2,1)S(1)}, bf16[64,2048]{1,0:T(8,128)(2,1)S(1)}, u32[]{:S(2)}, u32[]{:S(2)}) %collective-permute-start.26) | collective-permute-done | bytes 262176 | tf_op jit(solution)/shard_map/ppermute | solution.py:154
  83.3 1.6 %collective-permute-start.27 = (bf16[64,2048]{1,0:T(8,128)(2,1)S(1)}, bf16[64,2048]{1,0:T(8,128)(2,1)S(1)}, u32[]{:S(2)}, u32[]{:S(2)}) collective-permute-start(bf16[64,2048]{1,0:T(8,128)(2,1)S(1)} %add_convert_fusion.2), channel_id=1, source_target_pairs={{0,8},{2,10},{8,16},{10,18},{16,24},{18,26},{24,28},{26,30},{28,20... | collective-permute-start | bytes 786440 | tf_op jit(solution)/shard_map/ppermute | solution.py:154
  84.8 0.1 add_convert_fusion.4
  84.9 0.6 collective-permute-start.24
  85.5 4.4 %collective-permute-done.16 = bf16[64,2048]{1,0:T(8,128)(2,1)S(1)} collective-permute-done((bf16[64,2048]{1,0:T(8,128)(2,1)S(1)}, bf16[64,2048]{1,0:T(8,128)(2,1)S(1)}, u32[]{:S(2)}, u32[]{:S(2)}) %collective-permute-start.16) | collective-permute-done | bytes 262176 | tf_op jit(solution)/shard_map/ppermute | solution.py:154
  89.9 0.9 collective-permute-start.17
  90.9 1.2 %collective-permute-start.21 = (bf16[64,2048]{1,0:T(8,128)(2,1)S(1)}, bf16[64,2048]{1,0:T(8,128)(2,1)S(1)}, u32[]{:S(2)}, u32[]{:S(2)}) collective-permute-start(bf16[64,2048]{1,0:T(8,128)(2,1)S(1)} %add_convert_fusion.7), channel_id=1, source_target_pairs={{0,8},{2,10},{8,16},{10,18},{16,24},{18,26},{24,28},{26,30},{28,20... | collective-permute-start | bytes 786440 | tf_op jit(solution)/shard_map/ppermute | solution.py:154
  92.1 6.2 %collective-permute-done.17 = bf16[64,2048]{1,0:T(8,128)(2,1)S(1)} collective-permute-done((bf16[64,2048]{1,0:T(8,128)(2,1)S(1)}, bf16[64,2048]{1,0:T(8,128)(2,1)S(1)}, u32[]{:S(2)}, u32[]{:S(2)}) %collective-permute-start.17) | collective-permute-done | bytes 262176 | tf_op jit(solution)/shard_map/ppermute | solution.py:154
  98.3 0.1 add_convert_fusion.9
  98.4 0.9 collective-permute-start.18
  99.3 0.1 add_convert_fusion.1
  99.3 1.2 %collective-permute-start.28 = (bf16[64,2048]{1,0:T(8,128)(2,1)S(1)}, bf16[64,2048]{1,0:T(8,128)(2,1)S(1)}, u32[]{:S(2)}, u32[]{:S(2)}) collective-permute-start(bf16[64,2048]{1,0:T(8,128)(2,1)S(1)} %add_convert_fusion.1), channel_id=1, source_target_pairs={{0,8},{2,10},{8,16},{10,18},{16,24},{18,26},{24,28},{26,30},{28,20... | collective-permute-start | bytes 786440 | tf_op jit(solution)/shard_map/ppermute | solution.py:154
  100.6 4.2 %collective-permute-done.18 = bf16[64,2048]{1,0:T(8,128)(2,1)S(1)} collective-permute-done((bf16[64,2048]{1,0:T(8,128)(2,1)S(1)}, bf16[64,2048]{1,0:T(8,128)(2,1)S(1)}, u32[]{:S(2)}, u32[]{:S(2)}) %collective-permute-start.18) | collective-permute-done | bytes 262176 | tf_op jit(solution)/shard_map/ppermute | solution.py:154
  104.8 0.1 add_convert_fusion.6
  104.9 0.8 collective-permute-done.28
  105.8 0.1 add_convert_fusion
  105.9 0.8 pad_maximum_fusion
  (29 shorter events, 0.5 us)
Async XLA Ops:
  0.0 26.3 %copy-start = (bf16[1,2048,768]{2,1,0:T(8,128)(2,1)S(1)}, bf16[1,2048,768]{2,1,0:T(8,128)(2,1)}, u32[]{:S(2)}) copy-start(bf16[1,2048,768]{2,1,0:T(8,128)(2,1)} %refs_2_.5) | copy-start | bytes 9437188
  0.0 22.1 %collective-permute-start = (bf16[1,2048,768]{2,1,0:T(8,128)(2,1)}, bf16[1,2048,768]{2,1,0:T(8,128)(2,1)S(1)}, u32[]{:S(2)}, u32[]{:S(2)}) collective-permute-start(bf16[1,2048,768]{2,1,0:T(8,128)(2,1)} %refs_2_.5), channel_id=1, source_target_pairs={{0,2},{2,0},{4,6},{6,4},{8,10},{10,8},{12,14},{14,12},{16,18},{18,... | collective-permute-start | bytes 9437192 | tf_op jit(solution)/shard_map/ppermute | solution.py:115
  0.5 21.7 %collective-permute-start.1 = (bf16[1,2048,768]{2,1,0:T(8,128)(2,1)}, bf16[1,2048,768]{2,1,0:T(8,128)(2,1)S(1)}, u32[]{:S(2)}, u32[]{:S(2)}) collective-permute-start(bf16[1,2048,768]{2,1,0:T(8,128)(2,1)} %refs_3_.5), channel_id=1, source_target_pairs={{0,2},{2,0},{4,6},{6,4},{8,10},{10,8},{12,14},{14,12},{16,18},{18,... | collective-permute-start | bytes 9437192 | tf_op jit(solution)/shard_map/ppermute | solution.py:115
  0.5 21.6 %collective-permute-start.2 = (bf16[1,768,2048]{2,1,0:T(8,128)(2,1)}, bf16[1,768,2048]{2,1,0:T(8,128)(2,1)S(1)}, u32[]{:S(2)}, u32[]{:S(2)}) collective-permute-start(bf16[1,768,2048]{2,1,0:T(8,128)(2,1)} %refs_4_.7), channel_id=1, source_target_pairs={{0,2},{2,0},{4,6},{6,4},{8,10},{10,8},{12,14},{14,12},{16,18},{18,... | collective-permute-start | bytes 9437192 | tf_op jit(solution)/shard_map/ppermute | solution.py:115
  1.0 1.0 copy-start.3
  2.0 0.7 copy-start.4
  2.7 0.7 copy-start.5
  3.4 0.7 copy-start.6
  4.7 15.8 %collective-permute-start.3 = (bf16[128,2176]{1,0:T(8,128)(2,1)S(1)}, bf16[128,2176]{1,0:T(8,128)(2,1)S(1)}, u32[]{:S(2)}, u32[]{:S(2)}) collective-permute-start(bf16[128,2176]{1,0:T(8,128)(2,1)S(1)} %shard_map.73.refs_0_), channel_id=1, source_target_pairs={{0,8},{2,10},{8,16},{10,18},{16,24},{18,26},{24,28},{26,30},{28,20... | collective-permute-start | bytes 1671176 | tf_op jit(solution)/shard_map/ppermute | solution.py:116
  7.7 14.4 %collective-permute-start.5 = (bf16[128,2176]{1,0:T(8,128)(2,1)S(1)}, bf16[128,2176]{1,0:T(8,128)(2,1)S(1)}, u32[]{:S(2)}, u32[]{:S(2)}) collective-permute-start(bf16[128,2176]{1,0:T(8,128)(2,1)S(1)} %shard_map.73.refs_0_), channel_id=1, source_target_pairs={{0,4},{2,6},{8,0},{10,2},{16,8},{18,10},{24,16},{26,18},{28,24},{3... | collective-permute-start | bytes 1671176 | tf_op jit(solution)/shard_map/ppermute | solution.py:116
  22.2 15.8 %collective-permute-start.4 = (bf16[64,2176]{1,0:T(8,128)(2,1)S(1)}, bf16[64,2176]{1,0:T(8,128)(2,1)S(1)}, u32[]{:S(2)}, u32[]{:S(2)}) collective-permute-start(bf16[64,2176]{1,0:T(8,128)(2,1)S(1)} %get-tuple-element.46), channel_id=1, source_target_pairs={{0,8},{2,10},{8,16},{10,18},{16,24},{18,26},{24,28},{26,30},{28,20... | collective-permute-start | bytes 835592 | tf_op jit(solution)/shard_map/ppermute | solution.py:140
  23.8 14.1 %collective-permute-start.7 = (bf16[64,2176]{1,0:T(8,128)(2,1)S(1)}, bf16[64,2176]{1,0:T(8,128)(2,1)S(1)}, u32[]{:S(2)}, u32[]{:S(2)}) collective-permute-start(bf16[64,2176]{1,0:T(8,128)(2,1)S(1)} %get-tuple-element.49), channel_id=1, source_target_pairs={{0,4},{2,6},{8,0},{10,2},{16,8},{18,10},{24,16},{26,18},{28,24},{3... | collective-permute-start | bytes 835592 | tf_op jit(solution)/shard_map/ppermute | solution.py:140
  24.2 13.7 %collective-permute-start.8 = (bf16[64,2176]{1,0:T(8,128)(2,1)S(1)}, bf16[64,2176]{1,0:T(8,128)(2,1)S(1)}, u32[]{:S(2)}, u32[]{:S(2)}) collective-permute-start(bf16[64,2176]{1,0:T(8,128)(2,1)S(1)} %get-tuple-element.50), channel_id=1, source_target_pairs={{0,8},{2,10},{8,16},{10,18},{16,24},{18,26},{24,28},{26,30},{28,20... | collective-permute-start | bytes 835592 | tf_op jit(solution)/shard_map/ppermute | solution.py:140
  25.8 12.1 %collective-permute-start.9 = (bf16[64,2176]{1,0:T(8,128)(2,1)S(1)}, bf16[64,2176]{1,0:T(8,128)(2,1)S(1)}, u32[]{:S(2)}, u32[]{:S(2)}) collective-permute-start(bf16[64,2176]{1,0:T(8,128)(2,1)S(1)} %get-tuple-element.51), channel_id=1, source_target_pairs={{0,4},{2,6},{8,0},{10,2},{16,8},{18,10},{24,16},{26,18},{28,24},{3... | collective-permute-start | bytes 835592 | tf_op jit(solution)/shard_map/ppermute | solution.py:140
  26.3 1.9 %copy-start.1 = (bf16[1,2048,768]{2,1,0:T(8,128)(2,1)S(1)}, bf16[1,2048,768]{2,1,0:T(8,128)(2,1)}, u32[]{:S(2)}) copy-start(bf16[1,2048,768]{2,1,0:T(8,128)(2,1)} %refs_3_.5) | copy-start | bytes 9437188
  28.2 1.9 %copy-start.2 = (bf16[1,768,2048]{2,1,0:T(8,128)(2,1)S(1)}, bf16[1,768,2048]{2,1,0:T(8,128)(2,1)}, u32[]{:S(2)}) copy-start(bf16[1,768,2048]{2,1,0:T(8,128)(2,1)} %refs_4_.7) | copy-start | bytes 9437188
  38.0 9.5 %collective-permute-start.6 = (bf16[64,2176]{1,0:T(8,128)(2,1)S(1)}, bf16[64,2176]{1,0:T(8,128)(2,1)S(1)}, u32[]{:S(2)}, u32[]{:S(2)}) collective-permute-start(bf16[64,2176]{1,0:T(8,128)(2,1)S(1)} %collective-permute-done.4.refs_0_), channel_id=1, source_target_pairs={{0,8},{2,10},{8,16},{10,18},{16,24},{18,26},{24,28},{26,30},{28,20... | collective-permute-start | bytes 835592 | tf_op jit(solution)/shard_map/ppermute | solution.py:140
  39.6 9.2 %collective-permute-start.13 = (bf16[64,2176]{1,0:T(8,128)(2,1)S(1)}, bf16[64,2176]{1,0:T(8,128)(2,1)S(1)}, u32[]{:S(2)}, u32[]{:S(2)}) collective-permute-start(bf16[64,2176]{1,0:T(8,128)(2,1)S(1)} %collective-permute-done.7.refs_1_), channel_id=1, source_target_pairs={{0,4},{2,6},{8,0},{10,2},{16,8},{18,10},{24,16},{26,18},{28,24},{3... | collective-permute-start | bytes 835592 | tf_op jit(solution)/shard_map/ppermute | solution.py:140
  40.1 10.4 %collective-permute-start.10 = (bf16[64,2176]{1,0:T(8,128)(2,1)S(1)}, bf16[64,2176]{1,0:T(8,128)(2,1)S(1)}, u32[]{:S(2)}, u32[]{:S(2)}) collective-permute-start(bf16[64,2176]{1,0:T(8,128)(2,1)S(1)} %collective-permute-done.8.refs_2_), channel_id=1, source_target_pairs={{0,8},{2,10},{8,16},{10,18},{16,24},{18,26},{24,28},{26,30},{28,20... | collective-permute-start | bytes 835592 | tf_op jit(solution)/shard_map/ppermute | solution.py:140
  41.6 10.1 %collective-permute-start.12 = (bf16[64,2176]{1,0:T(8,128)(2,1)S(1)}, bf16[64,2176]{1,0:T(8,128)(2,1)S(1)}, u32[]{:S(2)}, u32[]{:S(2)}) collective-permute-start(bf16[64,2176]{1,0:T(8,128)(2,1)S(1)} %collective-permute-done.9.refs_3_), channel_id=1, source_target_pairs={{0,4},{2,6},{8,0},{10,2},{16,8},{18,10},{24,16},{26,18},{28,24},{3... | collective-permute-start | bytes 835592 | tf_op jit(solution)/shard_map/ppermute | solution.py:140
  51.8 7.1 %collective-permute-start.11 = (bf16[64,2176]{1,0:T(8,128)(2,1)S(1)}, bf16[64,2176]{1,0:T(8,128)(2,1)S(1)}, u32[]{:S(2)}, u32[]{:S(2)}) collective-permute-start(bf16[64,2176]{1,0:T(8,128)(2,1)S(1)} %collective-permute-done.6.refs_0_), channel_id=1, source_target_pairs={{0,8},{2,10},{8,16},{10,18},{16,24},{18,26},{24,28},{26,30},{28,20... | collective-permute-start | bytes 835592 | tf_op jit(solution)/shard_map/ppermute | solution.py:140
  53.3 6.5 %collective-permute-start.14 = (bf16[64,2176]{1,0:T(8,128)(2,1)S(1)}, bf16[64,2176]{1,0:T(8,128)(2,1)S(1)}, u32[]{:S(2)}, u32[]{:S(2)}) collective-permute-start(bf16[64,2176]{1,0:T(8,128)(2,1)S(1)} %collective-permute-done.12.refs_3_), channel_id=1, source_target_pairs={{0,4},{2,6},{8,0},{10,2},{16,8},{18,10},{24,16},{26,18},{28,24},{3... | collective-permute-start | bytes 835592 | tf_op jit(solution)/shard_map/ppermute | solution.py:140
  62.7 9.3 %collective-permute-start.25 = (bf16[64,2048]{1,0:T(8,128)(2,1)S(1)}, bf16[64,2048]{1,0:T(8,128)(2,1)S(1)}, u32[]{:S(2)}, u32[]{:S(2)}) collective-permute-start(bf16[64,2048]{1,0:T(8,128)(2,1)S(1)} %get-tuple-element.80), channel_id=1, source_target_pairs={{0,8},{2,10},{8,16},{10,18},{16,24},{18,26},{24,28},{26,30},{28,20... | collective-permute-start | bytes 786440 | tf_op jit(solution)/shard_map/ppermute | solution.py:154
  64.2 9.3 %collective-permute-start.22 = (bf16[64,2048]{1,0:T(8,128)(2,1)S(1)}, bf16[64,2048]{1,0:T(8,128)(2,1)S(1)}, u32[]{:S(2)}, u32[]{:S(2)}) collective-permute-start(bf16[64,2048]{1,0:T(8,128)(2,1)S(1)} %get-tuple-element.77), channel_id=1, source_target_pairs={{0,4},{2,6},{8,0},{10,2},{16,8},{18,10},{24,16},{26,18},{28,24},{3... | collective-permute-start | bytes 786440 | tf_op jit(solution)/shard_map/ppermute | solution.py:154
  64.8 12.8 %collective-permute-start.19 = (bf16[64,2048]{1,0:T(8,128)(2,1)S(1)}, bf16[64,2048]{1,0:T(8,128)(2,1)S(1)}, u32[]{:S(2)}, u32[]{:S(2)}) collective-permute-start(bf16[64,2048]{1,0:T(8,128)(2,1)S(1)} %get-tuple-element.72), channel_id=1, source_target_pairs={{0,8},{2,10},{8,16},{10,18},{16,24},{18,26},{24,28},{26,30},{28,20... | collective-permute-start | bytes 786440 | tf_op jit(solution)/shard_map/ppermute | solution.py:154
  66.3 12.9 %collective-permute-start.15 = (bf16[64,2048]{1,0:T(8,128)(2,1)S(1)}, bf16[64,2048]{1,0:T(8,128)(2,1)S(1)}, u32[]{:S(2)}, u32[]{:S(2)}) collective-permute-start(bf16[64,2048]{1,0:T(8,128)(2,1)S(1)} %get-tuple-element.69), channel_id=1, source_target_pairs={{0,4},{2,6},{8,0},{10,2},{16,8},{18,10},{24,16},{26,18},{28,24},{3... | collective-permute-start | bytes 786440 | tf_op jit(solution)/shard_map/ppermute | solution.py:154
  72.0 11.2 %collective-permute-start.26 = (bf16[64,2048]{1,0:T(8,128)(2,1)S(1)}, bf16[64,2048]{1,0:T(8,128)(2,1)S(1)}, u32[]{:S(2)}, u32[]{:S(2)}) collective-permute-start(bf16[64,2048]{1,0:T(8,128)(2,1)S(1)} %add_convert_fusion.3), channel_id=1, source_target_pairs={{0,8},{2,10},{8,16},{10,18},{16,24},{18,26},{24,28},{26,30},{28,20... | collective-permute-start | bytes 786440 | tf_op jit(solution)/shard_map/ppermute | solution.py:154
  73.6 11.2 %collective-permute-start.23 = (bf16[64,2048]{1,0:T(8,128)(2,1)S(1)}, bf16[64,2048]{1,0:T(8,128)(2,1)S(1)}, u32[]{:S(2)}, u32[]{:S(2)}) collective-permute-start(bf16[64,2048]{1,0:T(8,128)(2,1)S(1)} %add_convert_fusion.5), channel_id=1, source_target_pairs={{0,4},{2,6},{8,0},{10,2},{16,8},{18,10},{24,16},{26,18},{28,24},{3... | collective-permute-start | bytes 786440 | tf_op jit(solution)/shard_map/ppermute | solution.py:154
  77.6 13.2 %collective-permute-start.20 = (bf16[64,2048]{1,0:T(8,128)(2,1)S(1)}, bf16[64,2048]{1,0:T(8,128)(2,1)S(1)}, u32[]{:S(2)}, u32[]{:S(2)}) collective-permute-start(bf16[64,2048]{1,0:T(8,128)(2,1)S(1)} %add_convert_fusion.8), channel_id=1, source_target_pairs={{0,8},{2,10},{8,16},{10,18},{16,24},{18,26},{24,28},{26,30},{28,20... | collective-permute-start | bytes 786440 | tf_op jit(solution)/shard_map/ppermute | solution.py:154
  79.3 10.6 %collective-permute-start.16 = (bf16[64,2048]{1,0:T(8,128)(2,1)S(1)}, bf16[64,2048]{1,0:T(8,128)(2,1)S(1)}, u32[]{:S(2)}, u32[]{:S(2)}) collective-permute-start(bf16[64,2048]{1,0:T(8,128)(2,1)S(1)} %add_convert_fusion.11), channel_id=1, source_target_pairs={{0,4},{2,6},{8,0},{10,2},{16,8},{18,10},{24,16},{26,18},{28,24},{3... | collective-permute-start | bytes 786440 | tf_op jit(solution)/shard_map/ppermute | solution.py:154
  83.3 16.0 %collective-permute-start.27 = (bf16[64,2048]{1,0:T(8,128)(2,1)S(1)}, bf16[64,2048]{1,0:T(8,128)(2,1)S(1)}, u32[]{:S(2)}, u32[]{:S(2)}) collective-permute-start(bf16[64,2048]{1,0:T(8,128)(2,1)S(1)} %add_convert_fusion.2), channel_id=1, source_target_pairs={{0,8},{2,10},{8,16},{10,18},{16,24},{18,26},{24,28},{26,30},{28,20... | collective-permute-start | bytes 786440 | tf_op jit(solution)/shard_map/ppermute | solution.py:154
  84.9 20.0 %collective-permute-start.24 = (bf16[64,2048]{1,0:T(8,128)(2,1)S(1)}, bf16[64,2048]{1,0:T(8,128)(2,1)S(1)}, u32[]{:S(2)}, u32[]{:S(2)}) collective-permute-start(bf16[64,2048]{1,0:T(8,128)(2,1)S(1)} %add_convert_fusion.4), channel_id=1, source_target_pairs={{0,4},{2,6},{8,0},{10,2},{16,8},{18,10},{24,16},{26,18},{28,24},{3... | collective-permute-start | bytes 786440 | tf_op jit(solution)/shard_map/ppermute | solution.py:154
  89.9 8.4 %collective-permute-start.17 = (bf16[64,2048]{1,0:T(8,128)(2,1)S(1)}, bf16[64,2048]{1,0:T(8,128)(2,1)S(1)}, u32[]{:S(2)}, u32[]{:S(2)}) collective-permute-start(bf16[64,2048]{1,0:T(8,128)(2,1)S(1)} %add_convert_fusion.10), channel_id=1, source_target_pairs={{0,4},{2,6},{8,0},{10,2},{16,8},{18,10},{24,16},{26,18},{28,24},{3... | collective-permute-start | bytes 786440 | tf_op jit(solution)/shard_map/ppermute | solution.py:154
  90.9 9.7 %collective-permute-start.21 = (bf16[64,2048]{1,0:T(8,128)(2,1)S(1)}, bf16[64,2048]{1,0:T(8,128)(2,1)S(1)}, u32[]{:S(2)}, u32[]{:S(2)}) collective-permute-start(bf16[64,2048]{1,0:T(8,128)(2,1)S(1)} %add_convert_fusion.7), channel_id=1, source_target_pairs={{0,8},{2,10},{8,16},{10,18},{16,24},{18,26},{24,28},{26,30},{28,20... | collective-permute-start | bytes 786440 | tf_op jit(solution)/shard_map/ppermute | solution.py:154
  98.4 6.4 %collective-permute-start.18 = (bf16[64,2048]{1,0:T(8,128)(2,1)S(1)}, bf16[64,2048]{1,0:T(8,128)(2,1)S(1)}, u32[]{:S(2)}, u32[]{:S(2)}) collective-permute-start(bf16[64,2048]{1,0:T(8,128)(2,1)S(1)} %add_convert_fusion.9), channel_id=1, source_target_pairs={{0,4},{2,6},{8,0},{10,2},{16,8},{18,10},{24,16},{26,18},{28,24},{3... | collective-permute-start | bytes 786440 | tf_op jit(solution)/shard_map/ppermute | solution.py:154
  99.3 6.4 %collective-permute-start.28 = (bf16[64,2048]{1,0:T(8,128)(2,1)S(1)}, bf16[64,2048]{1,0:T(8,128)(2,1)S(1)}, u32[]{:S(2)}, u32[]{:S(2)}) collective-permute-start(bf16[64,2048]{1,0:T(8,128)(2,1)S(1)} %add_convert_fusion.1), channel_id=1, source_target_pairs={{0,8},{2,10},{8,16},{10,18},{16,24},{18,26},{24,28},{26,30},{28,20... | collective-permute-start | bytes 786440 | tf_op jit(solution)/shard_map/ppermute | solution.py:154

commit v3 on v2

--- a/solution.py
+++ b/solution.py
@@ -10,34 +10,53 @@
 LANES = 128
 
 
-def pack_kernel(n_dev, tokens_ref, ids_ref, scores_ref, partner_ref, out_ref):
+def pack_kernel(tokens_ref, scores_ref, out_ref):
     rows, width = tokens_ref.shape
-    extra = out_ref.shape[1] - width
-    lane = lax.broadcasted_iota(jnp.int32, (extra, 1), 0)
-    served = jnp.full((extra, 1), -1, jnp.int32)
-    for slot in range(n_dev):
-        hit = (lane == slot) | (lane == slot + n_dev)
-        served = jnp.where(hit, partner_ref[slot], served)
-    total = jnp.zeros((extra, rows), jnp.float32)
-    for k in range(ids_ref.shape[0]):
-        total += jnp.where(ids_ref[k : k + 1, :] == served, scores_ref[k : k + 1, :], 0.0)
-    high = total.astype(jnp.bfloat16).astype(jnp.float32)
-    tail = jnp.where(lane < n_dev, high, total - high).T.astype(jnp.bfloat16)
+    n_dev = scores_ref.shape[0]
+    scores = scores_ref[...]
+    high = scores.astype(jnp.bfloat16).astype(jnp.float32)
+    blank = jnp.zeros((out_ref.shape[1] - width - 2 * n_dev, rows), jnp.float32)
+    parts = [high, scores - high] + ([blank] if blank.shape[0] else [])
     out_ref[:, :width] = tokens_ref[...]
-    out_ref[:, width:] = tail
+    out_ref[:, width:] = jnp.concatenate(parts, axis=0).T.astype(jnp.bfloat16)
 
 
 def pack(tokens, expert_ids, gate_scores, partner, n_dev):
+    scores = jnp.sum(jnp.where(expert_ids.T[None] == partner[:, None, None], gate_scores.T[None], 0.0), axis=1)
     rows, width = tokens.shape
     extra = -(-2 * n_dev // LANES) * LANES
     near = pl.BlockSpec(memory_space=pltpu.VMEM)
     return pl.pallas_call(
-        functools.partial(pack_kernel, n_dev),
-        in_specs=[near, near, near, pl.BlockSpec(memory_space=pltpu.SMEM)],
+        pack_kernel,
+        in_specs=[near, near],
         out_specs=near,
         out_shape=jax.ShapeDtypeStruct((rows, width + extra), jnp.bfloat16),
-        compiler_params=pltpu.CompilerParams(vmem_limit_bytes=6 * 2**20),
-    )(tokens, expert_ids.T, gate_scores.T, partner)
+        compiler_params=pltpu.CompilerParams(vmem_limit_bytes=4 * 2**20),
+    )(tokens, scores)
+
+
+def load_kernel(*refs):
+    n = len(refs) // 2
+    sources, targets, sems = refs[:n], refs[n : 2 * n], refs[-1]
+    copies = [pltpu.make_async_copy(a, b, sems.at[i]) for i, (a, b) in enumerate(zip(sources, targets))]
+    for copy in copies:
+        copy.start()
+    for copy in copies:
+        copy.wait()
+
+
+def load(arrays):
+    return pl.pallas_call(
+        load_kernel,
+        in_specs=[pl.BlockSpec(memory_space=pltpu.HBM)] * len(arrays),
+        out_specs=[pl.BlockSpec(memory_space=pltpu.VMEM)] * len(arrays),
+        out_shape=[jax.ShapeDtypeStruct(a.shape, a.dtype) for a in arrays],
+        scratch_shapes=[pltpu.SemaphoreType.DMA((len(arrays),))],
+        compiler_params=pltpu.CompilerParams(vmem_limit_bytes=16 * 2**20),
+        cost_estimate=pl.CostEstimate(
+            flops=0, bytes_accessed=sum(a.size * a.dtype.itemsize for a in arrays), transcendentals=0
+        ),
+    )(*arrays)
 
 
 def ffn_kernel(n_in, n_out, n_dev, *refs):
@@ -110,48 +129,58 @@
     def tie(value, *deps):
         return lax.optimization_barrier((value, deps))[0]
 
-    packed = pack(tokens, expert_ids, gate_scores, partner, n_dev)
     half = tokens.shape[0] // 2
     other = [lax.ppermute(w, "ep", swap) for w in own]
+    packed = pack(tokens, expert_ids, gate_scores, partner, n_dev)
     first = [lax.ppermute(packed, "ep", perm[d]) for d in range(2)]
+    own = load(own)
     held = {(d, h, 1): block[h * half : (h + 1) * half] for d, block in enumerate(first) for h in range(2)}
     last = {(d, h): far if d == h else far - 1 for d in range(2) for h in range(2)}
-
-    def keys(s):
-        if s == 0:
-            return [(0, 0, 0), (0, 1, 0)]
-        return [(d, h, s) for h in range(2) for d in range(2) if s <= last[d, h]]
-
     done = {}
 
-    def compute(s, blocks):
-        names = [(d, h, 1) for d in range(2) for h in range(2)] if s == 1 else keys(s)
+    def compute(names, blocks, *deps):
         kinds = [jnp.bfloat16 if n[2] and n[2] == last[n[:2]] else jnp.float32 for n in names]
+        blocks = tie(blocks, *deps) if deps else blocks
         done.update(zip(names, ffn(blocks, half, kinds, own, other, n_dev)))
-
-    for s in range(1, far + 1):
-        if s > 1:
-            for d, h, _ in keys(s):
-                deps = other if s == 2 else [done[keys(s - 2)[0]]]
-                if s == 3:
-                    deps = deps + [done[keys(0)[0]]]
-                if s == far:
-                    deps = deps + [held[d, 1 - h, s - 1]]
-                held[d, h, s] = lax.ppermute(tie(held[d, h, s - 1], *deps), "ep", perm[d])
-        blocks = first if s == 1 else [held[k] for k in keys(s)]
-        compute(s, blocks if s == 1 else tie(blocks, done[keys(s - 1)[0]]))
-        if s == 1:
-            compute(0, [packed])
-    for k in keys(far - 1):
-        done[k] = tie(done[k], *[held[k] for k in keys(far)])
+        return done[names[0]]
+
+    def send(names, *deps):
+        for d, h, s in names:
+            held[d, h, s] = lax.ppermute(tie(held[d, h, s - 1], *deps), "ep", perm[d])
+
+    groups = ([(0, 0), (1, 1)], [(1, 0), (0, 1)])
+
+    def flows(g, s):
+        return [(d, h, s) for d, h in groups[g] if s <= last[d, h]]
+
+    for g in range(2):
+        send(flows(g, 2), *other, *own)
+    worked = []
+    for s in range(1, far):
+        for g in range(2):
+            names = flows(g, s)
+            worked.append(compute(names, [held[n] for n in names], *worked[-1:]))
+            if s + 2 <= far:
+                send(flows(g, s + 2), worked[-1])
+    names = flows(0, far)
+    worked.append(compute(names, [held[n] for n in names], worked[-1]))
 
     back = {}
-    for s in range(far, 0, -1):
-        for d, h, _ in keys(s):
+
+    def give(names, *deps):
+        for d, h, s in names:
             part = done[d, h, s]
             if (d, h) in back:
-                part = (back[d, h].astype(jnp.float32) + part).astype(jnp.bfloat16)
+                part = (tie(back[d, h], *deps).astype(jnp.float32) + part).astype(jnp.bfloat16)
             back[d, h] = lax.ppermute(part, "ep", perm[1 - d])
+
+    give(flows(1, far - 1))
+    give(flows(0, far))
+    for s in range(far - 1, 0, -1):
+        if s > 1:
+            give(flows(1, s - 1), worked[-1])
+        give(flows(0, s))
+    compute([(0, 0, 0), (0, 1, 0)], [packed], worked[-1])
     out = [
         (done[0, h, 0] + back[0, h].astype(jnp.float32) + back[1, h].astype(jnp.float32)).astype(jnp.bfloat16)
         for h in range(2)

time: 107 us -> 97.7 us (0.913)
  waiting for transfers between devices: 47.6 us -> 36.2 us
  Pallas kernels: 21.5 us -> 23.1 us
    ppermute x2, waiting for transfers between devices: 14.4 us -> 8.37 us  [on_device(): first = [lax.ppermute(packed, 'ep', perm[d]) for d in range(2)]]
    ppermute x24, waiting for transfers between devices: 33.3 us -> 27.8 us  [the longest x14 21.8 us: give(): back[d, h] = lax.ppermute(part, 'ep', perm[1 - d])]
    pallas_call x5 -> x8, Pallas kernels: 20.8 us -> 22.3 us  [ffn(): pl.pallas_call(functools.partial(ffn_kernel, n_in, n_out, n_dev), in_spec...]
    unnamed x14 -> x8, local copies, waits for them, and re-layouts: 6.85 us -> 6.7 us
  transfers between devices with their start and end apart: 29 -> 29, of which waited for: 14 -> 17; matrix products, arithmetic and copies ran while one was open for 1% -> 1% of each run, Pallas kernels for 17% -> 24%
where the time goes in v3:
time: 97.7 us; the launch traced here: 97.4 us
  waiting for transfers between devices  36.2 us (37%)
  starting transfers between devices  28.9 us (30%)
  Pallas kernels  23.1 us (24%)
  local copies, waits for them, and re-layouts  6.78 us (7%)
  other arithmetic  2.28 us (2%)
    pallas_call x8, Pallas kernels, ffn(): pl.pallas_call(functools.partial(ffn_kernel, n_in, n_out, n_dev), in_spec...  22.3 us
    ppermute x14, waiting for transfers between devices, give(): back[d, h] = lax.ppermute(part, 'ep', perm[1 - d])  21.8 us
    ppermute x14, starting transfers between devices, give(): back[d, h] = lax.ppermute(part, 'ep', perm[1 - d])  15.1 us
    ppermute x10, starting transfers between devices, send(): held[d, h, s] = lax.ppermute(tie(held[d, h, s - 1], *deps), 'ep', perm[d])  10.2 us
    ppermute x2, waiting for transfers between devices, on_device(): first = [lax.ppermute(packed, 'ep', perm[d]) for d in range(2)]  8.37 us
    unnamed x8, local copies, waits for them, and re-layouts  6.7 us
    ppermute x10, waiting for transfers between devices, send(): held[d, h, s] = lax.ppermute(tie(held[d, h, s - 1], *deps), 'ep', perm[d])  5.99 us
    ppermute x2, starting transfers between devices, on_device(): first = [lax.ppermute(packed, 'ep', perm[d]) for d in range(2)]  2.63 us
  transfers between devices with their start and end apart: 29, of which 17 were waited for; matrix products, arithmetic and copies ran while one was open for 1% of the time, Pallas kernels for 24%

profile of v3, /device:TPU:0, one launch (start us, length us, event | category | flops | bytes accessed | tf_op | source)
XLA Modules:
  0.0 97.4 jit_solution(2088075914133177836)
XLA Ops:
  0.0 0.5 collective-permute-start.1
  0.5 0.1 collective-permute-start.2
  0.5 0.5 collective-permute-start.3
  1.0 0.8 select_reduce_fusion.scores_ref
  1.8 0.0 copy-start.3
  1.8 1.0 %copy-done.3 = bf16[128,2048]{1,0:T(8,128)(2,1)S(1)} copy-done((bf16[128,2048]{1,0:T(8,128)(2,1)S(1)}, bf16[128,2048]{1,0:T(8,128)(2,1)}, u32[]{:S(2)}) %copy-start.3) | copy-done | bytes 524312
  2.8 0.1 shard_map.73.refs_0_
  2.9 2.6 %collective-permute-start = (bf16[128,2176]{1,0:T(8,128)(2,1)S(1)}, bf16[128,2176]{1,0:T(8,128)(2,1)S(1)}, u32[]{:S(2)}, u32[]{:S(2)}) collective-permute-start(bf16[128,2176]{1,0:T(8,128)(2,1)S(1)} %shard_map.73.refs_0_), channel_id=1, source_target_pairs={{0,8},{2,10},{8,16},{10,18},{16,24},{18,26},{24,28},{26,30},{28,20... | collective-permute-start | bytes 1671176 | tf_op jit(solution)/shard_map/ppermute | solution.py:135
  5.5 1.9 %copy-done = bf16[1,2048,768]{2,1,0:T(8,128)(2,1)S(1)} copy-done((bf16[1,2048,768]{2,1,0:T(8,128)(2,1)S(1)}, bf16[1,2048,768]{2,1,0:T(8,128)(2,1)}, u32[]{:S(2)}) %copy-start) | copy-done | bytes 3145752
  7.4 1.9 %copy-done.1 = bf16[1,2048,768]{2,1,0:T(8,128)(2,1)S(1)} copy-done((bf16[1,2048,768]{2,1,0:T(8,128)(2,1)S(1)}, bf16[1,2048,768]{2,1,0:T(8,128)(2,1)}, u32[]{:S(2)}) %copy-start.1) | copy-done | bytes 3145752
  9.3 1.9 %copy-done.2 = bf16[1,768,2048]{2,1,0:T(8,128)(2,1)S(1)} copy-done((bf16[1,768,2048]{2,1,0:T(8,128)(2,1)S(1)}, bf16[1,768,2048]{2,1,0:T(8,128)(2,1)}, u32[]{:S(2)}) %copy-start.2) | copy-done | bytes 3145752
  11.2 0.7 shard_map.74
  11.9 6.9 %collective-permute-done = bf16[128,2176]{1,0:T(8,128)(2,1)S(1)} collective-permute-done((bf16[128,2176]{1,0:T(8,128)(2,1)S(1)}, bf16[128,2176]{1,0:T(8,128)(2,1)S(1)}, u32[]{:S(2)}, u32[]{:S(2)}) %collective-permute-start) | collective-permute-done | bytes 557088 | tf_op jit(solution)/shard_map/ppermute | solution.py:135
  18.8 1.5 %collective-permute-done.5 = bf16[128,2176]{1,0:T(8,128)(2,1)S(1)} collective-permute-done((bf16[128,2176]{1,0:T(8,128)(2,1)S(1)}, bf16[128,2176]{1,0:T(8,128)(2,1)S(1)}, u32[]{:S(2)}, u32[]{:S(2)}) %collective-permute-start.5) | collective-permute-done | bytes 557088 | tf_op jit(solution)/shard_map/ppermute | solution.py:135
  20.4 1.6 %collective-permute-start.4 = (bf16[64,2176]{1,0:T(8,128)(2,1)S(1)}, bf16[64,2176]{1,0:T(8,128)(2,1)S(1)}, u32[]{:S(2)}, u32[]{:S(2)}) collective-permute-start(bf16[64,2176]{1,0:T(8,128)(2,1)S(1)} %get-tuple-element.54.refs_0_), channel_id=1, source_target_pairs={{0,8},{2,10},{8,16},{10,18},{16,24},{18,26},{24,28},{26,30},{28,20... | collective-permute-start | bytes 835592 | tf_op jit(solution)/shard_map/ppermute | solution.py:149
  22.0 0.4 collective-permute-start.7
  22.5 2.8 %shard_map.75 = (f32[64,2048]{1,0:T(8,128)S(1)}, f32[64,2048]{1,0:T(8,128)S(1)}) custom-call(bf16[64,2176]{1,0:T(8,128)(2,1)S(1)} %get-tuple-element.54.refs_0_, bf16[64,2176]{1,0:T(8,128)(2,1)S(1)} %get-tuple-element.57.refs_1_, bf16[1,2048,768]{2,1,0:T(8,128)(2,1)S(1)} %get-tuple-element.51.refs_2_.refs_1_, ...), custom_call_target="tpu_custom_call" | custom-call | flops 2415919104 | bytes 20447232 | tf_op jit(solution)/shard_map/pallas_call | solution.py:99
  25.2 0.3 collective-permute-start.11
  25.6 1.7 %collective-permute-start.13 = (bf16[64,2176]{1,0:T(8,128)(2,1)S(1)}, bf16[64,2176]{1,0:T(8,128)(2,1)S(1)}, u32[]{:S(2)}, u32[]{:S(2)}) collective-permute-start(bf16[64,2176]{1,0:T(8,128)(2,1)S(1)} %get-tuple-element.69.refs_1_), channel_id=1, source_target_pairs={{0,8},{2,10},{8,16},{10,18},{16,24},{18,26},{24,28},{26,30},{28,20... | collective-permute-start | bytes 835592 | tf_op jit(solution)/shard_map/ppermute | solution.py:149
  27.3 2.8 %shard_map.76 = (f32[64,2048]{1,0:T(8,128)S(1)}, f32[64,2048]{1,0:T(8,128)S(1)}) custom-call(bf16[64,2176]{1,0:T(8,128)(2,1)S(1)} %get-tuple-element.67.refs_0_, bf16[64,2176]{1,0:T(8,128)(2,1)S(1)} %get-tuple-element.69.refs_1_, bf16[1,2048,768]{2,1,0:T(8,128)(2,1)S(1)} %get-tuple-element.51.refs_2_.refs_1_, ...), custom_call_target="tpu_custom_call" | custom-call | flops 2415919104 | bytes 20447232 | tf_op jit(solution)/shard_map/pallas_call | solution.py:99
  30.1 1.5 %collective-permute-done.7.refs_1_ = bf16[64,2176]{1,0:T(8,128)(2,1)S(1)} collective-permute-done((bf16[64,2176]{1,0:T(8,128)(2,1)S(1)}, bf16[64,2176]{1,0:T(8,128)(2,1)S(1)}, u32[]{:S(2)}, u32[]{:S(2)}) %collective-permute-start.7) | collective-permute-done | bytes 278560 | tf_op jit(solution)/shard_map/ppermute | solution.py:149
  31.6 1.6 %collective-permute-start.6 = (bf16[64,2176]{1,0:T(8,128)(2,1)S(1)}, bf16[64,2176]{1,0:T(8,128)(2,1)S(1)}, u32[]{:S(2)}, u32[]{:S(2)}) collective-permute-start(bf16[64,2176]{1,0:T(8,128)(2,1)S(1)} %collective-permute-done.4.refs_0_), channel_id=1, source_target_pairs={{0,8},{2,10},{8,16},{10,18},{16,24},{18,26},{24,28},{26,30},{28,20... | collective-permute-start | bytes 835592 | tf_op jit(solution)/shard_map/ppermute | solution.py:149
  33.2 0.4 collective-permute-start.9
  33.6 2.8 %shard_map.77 = (f32[64,2048]{1,0:T(8,128)S(1)}, f32[64,2048]{1,0:T(8,128)S(1)}) custom-call(bf16[64,2176]{1,0:T(8,128)(2,1)S(1)} %collective-permute-done.4.refs_0_, bf16[64,2176]{1,0:T(8,128)(2,1)S(1)} %collective-permute-done.7.refs_1_, bf16[1,2048,768]{2,1,0:T(8,128)(2,1)S(1)} %get-tuple-element.51.refs_2_.refs_1_, ...), custom_call_target="tpu_custom_call" | custom-call | flops 2415919104 | bytes 20447232 | tf_op jit(solution)/shard_map/pallas_call | solution.py:99
  36.4 1.1 %collective-permute-done.11.refs_0_ = bf16[64,2176]{1,0:T(8,128)(2,1)S(1)} collective-permute-done((bf16[64,2176]{1,0:T(8,128)(2,1)S(1)}, bf16[64,2176]{1,0:T(8,128)(2,1)S(1)}, u32[]{:S(2)}, u32[]{:S(2)}) %collective-permute-start.11) | collective-permute-done | bytes 278560 | tf_op jit(solution)/shard_map/ppermute | solution.py:149
  37.6 0.5 collective-permute-start.12
  38.0 1.6 %collective-permute-start.14 = (bf16[64,2176]{1,0:T(8,128)(2,1)S(1)}, bf16[64,2176]{1,0:T(8,128)(2,1)S(1)}, u32[]{:S(2)}, u32[]{:S(2)}) collective-permute-start(bf16[64,2176]{1,0:T(8,128)(2,1)S(1)} %collective-permute-done.13.refs_1_), channel_id=1, source_target_pairs={{0,8},{2,10},{8,16},{10,18},{16,24},{18,26},{24,28},{26,30},{28,20... | collective-permute-start | bytes 835592 | tf_op jit(solution)/shard_map/ppermute | solution.py:149
  39.6 2.8 %shard_map.78 = (f32[64,2048]{1,0:T(8,128)S(1)}, f32[64,2048]{1,0:T(8,128)S(1)}) custom-call(bf16[64,2176]{1,0:T(8,128)(2,1)S(1)} %collective-permute-done.11.refs_0_, bf16[64,2176]{1,0:T(8,128)(2,1)S(1)} %collective-permute-done.13.refs_1_, bf16[1,2048,768]{2,1,0:T(8,128)(2,1)S(1)} %get-tuple-element.51.refs_2_.refs_1_, ...), custom_call_target="tpu_custom_call" | custom-call | flops 2415919104 | bytes 20447232 | tf_op jit(solution)/shard_map/pallas_call | solution.py:99
  42.4 1.1 %collective-permute-done.9.refs_1_ = bf16[64,2176]{1,0:T(8,128)(2,1)S(1)} collective-permute-done((bf16[64,2176]{1,0:T(8,128)(2,1)S(1)}, bf16[64,2176]{1,0:T(8,128)(2,1)S(1)}, u32[]{:S(2)}, u32[]{:S(2)}) %collective-permute-start.9) | collective-permute-done | bytes 278560 | tf_op jit(solution)/shard_map/ppermute | solution.py:149
  43.5 1.6 %collective-permute-start.8 = (bf16[64,2176]{1,0:T(8,128)(2,1)S(1)}, bf16[64,2176]{1,0:T(8,128)(2,1)S(1)}, u32[]{:S(2)}, u32[]{:S(2)}) collective-permute-start(bf16[64,2176]{1,0:T(8,128)(2,1)S(1)} %collective-permute-done.6.refs_0_), channel_id=1, source_target_pairs={{0,8},{2,10},{8,16},{10,18},{16,24},{18,26},{24,28},{26,30},{28,20... | collective-permute-start | bytes 835592 | tf_op jit(solution)/shard_map/ppermute | solution.py:149
  45.1 0.4 collective-permute-start.10
  45.6 2.8 %shard_map.79 = (f32[64,2048]{1,0:T(8,128)S(1)}, f32[64,2048]{1,0:T(8,128)S(1)}) custom-call(bf16[64,2176]{1,0:T(8,128)(2,1)S(1)} %collective-permute-done.6.refs_0_, bf16[64,2176]{1,0:T(8,128)(2,1)S(1)} %collective-permute-done.9.refs_1_, bf16[1,2048,768]{2,1,0:T(8,128)(2,1)S(1)} %get-tuple-element.51.refs_2_.refs_1_, ...), custom_call_target="tpu_custom_call" | custom-call | flops 2415919104 | bytes 20447232 | tf_op jit(solution)/shard_map/pallas_call | solution.py:99
  48.4 1.1 %collective-permute-done.12.refs_0_ = bf16[64,2176]{1,0:T(8,128)(2,1)S(1)} collective-permute-done((bf16[64,2176]{1,0:T(8,128)(2,1)S(1)}, bf16[64,2176]{1,0:T(8,128)(2,1)S(1)}, u32[]{:S(2)}, u32[]{:S(2)}) %collective-permute-start.12) | collective-permute-done | bytes 278560 | tf_op jit(solution)/shard_map/ppermute | solution.py:149
  49.5 2.8 %shard_map.80 = (bf16[64,2048]{1,0:T(8,128)(2,1)S(1)}, bf16[64,2048]{1,0:T(8,128)(2,1)S(1)}) custom-call(bf16[64,2176]{1,0:T(8,128)(2,1)S(1)} %collective-permute-done.12.refs_0_, bf16[64,2176]{1,0:T(8,128)(2,1)S(1)} %collective-permute-done.14.refs_1_, bf16[1,2048,768]{2,1,0:T(8,128)(2,1)S(1)} %get-tuple-element.51.refs_2_.refs_1_, ...), custom_call_target="tpu_custom_call" | custom-call | flops 2415919104 | bytes 20447232 | tf_op jit(solution)/shard_map/pallas_call | solution.py:99
  52.3 0.5 collective-permute-start.22
  52.8 1.6 %collective-permute-start.19 = (bf16[64,2048]{1,0:T(8,128)(2,1)S(1)}, bf16[64,2048]{1,0:T(8,128)(2,1)S(1)}, u32[]{:S(2)}, u32[]{:S(2)}) collective-permute-start(bf16[64,2048]{1,0:T(8,128)(2,1)S(1)} %get-tuple-element.79), channel_id=1, source_target_pairs={{0,8},{2,10},{8,16},{10,18},{16,24},{18,26},{24,28},{26,30},{28,20... | collective-permute-start | bytes 786440 | tf_op jit(solution)/shard_map/ppermute | solution.py:175
  54.4 1.1 %collective-permute-done.10.refs_1_ = bf16[64,2176]{1,0:T(8,128)(2,1)S(1)} collective-permute-done((bf16[64,2176]{1,0:T(8,128)(2,1)S(1)}, bf16[64,2176]{1,0:T(8,128)(2,1)S(1)}, u32[]{:S(2)}, u32[]{:S(2)}) %collective-permute-start.10) | collective-permute-done | bytes 278560 | tf_op jit(solution)/shard_map/ppermute | solution.py:149
  55.5 2.8 %shard_map.81 = (bf16[64,2048]{1,0:T(8,128)(2,1)S(1)}, bf16[64,2048]{1,0:T(8,128)(2,1)S(1)}) custom-call(bf16[64,2176]{1,0:T(8,128)(2,1)S(1)} %collective-permute-done.8.refs_0_, bf16[64,2176]{1,0:T(8,128)(2,1)S(1)} %collective-permute-done.10.refs_1_, bf16[1,2048,768]{2,1,0:T(8,128)(2,1)S(1)} %get-tuple-element.51.refs_2_.refs_1_, ...), custom_call_target="tpu_custom_call" | custom-call | flops 2415919104 | bytes 20447232 | tf_op jit(solution)/shard_map/pallas_call | solution.py:99
  58.3 0.5 collective-permute-start.15
  58.8 1.6 %collective-permute-start.25 = (bf16[64,2048]{1,0:T(8,128)(2,1)S(1)}, bf16[64,2048]{1,0:T(8,128)(2,1)S(1)}, u32[]{:S(2)}, u32[]{:S(2)}) collective-permute-start(bf16[64,2048]{1,0:T(8,128)(2,1)S(1)} %get-tuple-element.93), channel_id=1, source_target_pairs={{0,8},{2,10},{8,16},{10,18},{16,24},{18,26},{24,28},{26,30},{28,20... | collective-permute-start | bytes 786440 | tf_op jit(solution)/shard_map/ppermute | solution.py:175
  60.4 0.8 collective-permute-done.22
  61.2 0.5 collective-permute-start.23
  61.7 1.8 %collective-permute-start.20 = (bf16[64,2048]{1,0:T(8,128)(2,1)S(1)}, bf16[64,2048]{1,0:T(8,128)(2,1)S(1)}, u32[]{:S(2)}, u32[]{:S(2)}) collective-permute-start(bf16[64,2048]{1,0:T(8,128)(2,1)S(1)} %add_convert_fusion.8), channel_id=1, source_target_pairs={{0,8},{2,10},{8,16},{10,18},{16,24},{18,26},{24,28},{26,30},{28,20... | collective-permute-start | bytes 786440 | tf_op jit(solution)/shard_map/ppermute | solution.py:175
  63.6 2.8 %shard_map.82 = (f32[64,2048]{1,0:T(8,128)S(1)}, f32[64,2048]{1,0:T(8,128)S(1)}) custom-call(bf16[128,2176]{1,0:T(8,128)(2,1)S(1)} %shard_map.73.refs_0_, bf16[1,2048,768]{2,1,0:T(8,128)(2,1)S(1)} %get-tuple-element.51.refs_2_.refs_1_, bf16[1,2048,768]{2,1,0:T(8,128)(2,1)S(1)} %get-tuple-element.52.refs_3_.refs_2_, ...), custom_call_target="tpu_custom_call" | custom-call | flops 2415919104 | bytes 20447232 | tf_op jit(solution)/shard_map/pallas_call | solution.py:99
  66.4 1.7 %collective-permute-done.25 = bf16[64,2048]{1,0:T(8,128)(2,1)S(1)} collective-permute-done((bf16[64,2048]{1,0:T(8,128)(2,1)S(1)}, bf16[64,2048]{1,0:T(8,128)(2,1)S(1)}, u32[]{:S(2)}, u32[]{:S(2)}) %collective-permute-start.25) | collective-permute-done | bytes 262176 | tf_op jit(solution)/shard_map/ppermute | solution.py:175
  68.1 1.6 %collective-permute-start.26 = (bf16[64,2048]{1,0:T(8,128)(2,1)S(1)}, bf16[64,2048]{1,0:T(8,128)(2,1)S(1)}, u32[]{:S(2)}, u32[]{:S(2)}) collective-permute-start(bf16[64,2048]{1,0:T(8,128)(2,1)S(1)} %add_convert_fusion.3), channel_id=1, source_target_pairs={{0,8},{2,10},{8,16},{10,18},{16,24},{18,26},{24,28},{26,30},{28,20... | collective-permute-start | bytes 786440 | tf_op jit(solution)/shard_map/ppermute | solution.py:175
  69.7 0.7 collective-permute-done.23
  70.5 0.5 collective-permute-start.24
  71.0 2.7 %collective-permute-done.20 = bf16[64,2048]{1,0:T(8,128)(2,1)S(1)} collective-permute-done((bf16[64,2048]{1,0:T(8,128)(2,1)S(1)}, bf16[64,2048]{1,0:T(8,128)(2,1)S(1)}, u32[]{:S(2)}, u32[]{:S(2)}) %collective-permute-start.20) | collective-permute-done | bytes 262176 | tf_op jit(solution)/shard_map/ppermute | solution.py:175
  73.7 1.6 %collective-permute-start.21 = (bf16[64,2048]{1,0:T(8,128)(2,1)S(1)}, bf16[64,2048]{1,0:T(8,128)(2,1)S(1)}, u32[]{:S(2)}, u32[]{:S(2)}) collective-permute-start(bf16[64,2048]{1,0:T(8,128)(2,1)S(1)} %add_convert_fusion.7), channel_id=1, source_target_pairs={{0,8},{2,10},{8,16},{10,18},{16,24},{18,26},{24,28},{26,30},{28,20... | collective-permute-start | bytes 786440 | tf_op jit(solution)/shard_map/ppermute | solution.py:175
  75.4 0.5 collective-permute-start.16
  75.9 3.4 %collective-permute-done.26 = bf16[64,2048]{1,0:T(8,128)(2,1)S(1)} collective-permute-done((bf16[64,2048]{1,0:T(8,128)(2,1)S(1)}, bf16[64,2048]{1,0:T(8,128)(2,1)S(1)}, u32[]{:S(2)}, u32[]{:S(2)}) %collective-permute-start.26) | collective-permute-done | bytes 262176 | tf_op jit(solution)/shard_map/ppermute | solution.py:175
  79.3 1.6 %collective-permute-start.27 = (bf16[64,2048]{1,0:T(8,128)(2,1)S(1)}, bf16[64,2048]{1,0:T(8,128)(2,1)S(1)}, u32[]{:S(2)}, u32[]{:S(2)}) collective-permute-start(bf16[64,2048]{1,0:T(8,128)(2,1)S(1)} %add_convert_fusion.2), channel_id=1, source_target_pairs={{0,8},{2,10},{8,16},{10,18},{16,24},{18,26},{24,28},{26,30},{28,20... | collective-permute-start | bytes 786440 | tf_op jit(solution)/shard_map/ppermute | solution.py:175
  80.9 1.8 %collective-permute-done.16 = bf16[64,2048]{1,0:T(8,128)(2,1)S(1)} collective-permute-done((bf16[64,2048]{1,0:T(8,128)(2,1)S(1)}, bf16[64,2048]{1,0:T(8,128)(2,1)S(1)}, u32[]{:S(2)}, u32[]{:S(2)}) %collective-permute-start.16) | collective-permute-done | bytes 262176 | tf_op jit(solution)/shard_map/ppermute | solution.py:175
  82.7 0.5 collective-permute-start.17
  83.3 4.4 %collective-permute-done.27 = bf16[64,2048]{1,0:T(8,128)(2,1)S(1)} collective-permute-done((bf16[64,2048]{1,0:T(8,128)(2,1)S(1)}, bf16[64,2048]{1,0:T(8,128)(2,1)S(1)}, u32[]{:S(2)}, u32[]{:S(2)}) %collective-permute-start.27) | collective-permute-done | bytes 262176 | tf_op jit(solution)/shard_map/ppermute | solution.py:175
  87.7 1.6 %collective-permute-start.28 = (bf16[64,2048]{1,0:T(8,128)(2,1)S(1)}, bf16[64,2048]{1,0:T(8,128)(2,1)S(1)}, u32[]{:S(2)}, u32[]{:S(2)}) collective-permute-start(bf16[64,2048]{1,0:T(8,128)(2,1)S(1)} %add_convert_fusion.1), channel_id=1, source_target_pairs={{0,8},{2,10},{8,16},{10,18},{16,24},{18,26},{24,28},{26,30},{28,20... | collective-permute-start | bytes 786440 | tf_op jit(solution)/shard_map/ppermute | solution.py:175
  89.3 0.7 collective-permute-done.17
  90.1 0.5 collective-permute-start.18
  90.6 3.5 %collective-permute-done.28 = bf16[64,2048]{1,0:T(8,128)(2,1)S(1)} collective-permute-done((bf16[64,2048]{1,0:T(8,128)(2,1)S(1)}, bf16[64,2048]{1,0:T(8,128)(2,1)S(1)}, u32[]{:S(2)}, u32[]{:S(2)}) %collective-permute-start.28) | collective-permute-done | bytes 262176 | tf_op jit(solution)/shard_map/ppermute | solution.py:175
  94.1 0.1 add_convert_fusion
  94.2 2.3 %collective-permute-done.18 = bf16[64,2048]{1,0:T(8,128)(2,1)S(1)} collective-permute-done((bf16[64,2048]{1,0:T(8,128)(2,1)S(1)}, bf16[64,2048]{1,0:T(8,128)(2,1)S(1)}, u32[]{:S(2)}, u32[]{:S(2)}) %collective-permute-start.18) | collective-permute-done | bytes 262176 | tf_op jit(solution)/shard_map/ppermute | solution.py:175
  96.5 0.1 add_convert_fusion.6
  96.6 0.8 pad_maximum_fusion
  (28 shorter events, 0.6 us)
Async XLA Ops:
  0.0 20.3 %collective-permute-start.1 = (bf16[1,2048,768]{2,1,0:T(8,128)(2,1)}, bf16[1,2048,768]{2,1,0:T(8,128)(2,1)S(1)}, u32[]{:S(2)}, u32[]{:S(2)}) collective-permute-start(bf16[1,2048,768]{2,1,0:T(8,128)(2,1)} %refs_0_.1), channel_id=1, source_target_pairs={{0,2},{2,0},{4,6},{6,4},{8,10},{10,8},{12,14},{14,12},{16,18},{18,... | collective-permute-start | bytes 9437192 | tf_op jit(solution)/shard_map/ppermute | solution.py:133
  0.5 19.9 %collective-permute-start.2 = (bf16[1,2048,768]{2,1,0:T(8,128)(2,1)}, bf16[1,2048,768]{2,1,0:T(8,128)(2,1)S(1)}, u32[]{:S(2)}, u32[]{:S(2)}) collective-permute-start(bf16[1,2048,768]{2,1,0:T(8,128)(2,1)} %refs_1_.1), channel_id=1, source_target_pairs={{0,2},{2,0},{4,6},{6,4},{8,10},{10,8},{12,14},{14,12},{16,18},{18,... | collective-permute-start | bytes 9437192 | tf_op jit(solution)/shard_map/ppermute | solution.py:133
  0.5 19.9 %collective-permute-start.3 = (bf16[1,768,2048]{2,1,0:T(8,128)(2,1)}, bf16[1,768,2048]{2,1,0:T(8,128)(2,1)S(1)}, u32[]{:S(2)}, u32[]{:S(2)}) collective-permute-start(bf16[1,768,2048]{2,1,0:T(8,128)(2,1)} %refs_2_.1), channel_id=1, source_target_pairs={{0,2},{2,0},{4,6},{6,4},{8,10},{10,8},{12,14},{14,12},{16,18},{18,... | collective-permute-start | bytes 9437192 | tf_op jit(solution)/shard_map/ppermute | solution.py:133
  1.8 1.0 %copy-start.3 = (bf16[128,2048]{1,0:T(8,128)(2,1)S(1)}, bf16[128,2048]{1,0:T(8,128)(2,1)}, u32[]{:S(2)}) copy-start(bf16[128,2048]{1,0:T(8,128)(2,1)} %tokens_ref.1) | copy-start | bytes 1572868
  2.9 15.8 %collective-permute-start = (bf16[128,2176]{1,0:T(8,128)(2,1)S(1)}, bf16[128,2176]{1,0:T(8,128)(2,1)S(1)}, u32[]{:S(2)}, u32[]{:S(2)}) collective-permute-start(bf16[128,2176]{1,0:T(8,128)(2,1)S(1)} %shard_map.73.refs_0_), channel_id=1, source_target_pairs={{0,8},{2,10},{8,16},{10,18},{16,24},{18,26},{24,28},{26,30},{28,20... | collective-permute-start | bytes 1671176 | tf_op jit(solution)/shard_map/ppermute | solution.py:135
  5.5 14.8 %collective-permute-start.5 = (bf16[128,2176]{1,0:T(8,128)(2,1)S(1)}, bf16[128,2176]{1,0:T(8,128)(2,1)S(1)}, u32[]{:S(2)}, u32[]{:S(2)}) collective-permute-start(bf16[128,2176]{1,0:T(8,128)(2,1)S(1)} %shard_map.73.refs_0_), channel_id=1, source_target_pairs={{0,4},{2,6},{8,0},{10,2},{16,8},{18,10},{24,16},{26,18},{28,24},{3... | collective-permute-start | bytes 1671176 | tf_op jit(solution)/shard_map/ppermute | solution.py:135
  5.5 1.9 %copy-start = (bf16[1,2048,768]{2,1,0:T(8,128)(2,1)S(1)}, bf16[1,2048,768]{2,1,0:T(8,128)(2,1)}, u32[]{:S(2)}) copy-start(bf16[1,2048,768]{2,1,0:T(8,128)(2,1)} %refs_0_.1) | copy-start | bytes 9437188
  7.4 1.9 %copy-start.1 = (bf16[1,2048,768]{2,1,0:T(8,128)(2,1)S(1)}, bf16[1,2048,768]{2,1,0:T(8,128)(2,1)}, u32[]{:S(2)}) copy-start(bf16[1,2048,768]{2,1,0:T(8,128)(2,1)} %refs_1_.1) | copy-start | bytes 9437188
  9.3 1.9 %copy-start.2 = (bf16[1,768,2048]{2,1,0:T(8,128)(2,1)S(1)}, bf16[1,768,2048]{2,1,0:T(8,128)(2,1)}, u32[]{:S(2)}) copy-start(bf16[1,768,2048]{2,1,0:T(8,128)(2,1)} %refs_2_.1) | copy-start | bytes 9437188
  20.4 9.7 %collective-permute-start.4 = (bf16[64,2176]{1,0:T(8,128)(2,1)S(1)}, bf16[64,2176]{1,0:T(8,128)(2,1)S(1)}, u32[]{:S(2)}, u32[]{:S(2)}) collective-permute-start(bf16[64,2176]{1,0:T(8,128)(2,1)S(1)} %get-tuple-element.54.refs_0_), channel_id=1, source_target_pairs={{0,8},{2,10},{8,16},{10,18},{16,24},{18,26},{24,28},{26,30},{28,20... | collective-permute-start | bytes 835592 | tf_op jit(solution)/shard_map/ppermute | solution.py:149
  22.0 9.6 %collective-permute-start.7 = (bf16[64,2176]{1,0:T(8,128)(2,1)S(1)}, bf16[64,2176]{1,0:T(8,128)(2,1)S(1)}, u32[]{:S(2)}, u32[]{:S(2)}) collective-permute-start(bf16[64,2176]{1,0:T(8,128)(2,1)S(1)} %get-tuple-element.57.refs_1_), channel_id=1, source_target_pairs={{0,4},{2,6},{8,0},{10,2},{16,8},{18,10},{24,16},{26,18},{28,24},{3... | collective-permute-start | bytes 835592 | tf_op jit(solution)/shard_map/ppermute | solution.py:149
  25.2 12.3 %collective-permute-start.11 = (bf16[64,2176]{1,0:T(8,128)(2,1)S(1)}, bf16[64,2176]{1,0:T(8,128)(2,1)S(1)}, u32[]{:S(2)}, u32[]{:S(2)}) collective-permute-start(bf16[64,2176]{1,0:T(8,128)(2,1)S(1)} %get-tuple-element.67.refs_0_), channel_id=1, source_target_pairs={{0,4},{2,6},{8,0},{10,2},{16,8},{18,10},{24,16},{26,18},{28,24},{3... | collective-permute-start | bytes 835592 | tf_op jit(solution)/shard_map/ppermute | solution.py:149
  25.6 12.0 %collective-permute-start.13 = (bf16[64,2176]{1,0:T(8,128)(2,1)S(1)}, bf16[64,2176]{1,0:T(8,128)(2,1)S(1)}, u32[]{:S(2)}, u32[]{:S(2)}) collective-permute-start(bf16[64,2176]{1,0:T(8,128)(2,1)S(1)} %get-tuple-element.69.refs_1_), channel_id=1, source_target_pairs={{0,8},{2,10},{8,16},{10,18},{16,24},{18,26},{24,28},{26,30},{28,20... | collective-permute-start | bytes 835592 | tf_op jit(solution)/shard_map/ppermute | solution.py:149
  31.6 10.8 %collective-permute-start.6 = (bf16[64,2176]{1,0:T(8,128)(2,1)S(1)}, bf16[64,2176]{1,0:T(8,128)(2,1)S(1)}, u32[]{:S(2)}, u32[]{:S(2)}) collective-permute-start(bf16[64,2176]{1,0:T(8,128)(2,1)S(1)} %collective-permute-done.4.refs_0_), channel_id=1, source_target_pairs={{0,8},{2,10},{8,16},{10,18},{16,24},{18,26},{24,28},{26,30},{28,20... | collective-permute-start | bytes 835592 | tf_op jit(solution)/shard_map/ppermute | solution.py:149
  33.2 10.4 %collective-permute-start.9 = (bf16[64,2176]{1,0:T(8,128)(2,1)S(1)}, bf16[64,2176]{1,0:T(8,128)(2,1)S(1)}, u32[]{:S(2)}, u32[]{:S(2)}) collective-permute-start(bf16[64,2176]{1,0:T(8,128)(2,1)S(1)} %collective-permute-done.7.refs_1_), channel_id=1, source_target_pairs={{0,4},{2,6},{8,0},{10,2},{16,8},{18,10},{24,16},{26,18},{28,24},{3... | collective-permute-start | bytes 835592 | tf_op jit(solution)/shard_map/ppermute | solution.py:149
  37.6 11.9 %collective-permute-start.12 = (bf16[64,2176]{1,0:T(8,128)(2,1)S(1)}, bf16[64,2176]{1,0:T(8,128)(2,1)S(1)}, u32[]{:S(2)}, u32[]{:S(2)}) collective-permute-start(bf16[64,2176]{1,0:T(8,128)(2,1)S(1)} %collective-permute-done.11.refs_0_), channel_id=1, source_target_pairs={{0,4},{2,6},{8,0},{10,2},{16,8},{18,10},{24,16},{26,18},{28,24},{3... | collective-permute-start | bytes 835592 | tf_op jit(solution)/shard_map/ppermute | solution.py:149
  38.0 11.5 %collective-permute-start.14 = (bf16[64,2176]{1,0:T(8,128)(2,1)S(1)}, bf16[64,2176]{1,0:T(8,128)(2,1)S(1)}, u32[]{:S(2)}, u32[]{:S(2)}) collective-permute-start(bf16[64,2176]{1,0:T(8,128)(2,1)S(1)} %collective-permute-done.13.refs_1_), channel_id=1, source_target_pairs={{0,8},{2,10},{8,16},{10,18},{16,24},{18,26},{24,28},{26,30},{28,20... | collective-permute-start | bytes 835592 | tf_op jit(solution)/shard_map/ppermute | solution.py:149
  43.5 10.9 %collective-permute-start.8 = (bf16[64,2176]{1,0:T(8,128)(2,1)S(1)}, bf16[64,2176]{1,0:T(8,128)(2,1)S(1)}, u32[]{:S(2)}, u32[]{:S(2)}) collective-permute-start(bf16[64,2176]{1,0:T(8,128)(2,1)S(1)} %collective-permute-done.6.refs_0_), channel_id=1, source_target_pairs={{0,8},{2,10},{8,16},{10,18},{16,24},{18,26},{24,28},{26,30},{28,20... | collective-permute-start | bytes 835592 | tf_op jit(solution)/shard_map/ppermute | solution.py:149
  45.1 10.4 %collective-permute-start.10 = (bf16[64,2176]{1,0:T(8,128)(2,1)S(1)}, bf16[64,2176]{1,0:T(8,128)(2,1)S(1)}, u32[]{:S(2)}, u32[]{:S(2)}) collective-permute-start(bf16[64,2176]{1,0:T(8,128)(2,1)S(1)} %collective-permute-done.9.refs_1_), channel_id=1, source_target_pairs={{0,4},{2,6},{8,0},{10,2},{16,8},{18,10},{24,16},{26,18},{28,24},{3... | collective-permute-start | bytes 835592 | tf_op jit(solution)/shard_map/ppermute | solution.py:149
  52.3 8.8 %collective-permute-start.22 = (bf16[64,2048]{1,0:T(8,128)(2,1)S(1)}, bf16[64,2048]{1,0:T(8,128)(2,1)S(1)}, u32[]{:S(2)}, u32[]{:S(2)}) collective-permute-start(bf16[64,2048]{1,0:T(8,128)(2,1)S(1)} %get-tuple-element.88), channel_id=1, source_target_pairs={{0,4},{2,6},{8,0},{10,2},{16,8},{18,10},{24,16},{26,18},{28,24},{3... | collective-permute-start | bytes 786440 | tf_op jit(solution)/shard_map/ppermute | solution.py:175
  52.8 8.9 %collective-permute-start.19 = (bf16[64,2048]{1,0:T(8,128)(2,1)S(1)}, bf16[64,2048]{1,0:T(8,128)(2,1)S(1)}, u32[]{:S(2)}, u32[]{:S(2)}) collective-permute-start(bf16[64,2048]{1,0:T(8,128)(2,1)S(1)} %get-tuple-element.79), channel_id=1, source_target_pairs={{0,8},{2,10},{8,16},{10,18},{16,24},{18,26},{24,28},{26,30},{28,20... | collective-permute-start | bytes 786440 | tf_op jit(solution)/shard_map/ppermute | solution.py:175
  58.3 17.1 %collective-permute-start.15 = (bf16[64,2048]{1,0:T(8,128)(2,1)S(1)}, bf16[64,2048]{1,0:T(8,128)(2,1)S(1)}, u32[]{:S(2)}, u32[]{:S(2)}) collective-permute-start(bf16[64,2048]{1,0:T(8,128)(2,1)S(1)} %get-tuple-element.82), channel_id=1, source_target_pairs={{0,4},{2,6},{8,0},{10,2},{16,8},{18,10},{24,16},{26,18},{28,24},{3... | collective-permute-start | bytes 786440 | tf_op jit(solution)/shard_map/ppermute | solution.py:175
  58.8 9.2 %collective-permute-start.25 = (bf16[64,2048]{1,0:T(8,128)(2,1)S(1)}, bf16[64,2048]{1,0:T(8,128)(2,1)S(1)}, u32[]{:S(2)}, u32[]{:S(2)}) collective-permute-start(bf16[64,2048]{1,0:T(8,128)(2,1)S(1)} %get-tuple-element.93), channel_id=1, source_target_pairs={{0,8},{2,10},{8,16},{10,18},{16,24},{18,26},{24,28},{26,30},{28,20... | collective-permute-start | bytes 786440 | tf_op jit(solution)/shard_map/ppermute | solution.py:175
  61.2 9.3 %collective-permute-start.23 = (bf16[64,2048]{1,0:T(8,128)(2,1)S(1)}, bf16[64,2048]{1,0:T(8,128)(2,1)S(1)}, u32[]{:S(2)}, u32[]{:S(2)}) collective-permute-start(bf16[64,2048]{1,0:T(8,128)(2,1)S(1)} %add_convert_fusion.5), channel_id=1, source_target_pairs={{0,4},{2,6},{8,0},{10,2},{16,8},{18,10},{24,16},{26,18},{28,24},{3... | collective-permute-start | bytes 786440 | tf_op jit(solution)/shard_map/ppermute | solution.py:175
  61.7 11.9 %collective-permute-start.20 = (bf16[64,2048]{1,0:T(8,128)(2,1)S(1)}, bf16[64,2048]{1,0:T(8,128)(2,1)S(1)}, u32[]{:S(2)}, u32[]{:S(2)}) collective-permute-start(bf16[64,2048]{1,0:T(8,128)(2,1)S(1)} %add_convert_fusion.8), channel_id=1, source_target_pairs={{0,8},{2,10},{8,16},{10,18},{16,24},{18,26},{24,28},{26,30},{28,20... | collective-permute-start | bytes 786440 | tf_op jit(solution)/shard_map/ppermute | solution.py:175
  68.1 11.2 %collective-permute-start.26 = (bf16[64,2048]{1,0:T(8,128)(2,1)S(1)}, bf16[64,2048]{1,0:T(8,128)(2,1)S(1)}, u32[]{:S(2)}, u32[]{:S(2)}) collective-permute-start(bf16[64,2048]{1,0:T(8,128)(2,1)S(1)} %add_convert_fusion.3), channel_id=1, source_target_pairs={{0,8},{2,10},{8,16},{10,18},{16,24},{18,26},{24,28},{26,30},{28,20... | collective-permute-start | bytes 786440 | tf_op jit(solution)/shard_map/ppermute | solution.py:175
  70.5 20.1 %collective-permute-start.24 = (bf16[64,2048]{1,0:T(8,128)(2,1)S(1)}, bf16[64,2048]{1,0:T(8,128)(2,1)S(1)}, u32[]{:S(2)}, u32[]{:S(2)}) collective-permute-start(bf16[64,2048]{1,0:T(8,128)(2,1)S(1)} %add_convert_fusion.4), channel_id=1, source_target_pairs={{0,4},{2,6},{8,0},{10,2},{16,8},{18,10},{24,16},{26,18},{28,24},{3... | collective-permute-start | bytes 786440 | tf_op jit(solution)/shard_map/ppermute | solution.py:175
  73.7 20.5 %collective-permute-start.21 = (bf16[64,2048]{1,0:T(8,128)(2,1)S(1)}, bf16[64,2048]{1,0:T(8,128)(2,1)S(1)}, u32[]{:S(2)}, u32[]{:S(2)}) collective-permute-start(bf16[64,2048]{1,0:T(8,128)(2,1)S(1)} %add_convert_fusion.7), channel_id=1, source_target_pairs={{0,8},{2,10},{8,16},{10,18},{16,24},{18,26},{24,28},{26,30},{28,20... | collective-permute-start | bytes 786440 | tf_op jit(solution)/shard_map/ppermute | solution.py:175
  75.4 7.3 %collective-permute-start.16 = (bf16[64,2048]{1,0:T(8,128)(2,1)S(1)}, bf16[64,2048]{1,0:T(8,128)(2,1)S(1)}, u32[]{:S(2)}, u32[]{:S(2)}) collective-permute-start(bf16[64,2048]{1,0:T(8,128)(2,1)S(1)} %add_convert_fusion.11), channel_id=1, source_target_pairs={{0,4},{2,6},{8,0},{10,2},{16,8},{18,10},{24,16},{26,18},{28,24},{3... | collective-permute-start | bytes 786440 | tf_op jit(solution)/shard_map/ppermute | solution.py:175
  79.3 8.3 %collective-permute-start.27 = (bf16[64,2048]{1,0:T(8,128)(2,1)S(1)}, bf16[64,2048]{1,0:T(8,128)(2,1)S(1)}, u32[]{:S(2)}, u32[]{:S(2)}) collective-permute-start(bf16[64,2048]{1,0:T(8,128)(2,1)S(1)} %add_convert_fusion.2), channel_id=1, source_target_pairs={{0,8},{2,10},{8,16},{10,18},{16,24},{18,26},{24,28},{26,30},{28,20... | collective-permute-start | bytes 786440 | tf_op jit(solution)/shard_map/ppermute | solution.py:175
  82.7 7.3 %collective-permute-start.17 = (bf16[64,2048]{1,0:T(8,128)(2,1)S(1)}, bf16[64,2048]{1,0:T(8,128)(2,1)S(1)}, u32[]{:S(2)}, u32[]{:S(2)}) collective-permute-start(bf16[64,2048]{1,0:T(8,128)(2,1)S(1)} %add_convert_fusion.10), channel_id=1, source_target_pairs={{0,4},{2,6},{8,0},{10,2},{16,8},{18,10},{24,16},{26,18},{28,24},{3... | collective-permute-start | bytes 786440 | tf_op jit(solution)/shard_map/ppermute | solution.py:175
  87.7 6.4 %collective-permute-start.28 = (bf16[64,2048]{1,0:T(8,128)(2,1)S(1)}, bf16[64,2048]{1,0:T(8,128)(2,1)S(1)}, u32[]{:S(2)}, u32[]{:S(2)}) collective-permute-start(bf16[64,2048]{1,0:T(8,128)(2,1)S(1)} %add_convert_fusion.1), channel_id=1, source_target_pairs={{0,8},{2,10},{8,16},{10,18},{16,24},{18,26},{24,28},{26,30},{28,20... | collective-permute-start | bytes 786440 | tf_op jit(solution)/shard_map/ppermute | solution.py:175
  90.1 6.4 %collective-permute-start.18 = (bf16[64,2048]{1,0:T(8,128)(2,1)S(1)}, bf16[64,2048]{1,0:T(8,128)(2,1)S(1)}, u32[]{:S(2)}, u32[]{:S(2)}) collective-permute-start(bf16[64,2048]{1,0:T(8,128)(2,1)S(1)} %add_convert_fusion.9), channel_id=1, source_target_pairs={{0,4},{2,6},{8,0},{10,2},{16,8},{18,10},{24,16},{26,18},{28,24},{3... | collective-permute-start | bytes 786440 | tf_op jit(solution)/shard_map/ppermute | solution.py:175

commit v4 on v3

--- a/solution.py
+++ b/solution.py
@@ -8,29 +8,38 @@
 from jax.sharding import PartitionSpec as P
 
 LANES = 128
+TILE = 16
 
 
 def pack_kernel(tokens_ref, scores_ref, out_ref):
     rows, width = tokens_ref.shape
-    n_dev = scores_ref.shape[0]
-    scores = scores_ref[...]
-    high = scores.astype(jnp.bfloat16).astype(jnp.float32)
-    blank = jnp.zeros((out_ref.shape[1] - width - 2 * n_dev, rows), jnp.float32)
-    parts = [high, scores - high] + ([blank] if blank.shape[0] else [])
-    out_ref[:, :width] = tokens_ref[...]
-    out_ref[:, width:] = jnp.concatenate(parts, axis=0).T.astype(jnp.bfloat16)
-
-
-def pack(tokens, expert_ids, gate_scores, partner, n_dev):
+    chips = scores_ref.shape[0] // 2
+    half = rows // 2
+    lane = lax.broadcasted_iota(jnp.int32, (chips, LANES), 1)
+    even, odd = (scores_ref[pl.ds(i, chips, stride=2), :] for i in range(2))
+    at = 0
+    for h in range(2):
+        for g in range(0, half, TILE):
+            for j in range(0, width, LANES):
+                out_ref[pl.ds(at, TILE), :] = tokens_ref[pl.ds(h * half + g, TILE), pl.ds(j, LANES)]
+                at += TILE
+        first, second = (even, pltpu.roll(odd, half, 1)) if h == 0 else (pltpu.roll(even, half, 1), odd)
+        scores = jnp.where(lane < half, first, second)
+        high = scores.astype(jnp.bfloat16).astype(jnp.float32)
+        tail = jnp.concatenate([high, scores - high], axis=0).astype(jnp.bfloat16)
+        out_ref[pl.ds(at, 2 * chips), :] = tail
+        at += 2 * chips
+
+
+def pack(tokens, expert_ids, gate_scores, partner):
     scores = jnp.sum(jnp.where(expert_ids.T[None] == partner[:, None, None], gate_scores.T[None], 0.0), axis=1)
     rows, width = tokens.shape
-    extra = -(-2 * n_dev // LANES) * LANES
     near = pl.BlockSpec(memory_space=pltpu.VMEM)
     return pl.pallas_call(
         pack_kernel,
         in_specs=[near, near],
         out_specs=near,
-        out_shape=jax.ShapeDtypeStruct((rows, width + extra), jnp.bfloat16),
+        out_shape=jax.ShapeDtypeStruct((rows * width // LANES + 2 * scores.shape[0], LANES), jnp.bfloat16),
         compiler_params=pltpu.CompilerParams(vmem_limit_bytes=4 * 2**20),
     )(tokens, scores)
 
@@ -62,21 +71,26 @@
 def ffn_kernel(n_in, n_out, n_dev, *refs):
     x_refs, weights, refs = refs[:n_in], refs[n_in : n_in + 6], refs[n_in + 6 :]
     out_refs, (rows, total) = refs[:n_out], refs[n_out:]
-    half = out_refs[0].shape[0]
-    width = total.shape[1]
+    half, width = out_refs[0].shape
     me = lax.axis_index("ep")
-    slots = (me, me + 1 - 2 * (me % 2))
-    tails = []
-    at = 0
+    chip, core = me // 2, me % 2
+    row = lax.broadcasted_iota(jnp.int32, (n_dev, LANES), 0)
+    hit = (row == chip) | (row == chip + n_dev // 2)
+    columns = []
     for x_ref in x_refs:
-        rows[pl.ds(at, x_ref.shape[0]), :] = x_ref[:, :width]
-        tails.append(x_ref[:, width:].astype(jnp.float32))
-        at += x_ref.shape[0]
-    tails = jnp.concatenate(tails, axis=0)
-    lane = lax.broadcasted_iota(jnp.int32, tails.shape, 1)
-    for expert, slot in enumerate(slots):
-        hit = (lane == slot) | (lane == slot + n_dev)
-        score = jnp.sum(jnp.where(hit, tails, 0.0), axis=1, keepdims=True)
+        at = 0
+        while at < x_ref.shape[0]:
+            for g in range(0, half, TILE):
+                for j in range(0, width, LANES):
+                    rows[pl.ds(len(columns) * half + g, TILE), pl.ds(j, LANES)] = x_ref[pl.ds(at, TILE), :]
+                    at += TILE
+            tail = jnp.where(hit, x_ref[pl.ds(at, n_dev), :].astype(jnp.float32), 0.0)
+            both = jnp.broadcast_to(jnp.sum(tail, axis=0, keepdims=True), (LANES, LANES)).T[:, 0:1]
+            columns.append((both[:half], both[half:]))
+            at += n_dev
+    first, second = (jnp.concatenate([pair[i] for pair in columns], axis=0) for i in range(2))
+    for expert in range(2):
+        score = jnp.where(core == expert, first, second)
         gate_ref, up_ref, down_ref = weights[3 * expert : 3 * expert + 3]
         x = rows[...]
         gate = jnp.dot(x, gate_ref[0], preferred_element_type=jnp.float32)
@@ -93,8 +107,8 @@
 
 def ffn(blocks, half, kinds, own, other, n_dev):
     _, width, ff = own[0].shape
-    m = sum(block.shape[0] for block in blocks)
     n_in, n_out = len(blocks), len(kinds)
+    m = n_out * half
     near = pl.BlockSpec(memory_space=pltpu.VMEM)
     return pl.pallas_call(
         functools.partial(ffn_kernel, n_in, n_out, n_dev),
@@ -131,10 +145,10 @@
 
     half = tokens.shape[0] // 2
     other = [lax.ppermute(w, "ep", swap) for w in own]
-    packed = pack(tokens, expert_ids, gate_scores, partner, n_dev)
+    packed = pack(tokens, expert_ids, gate_scores, partner)
     first = [lax.ppermute(packed, "ep", perm[d]) for d in range(2)]
     own = load(own)
-    held = {(d, h, 1): block[h * half : (h + 1) * half] for d, block in enumerate(first) for h in range(2)}
+    held = {(d, h, 1): part for d, block in enumerate(first) for h, part in enumerate(jnp.split(block, 2))}
     last = {(d, h): far if d == h else far - 1 for d in range(2) for h in range(2)}
     done = {}
 
@@ -168,10 +182,12 @@
     back = {}
 
     def give(names, *deps):
-        for d, h, s in names:
+        arrived = [back[n[:2]] for n in names if n[:2] in back]
+        arrived = tie(arrived, *deps) if arrived else [None] * len(names)
+        for (d, h, s), old in zip(names, arrived):
             part = done[d, h, s]
-            if (d, h) in back:
-                part = (tie(back[d, h], *deps).astype(jnp.float32) + part).astype(jnp.bfloat16)
+            if old is not None:
+                part = (old.astype(jnp.float32) + part).astype(jnp.bfloat16)
             back[d, h] = lax.ppermute(part, "ep", perm[1 - d])
 
     give(flows(1, far - 1))
@@ -179,7 +195,7 @@
     for s in range(far - 1, 0, -1):
         if s > 1:
             give(flows(1, s - 1), worked[-1])
-        give(flows(0, s))
+        give(flows(0, s), *([back[f] for f in groups[1]] if s == 1 else []))
     compute([(0, 0, 0), (0, 1, 0)], [packed], worked[-1])
     out = [
         (done[0, h, 0] + back[0, h].astype(jnp.float32) + back[1, h].astype(jnp.float32)).astype(jnp.bfloat16)

time: 97.7 us -> 95.8 us (0.981)
  waiting for transfers between devices: 36.2 us -> 32.9 us
  Pallas kernels: 23.1 us -> 24.4 us
    ppermute x10, waiting for transfers between devices: 5.99 us -> 2.99 us  [send(): held[d, h, s] = lax.ppermute(tie(held[d, h, s - 1], *deps), 'ep', perm[d])]
    pallas_call x8, Pallas kernels: 22.3 us -> 23.7 us  [ffn(): pl.pallas_call(functools.partial(ffn_kernel, n_in, n_out, n_dev), in_spec...]
  transfers between devices with their start and end apart: 29 -> 29, of which waited for: 17 -> 15; matrix products, arithmetic and copies ran while one was open for 1% -> 2% of each run, Pallas kernels for 24% -> 26%
where the time goes in v4:
time: 95.8 us; the launch traced here: 95.5 us
  waiting for transfers between devices  32.9 us (34%)
  starting transfers between devices  28.9 us (30%)
  Pallas kernels  24.4 us (25%)
  local copies, waits for them, and re-layouts  6.77 us (7%)
  other arithmetic  2.34 us (2%)
    pallas_call x8, Pallas kernels, ffn(): pl.pallas_call(functools.partial(ffn_kernel, n_in, n_out, n_dev), in_spec...  23.7 us
    ppermute x14, waiting for transfers between devices, give(): back[d, h] = lax.ppermute(part, 'ep', perm[1 - d])  22 us
    ppermute x14, starting transfers between devices, give(): back[d, h] = lax.ppermute(part, 'ep', perm[1 - d])  15.1 us
    ppermute x10, starting transfers between devices, send(): held[d, h, s] = lax.ppermute(tie(held[d, h, s - 1], *deps), 'ep', perm[d])  10.2 us
    ppermute x2, waiting for transfers between devices, on_device(): first = [lax.ppermute(packed, 'ep', perm[d]) for d in range(2)]  7.85 us
    unnamed x8, local copies, waits for them, and re-layouts  6.7 us
    ppermute x10, waiting for transfers between devices, send(): held[d, h, s] = lax.ppermute(tie(held[d, h, s - 1], *deps), 'ep', perm[d])  2.99 us
    ppermute x2, starting transfers between devices, on_device(): first = [lax.ppermute(packed, 'ep', perm[d]) for d in range(2)]  2.63 us
  transfers between devices with their start and end apart: 29, of which 15 were waited for; matrix products, arithmetic and copies ran while one was open for 2% of the time, Pallas kernels for 26%

profile of v4, /device:TPU:0, one launch (start us, length us, event | category | flops | bytes accessed | tf_op | source)
XLA Modules:
  0.0 95.5 jit_solution(13657085427612533406)
XLA Ops:
  0.0 0.5 collective-permute-start.1
  0.5 0.5 collective-permute-start.3
  1.0 0.8 select_reduce_fusion.scores_ref
  1.8 1.0 %copy-done.3 = bf16[128,2048]{1,0:T(8,128)(2,1)S(1)} copy-done((bf16[128,2048]{1,0:T(8,128)(2,1)S(1)}, bf16[128,2048]{1,0:T(8,128)(2,1)}, u32[]{:S(2)}) %copy-start.3) | copy-done | bytes 524312
  2.8 0.1 shard_map.73.refs_0_
  2.9 2.6 %collective-permute-start = (bf16[2080,128]{1,0:T(8,128)(2,1)S(1)}, bf16[2080,128]{1,0:T(8,128)(2,1)S(1)}, u32[]{:S(2)}, u32[]{:S(2)}) collective-permute-start(bf16[2080,128]{1,0:T(8,128)(2,1)S(1)} %shard_map.73.refs_0_), channel_id=1, source_target_pairs={{0,8},{2,10},{8,16},{10,18},{16,24},{18,26},{24,28},{26,30},{28,20... | collective-permute-start | bytes 1597448 | tf_op jit(solution)/shard_map/ppermute | solution.py:149
  5.5 1.9 %copy-done = bf16[1,2048,768]{2,1,0:T(8,128)(2,1)S(1)} copy-done((bf16[1,2048,768]{2,1,0:T(8,128)(2,1)S(1)}, bf16[1,2048,768]{2,1,0:T(8,128)(2,1)}, u32[]{:S(2)}) %copy-start) | copy-done | bytes 3145752
  7.4 1.9 %copy-done.1 = bf16[1,2048,768]{2,1,0:T(8,128)(2,1)S(1)} copy-done((bf16[1,2048,768]{2,1,0:T(8,128)(2,1)S(1)}, bf16[1,2048,768]{2,1,0:T(8,128)(2,1)}, u32[]{:S(2)}) %copy-start.1) | copy-done | bytes 3145752
  9.3 1.9 %copy-done.2 = bf16[1,768,2048]{2,1,0:T(8,128)(2,1)S(1)} copy-done((bf16[1,768,2048]{2,1,0:T(8,128)(2,1)S(1)}, bf16[1,768,2048]{2,1,0:T(8,128)(2,1)}, u32[]{:S(2)}) %copy-start.2) | copy-done | bytes 3145752
  11.2 0.7 shard_map.74
  11.9 6.3 %collective-permute-done = bf16[2080,128]{1,0:T(8,128)(2,1)S(1)} collective-permute-done((bf16[2080,128]{1,0:T(8,128)(2,1)S(1)}, bf16[2080,128]{1,0:T(8,128)(2,1)S(1)}, u32[]{:S(2)}, u32[]{:S(2)}) %collective-permute-start) | collective-permute-done | bytes 532512 | tf_op jit(solution)/shard_map/ppermute | solution.py:149
  18.3 1.5 %collective-permute-done.5 = bf16[2080,128]{1,0:T(8,128)(2,1)S(1)} collective-permute-done((bf16[2080,128]{1,0:T(8,128)(2,1)S(1)}, bf16[2080,128]{1,0:T(8,128)(2,1)S(1)}, u32[]{:S(2)}, u32[]{:S(2)}) %collective-permute-start.5) | collective-permute-done | bytes 532512 | tf_op jit(solution)/shard_map/ppermute | solution.py:149
  19.8 1.6 %collective-permute-start.4 = (bf16[1040,128]{1,0:T(8,128)(2,1)S(1)}, bf16[1040,128]{1,0:T(8,128)(2,1)S(1)}, u32[]{:S(2)}, u32[]{:S(2)}) collective-permute-start(bf16[1040,128]{1,0:T(8,128)(2,1)S(1)} %get-tuple-element.60.refs_0_), channel_id=1, source_target_pairs={{0,8},{2,10},{8,16},{10,18},{16,24},{18,26},{24,28},{26,30},{28,20... | collective-permute-start | bytes 798728 | tf_op jit(solution)/shard_map/ppermute | solution.py:163
  21.5 0.4 collective-permute-start.7
  21.9 3.0 %shard_map.75 = (f32[64,2048]{1,0:T(8,128)S(1)}, f32[64,2048]{1,0:T(8,128)S(1)}) custom-call(bf16[1040,128]{1,0:T(8,128)(2,1)S(1)} %get-tuple-element.60.refs_0_, bf16[1040,128]{1,0:T(8,128)(2,1)S(1)} %get-tuple-element.63.refs_1_, bf16[1,2048,768]{2,1,0:T(8,128)(2,1)S(1)} %get-tuple-element.57.refs_2_.refs_1_, ...), custom_call_target="tpu_custom_call" | custom-call | flops 2415919104 | bytes 20447232 | tf_op jit(solution)/shard_map/pallas_call | solution.py:113
  24.9 0.3 collective-permute-start.11
  25.2 1.7 %collective-permute-start.13 = (bf16[1040,128]{1,0:T(8,128)(2,1)S(1)}, bf16[1040,128]{1,0:T(8,128)(2,1)S(1)}, u32[]{:S(2)}, u32[]{:S(2)}) collective-permute-start(bf16[1040,128]{1,0:T(8,128)(2,1)S(1)} %get-tuple-element.75.refs_1_), channel_id=1, source_target_pairs={{0,8},{2,10},{8,16},{10,18},{16,24},{18,26},{24,28},{26,30},{28,20... | collective-permute-start | bytes 798728 | tf_op jit(solution)/shard_map/ppermute | solution.py:163
  27.0 3.0 %shard_map.76 = (f32[64,2048]{1,0:T(8,128)S(1)}, f32[64,2048]{1,0:T(8,128)S(1)}) custom-call(bf16[1040,128]{1,0:T(8,128)(2,1)S(1)} %get-tuple-element.73.refs_0_, bf16[1040,128]{1,0:T(8,128)(2,1)S(1)} %get-tuple-element.75.refs_1_, bf16[1,2048,768]{2,1,0:T(8,128)(2,1)S(1)} %get-tuple-element.57.refs_2_.refs_1_, ...), custom_call_target="tpu_custom_call" | custom-call | flops 2415919104 | bytes 20447232 | tf_op jit(solution)/shard_map/pallas_call | solution.py:113
  29.9 0.9 collective-permute-done.7.refs_1_
  30.8 1.6 %collective-permute-start.6 = (bf16[1040,128]{1,0:T(8,128)(2,1)S(1)}, bf16[1040,128]{1,0:T(8,128)(2,1)S(1)}, u32[]{:S(2)}, u32[]{:S(2)}) collective-permute-start(bf16[1040,128]{1,0:T(8,128)(2,1)S(1)} %collective-permute-done.4.refs_0_), channel_id=1, source_target_pairs={{0,8},{2,10},{8,16},{10,18},{16,24},{18,26},{24,28},{26,30},{28,20... | collective-permute-start | bytes 798728 | tf_op jit(solution)/shard_map/ppermute | solution.py:163
  32.4 0.4 collective-permute-start.9
  32.8 3.0 %shard_map.77 = (f32[64,2048]{1,0:T(8,128)S(1)}, f32[64,2048]{1,0:T(8,128)S(1)}) custom-call(bf16[1040,128]{1,0:T(8,128)(2,1)S(1)} %collective-permute-done.4.refs_0_, bf16[1040,128]{1,0:T(8,128)(2,1)S(1)} %collective-permute-done.7.refs_1_, bf16[1,2048,768]{2,1,0:T(8,128)(2,1)S(1)} %get-tuple-element.57.refs_2_.refs_1_, ...), custom_call_target="tpu_custom_call" | custom-call | flops 2415919104 | bytes 20447232 | tf_op jit(solution)/shard_map/pallas_call | solution.py:113
  35.8 0.7 collective-permute-done.11.refs_0_
  36.5 0.5 collective-permute-start.12
  37.0 1.6 %collective-permute-start.14 = (bf16[1040,128]{1,0:T(8,128)(2,1)S(1)}, bf16[1040,128]{1,0:T(8,128)(2,1)S(1)}, u32[]{:S(2)}, u32[]{:S(2)}) collective-permute-start(bf16[1040,128]{1,0:T(8,128)(2,1)S(1)} %collective-permute-done.13.refs_1_), channel_id=1, source_target_pairs={{0,8},{2,10},{8,16},{10,18},{16,24},{18,26},{24,28},{26,30},{28,20... | collective-permute-start | bytes 798728 | tf_op jit(solution)/shard_map/ppermute | solution.py:163
  38.5 3.0 %shard_map.78 = (f32[64,2048]{1,0:T(8,128)S(1)}, f32[64,2048]{1,0:T(8,128)S(1)}) custom-call(bf16[1040,128]{1,0:T(8,128)(2,1)S(1)} %collective-permute-done.11.refs_0_, bf16[1040,128]{1,0:T(8,128)(2,1)S(1)} %collective-permute-done.13.refs_1_, bf16[1,2048,768]{2,1,0:T(8,128)(2,1)S(1)} %get-tuple-element.57.refs_2_.refs_1_, ...), custom_call_target="tpu_custom_call" | custom-call | flops 2415919104 | bytes 20447232 | tf_op jit(solution)/shard_map/pallas_call | solution.py:113
  41.5 0.7 collective-permute-done.9.refs_1_
  42.2 1.6 %collective-permute-start.8 = (bf16[1040,128]{1,0:T(8,128)(2,1)S(1)}, bf16[1040,128]{1,0:T(8,128)(2,1)S(1)}, u32[]{:S(2)}, u32[]{:S(2)}) collective-permute-start(bf16[1040,128]{1,0:T(8,128)(2,1)S(1)} %collective-permute-done.6.refs_0_), channel_id=1, source_target_pairs={{0,8},{2,10},{8,16},{10,18},{16,24},{18,26},{24,28},{26,30},{28,20... | collective-permute-start | bytes 798728 | tf_op jit(solution)/shard_map/ppermute | solution.py:163
  43.8 0.4 collective-permute-start.10
  44.2 3.0 %shard_map.79 = (f32[64,2048]{1,0:T(8,128)S(1)}, f32[64,2048]{1,0:T(8,128)S(1)}) custom-call(bf16[1040,128]{1,0:T(8,128)(2,1)S(1)} %collective-permute-done.6.refs_0_, bf16[1040,128]{1,0:T(8,128)(2,1)S(1)} %collective-permute-done.9.refs_1_, bf16[1,2048,768]{2,1,0:T(8,128)(2,1)S(1)} %get-tuple-element.57.refs_2_.refs_1_, ...), custom_call_target="tpu_custom_call" | custom-call | flops 2415919104 | bytes 20447232 | tf_op jit(solution)/shard_map/pallas_call | solution.py:113
  47.2 0.7 collective-permute-done.12.refs_0_
  47.9 3.0 %shard_map.80 = (bf16[64,2048]{1,0:T(8,128)(2,1)S(1)}, bf16[64,2048]{1,0:T(8,128)(2,1)S(1)}) custom-call(bf16[1040,128]{1,0:T(8,128)(2,1)S(1)} %collective-permute-done.12.refs_0_, bf16[1040,128]{1,0:T(8,128)(2,1)S(1)} %collective-permute-done.14.refs_1_, bf16[1,2048,768]{2,1,0:T(8,128)(2,1)S(1)} %get-tuple-element.57.refs_2_.refs_1_, ...), custom_call_target="tpu_custom_call" | custom-call | flops 2415919104 | bytes 20447232 | tf_op jit(solution)/shard_map/pallas_call | solution.py:113
  50.9 1.6 %collective-permute-start.21 = (bf16[64,2048]{1,0:T(8,128)(2,1)S(1)}, bf16[64,2048]{1,0:T(8,128)(2,1)S(1)}, u32[]{:S(2)}, u32[]{:S(2)}) collective-permute-start(bf16[64,2048]{1,0:T(8,128)(2,1)S(1)} %get-tuple-element.85), channel_id=1, source_target_pairs={{0,8},{2,10},{8,16},{10,18},{16,24},{18,26},{24,28},{26,30},{28,20... | collective-permute-start | bytes 786440 | tf_op jit(solution)/shard_map/ppermute | solution.py:191
  52.5 0.4 collective-permute-start.22
  53.0 3.0 %shard_map.81 = (bf16[64,2048]{1,0:T(8,128)(2,1)S(1)}, bf16[64,2048]{1,0:T(8,128)(2,1)S(1)}) custom-call(bf16[1040,128]{1,0:T(8,128)(2,1)S(1)} %collective-permute-done.8.refs_0_, bf16[1040,128]{1,0:T(8,128)(2,1)S(1)} %collective-permute-done.10.refs_1_, bf16[1,2048,768]{2,1,0:T(8,128)(2,1)S(1)} %get-tuple-element.57.refs_2_.refs_1_, ...), custom_call_target="tpu_custom_call" | custom-call | flops 2415919104 | bytes 20447232 | tf_op jit(solution)/shard_map/pallas_call | solution.py:113
  56.0 0.5 collective-permute-start.15
  56.5 1.6 %collective-permute-start.16 = (bf16[64,2048]{1,0:T(8,128)(2,1)S(1)}, bf16[64,2048]{1,0:T(8,128)(2,1)S(1)}, u32[]{:S(2)}, u32[]{:S(2)}) collective-permute-start(bf16[64,2048]{1,0:T(8,128)(2,1)S(1)} %get-tuple-element.91), channel_id=1, source_target_pairs={{0,8},{2,10},{8,16},{10,18},{16,24},{18,26},{24,28},{26,30},{28,20... | collective-permute-start | bytes 786440 | tf_op jit(solution)/shard_map/ppermute | solution.py:191
  58.1 0.8 collective-permute-done.21
  58.9 2.7 %collective-permute-done.22 = bf16[64,2048]{1,0:T(8,128)(2,1)S(1)} collective-permute-done((bf16[64,2048]{1,0:T(8,128)(2,1)S(1)}, bf16[64,2048]{1,0:T(8,128)(2,1)S(1)}, u32[]{:S(2)}, u32[]{:S(2)}) %collective-permute-start.22) | collective-permute-done | bytes 262176 | tf_op jit(solution)/shard_map/ppermute | solution.py:191
  61.6 0.1 add_convert_fusion.7
  61.7 1.5 %collective-permute-start.23 = (bf16[64,2048]{1,0:T(8,128)(2,1)S(1)}, bf16[64,2048]{1,0:T(8,128)(2,1)S(1)}, u32[]{:S(2)}, u32[]{:S(2)}) collective-permute-start(bf16[64,2048]{1,0:T(8,128)(2,1)S(1)} %add_convert_fusion.7), channel_id=1, source_target_pairs={{0,8},{2,10},{8,16},{10,18},{16,24},{18,26},{24,28},{26,30},{28,20... | collective-permute-start | bytes 786440 | tf_op jit(solution)/shard_map/ppermute | solution.py:191
  63.2 0.1 add_convert_fusion.6
  63.3 0.8 collective-permute-start.24
  64.1 3.1 %collective-permute-done.15 = bf16[64,2048]{1,0:T(8,128)(2,1)S(1)} collective-permute-done((bf16[64,2048]{1,0:T(8,128)(2,1)S(1)}, bf16[64,2048]{1,0:T(8,128)(2,1)S(1)}, u32[]{:S(2)}, u32[]{:S(2)}) %collective-permute-start.15) | collective-permute-done | bytes 262176 | tf_op jit(solution)/shard_map/ppermute | solution.py:191
  67.3 0.5 collective-permute-start.17
  67.9 1.6 %collective-permute-start.18 = (bf16[64,2048]{1,0:T(8,128)(2,1)S(1)}, bf16[64,2048]{1,0:T(8,128)(2,1)S(1)}, u32[]{:S(2)}, u32[]{:S(2)}) collective-permute-start(bf16[64,2048]{1,0:T(8,128)(2,1)S(1)} %add_convert_fusion.10), channel_id=1, source_target_pairs={{0,8},{2,10},{8,16},{10,18},{16,24},{18,26},{24,28},{26,30},{28,20... | collective-permute-start | bytes 786440 | tf_op jit(solution)/shard_map/ppermute | solution.py:191
  69.5 1.9 %collective-permute-done.23 = bf16[64,2048]{1,0:T(8,128)(2,1)S(1)} collective-permute-done((bf16[64,2048]{1,0:T(8,128)(2,1)S(1)}, bf16[64,2048]{1,0:T(8,128)(2,1)S(1)}, u32[]{:S(2)}, u32[]{:S(2)}) %collective-permute-start.23) | collective-permute-done | bytes 262176 | tf_op jit(solution)/shard_map/ppermute | solution.py:191
  71.4 1.5 %collective-permute-done.24 = bf16[64,2048]{1,0:T(8,128)(2,1)S(1)} collective-permute-done((bf16[64,2048]{1,0:T(8,128)(2,1)S(1)}, bf16[64,2048]{1,0:T(8,128)(2,1)S(1)}, u32[]{:S(2)}, u32[]{:S(2)}) %collective-permute-start.24) | collective-permute-done | bytes 262176 | tf_op jit(solution)/shard_map/ppermute | solution.py:191
  72.9 1.5 %collective-permute-start.25 = (bf16[64,2048]{1,0:T(8,128)(2,1)S(1)}, bf16[64,2048]{1,0:T(8,128)(2,1)S(1)}, u32[]{:S(2)}, u32[]{:S(2)}) collective-permute-start(bf16[64,2048]{1,0:T(8,128)(2,1)S(1)} %add_convert_fusion.5), channel_id=1, source_target_pairs={{0,8},{2,10},{8,16},{10,18},{16,24},{18,26},{24,28},{26,30},{28,20... | collective-permute-start | bytes 786440 | tf_op jit(solution)/shard_map/ppermute | solution.py:191
  74.5 0.6 collective-permute-start.26
  75.1 3.4 %collective-permute-done.17 = bf16[64,2048]{1,0:T(8,128)(2,1)S(1)} collective-permute-done((bf16[64,2048]{1,0:T(8,128)(2,1)S(1)}, bf16[64,2048]{1,0:T(8,128)(2,1)S(1)}, u32[]{:S(2)}, u32[]{:S(2)}) %collective-permute-start.17) | collective-permute-done | bytes 262176 | tf_op jit(solution)/shard_map/ppermute | solution.py:191
  78.5 0.1 add_convert_fusion.9
  78.6 0.5 collective-permute-start.19
  79.1 0.1 add_convert_fusion.8
  79.1 1.6 %collective-permute-start.20 = (bf16[64,2048]{1,0:T(8,128)(2,1)S(1)}, bf16[64,2048]{1,0:T(8,128)(2,1)S(1)}, u32[]{:S(2)}, u32[]{:S(2)}) collective-permute-start(bf16[64,2048]{1,0:T(8,128)(2,1)S(1)} %add_convert_fusion.8), channel_id=1, source_target_pairs={{0,8},{2,10},{8,16},{10,18},{16,24},{18,26},{24,28},{26,30},{28,20... | collective-permute-start | bytes 786440 | tf_op jit(solution)/shard_map/ppermute | solution.py:191
  80.7 2.9 %shard_map.82 = (f32[64,2048]{1,0:T(8,128)S(1)}, f32[64,2048]{1,0:T(8,128)S(1)}) custom-call(bf16[2080,128]{1,0:T(8,128)(2,1)S(1)} %shard_map.73.refs_0_, bf16[1,2048,768]{2,1,0:T(8,128)(2,1)S(1)} %get-tuple-element.57.refs_2_.refs_1_, bf16[1,2048,768]{2,1,0:T(8,128)(2,1)S(1)} %get-tuple-element.58.refs_3_.refs_2_, ...), custom_call_target="tpu_custom_call" | custom-call | flops 2415919104 | bytes 20447232 | tf_op jit(solution)/shard_map/pallas_call | solution.py:113
  83.7 2.7 %collective-permute-done.19 = bf16[64,2048]{1,0:T(8,128)(2,1)S(1)} collective-permute-done((bf16[64,2048]{1,0:T(8,128)(2,1)S(1)}, bf16[64,2048]{1,0:T(8,128)(2,1)S(1)}, u32[]{:S(2)}, u32[]{:S(2)}) %collective-permute-start.19) | collective-permute-done | bytes 262176 | tf_op jit(solution)/shard_map/ppermute | solution.py:191
  86.5 1.6 %collective-permute-start.28 = (bf16[64,2048]{1,0:T(8,128)(2,1)S(1)}, bf16[64,2048]{1,0:T(8,128)(2,1)S(1)}, u32[]{:S(2)}, u32[]{:S(2)}) collective-permute-start(bf16[64,2048]{1,0:T(8,128)(2,1)S(1)} %add_convert_fusion.1), channel_id=1, source_target_pairs={{0,8},{2,10},{8,16},{10,18},{16,24},{18,26},{24,28},{26,30},{28,20... | collective-permute-start | bytes 786440 | tf_op jit(solution)/shard_map/ppermute | solution.py:191
  88.2 0.5 collective-permute-start.27
  88.7 4.2 %collective-permute-done.28 = bf16[64,2048]{1,0:T(8,128)(2,1)S(1)} collective-permute-done((bf16[64,2048]{1,0:T(8,128)(2,1)S(1)}, bf16[64,2048]{1,0:T(8,128)(2,1)S(1)}, u32[]{:S(2)}, u32[]{:S(2)}) %collective-permute-start.28) | collective-permute-done | bytes 262176 | tf_op jit(solution)/shard_map/ppermute | solution.py:191
  92.9 0.1 add_convert_fusion
  93.0 1.6 %collective-permute-done.27 = bf16[64,2048]{1,0:T(8,128)(2,1)S(1)} collective-permute-done((bf16[64,2048]{1,0:T(8,128)(2,1)S(1)}, bf16[64,2048]{1,0:T(8,128)(2,1)S(1)}, u32[]{:S(2)}, u32[]{:S(2)}) %collective-permute-start.27) | collective-permute-done | bytes 262176 | tf_op jit(solution)/shard_map/ppermute | solution.py:191
  94.6 0.1 add_convert_fusion.2
  94.7 0.8 pad_maximum_fusion
  (28 shorter events, 0.5 us)
Async XLA Ops:
  0.0 19.8 %collective-permute-start.1 = (bf16[1,2048,768]{2,1,0:T(8,128)(2,1)}, bf16[1,2048,768]{2,1,0:T(8,128)(2,1)S(1)}, u32[]{:S(2)}, u32[]{:S(2)}) collective-permute-start(bf16[1,2048,768]{2,1,0:T(8,128)(2,1)} %refs_0_.1), channel_id=1, source_target_pairs={{0,2},{2,0},{4,6},{6,4},{8,10},{10,8},{12,14},{14,12},{16,18},{18,... | collective-permute-start | bytes 9437192 | tf_op jit(solution)/shard_map/ppermute | solution.py:147
  0.5 19.4 %collective-permute-start.2 = (bf16[1,2048,768]{2,1,0:T(8,128)(2,1)}, bf16[1,2048,768]{2,1,0:T(8,128)(2,1)S(1)}, u32[]{:S(2)}, u32[]{:S(2)}) collective-permute-start(bf16[1,2048,768]{2,1,0:T(8,128)(2,1)} %refs_1_.1), channel_id=1, source_target_pairs={{0,2},{2,0},{4,6},{6,4},{8,10},{10,8},{12,14},{14,12},{16,18},{18,... | collective-permute-start | bytes 9437192 | tf_op jit(solution)/shard_map/ppermute | solution.py:147
  0.5 19.3 %collective-permute-start.3 = (bf16[1,768,2048]{2,1,0:T(8,128)(2,1)}, bf16[1,768,2048]{2,1,0:T(8,128)(2,1)S(1)}, u32[]{:S(2)}, u32[]{:S(2)}) collective-permute-start(bf16[1,768,2048]{2,1,0:T(8,128)(2,1)} %refs_2_.1), channel_id=1, source_target_pairs={{0,2},{2,0},{4,6},{6,4},{8,10},{10,8},{12,14},{14,12},{16,18},{18,... | collective-permute-start | bytes 9437192 | tf_op jit(solution)/shard_map/ppermute | solution.py:147
  1.8 1.0 %copy-start.3 = (bf16[128,2048]{1,0:T(8,128)(2,1)S(1)}, bf16[128,2048]{1,0:T(8,128)(2,1)}, u32[]{:S(2)}) copy-start(bf16[128,2048]{1,0:T(8,128)(2,1)} %tokens_ref.1) | copy-start | bytes 1572868
  2.9 15.3 %collective-permute-start = (bf16[2080,128]{1,0:T(8,128)(2,1)S(1)}, bf16[2080,128]{1,0:T(8,128)(2,1)S(1)}, u32[]{:S(2)}, u32[]{:S(2)}) collective-permute-start(bf16[2080,128]{1,0:T(8,128)(2,1)S(1)} %shard_map.73.refs_0_), channel_id=1, source_target_pairs={{0,8},{2,10},{8,16},{10,18},{16,24},{18,26},{24,28},{26,30},{28,20... | collective-permute-start | bytes 1597448 | tf_op jit(solution)/shard_map/ppermute | solution.py:149
  5.5 14.2 %collective-permute-start.5 = (bf16[2080,128]{1,0:T(8,128)(2,1)S(1)}, bf16[2080,128]{1,0:T(8,128)(2,1)S(1)}, u32[]{:S(2)}, u32[]{:S(2)}) collective-permute-start(bf16[2080,128]{1,0:T(8,128)(2,1)S(1)} %shard_map.73.refs_0_), channel_id=1, source_target_pairs={{0,4},{2,6},{8,0},{10,2},{16,8},{18,10},{24,16},{26,18},{28,24},{3... | collective-permute-start | bytes 1597448 | tf_op jit(solution)/shard_map/ppermute | solution.py:149
  5.5 1.9 %copy-start = (bf16[1,2048,768]{2,1,0:T(8,128)(2,1)S(1)}, bf16[1,2048,768]{2,1,0:T(8,128)(2,1)}, u32[]{:S(2)}) copy-start(bf16[1,2048,768]{2,1,0:T(8,128)(2,1)} %refs_0_.1) | copy-start | bytes 9437188
  7.4 1.9 %copy-start.1 = (bf16[1,2048,768]{2,1,0:T(8,128)(2,1)S(1)}, bf16[1,2048,768]{2,1,0:T(8,128)(2,1)}, u32[]{:S(2)}) copy-start(bf16[1,2048,768]{2,1,0:T(8,128)(2,1)} %refs_1_.1) | copy-start | bytes 9437188
  9.3 1.9 %copy-start.2 = (bf16[1,768,2048]{2,1,0:T(8,128)(2,1)S(1)}, bf16[1,768,2048]{2,1,0:T(8,128)(2,1)}, u32[]{:S(2)}) copy-start(bf16[1,768,2048]{2,1,0:T(8,128)(2,1)} %refs_2_.1) | copy-start | bytes 9437188
  19.8 10.1 %collective-permute-start.4 = (bf16[1040,128]{1,0:T(8,128)(2,1)S(1)}, bf16[1040,128]{1,0:T(8,128)(2,1)S(1)}, u32[]{:S(2)}, u32[]{:S(2)}) collective-permute-start(bf16[1040,128]{1,0:T(8,128)(2,1)S(1)} %get-tuple-element.60.refs_0_), channel_id=1, source_target_pairs={{0,8},{2,10},{8,16},{10,18},{16,24},{18,26},{24,28},{26,30},{28,20... | collective-permute-start | bytes 798728 | tf_op jit(solution)/shard_map/ppermute | solution.py:163
  21.5 9.3 %collective-permute-start.7 = (bf16[1040,128]{1,0:T(8,128)(2,1)S(1)}, bf16[1040,128]{1,0:T(8,128)(2,1)S(1)}, u32[]{:S(2)}, u32[]{:S(2)}) collective-permute-start(bf16[1040,128]{1,0:T(8,128)(2,1)S(1)} %get-tuple-element.63.refs_1_), channel_id=1, source_target_pairs={{0,4},{2,6},{8,0},{10,2},{16,8},{18,10},{24,16},{26,18},{28,24},{3... | collective-permute-start | bytes 798728 | tf_op jit(solution)/shard_map/ppermute | solution.py:163
  24.9 11.6 %collective-permute-start.11 = (bf16[1040,128]{1,0:T(8,128)(2,1)S(1)}, bf16[1040,128]{1,0:T(8,128)(2,1)S(1)}, u32[]{:S(2)}, u32[]{:S(2)}) collective-permute-start(bf16[1040,128]{1,0:T(8,128)(2,1)S(1)} %get-tuple-element.73.refs_0_), channel_id=1, source_target_pairs={{0,4},{2,6},{8,0},{10,2},{16,8},{18,10},{24,16},{26,18},{28,24},{3... | collective-permute-start | bytes 798728 | tf_op jit(solution)/shard_map/ppermute | solution.py:163
  25.2 11.3 %collective-permute-start.13 = (bf16[1040,128]{1,0:T(8,128)(2,1)S(1)}, bf16[1040,128]{1,0:T(8,128)(2,1)S(1)}, u32[]{:S(2)}, u32[]{:S(2)}) collective-permute-start(bf16[1040,128]{1,0:T(8,128)(2,1)S(1)} %get-tuple-element.75.refs_1_), channel_id=1, source_target_pairs={{0,8},{2,10},{8,16},{10,18},{16,24},{18,26},{24,28},{26,30},{28,20... | collective-permute-start | bytes 798728 | tf_op jit(solution)/shard_map/ppermute | solution.py:163
  30.8 10.7 %collective-permute-start.6 = (bf16[1040,128]{1,0:T(8,128)(2,1)S(1)}, bf16[1040,128]{1,0:T(8,128)(2,1)S(1)}, u32[]{:S(2)}, u32[]{:S(2)}) collective-permute-start(bf16[1040,128]{1,0:T(8,128)(2,1)S(1)} %collective-permute-done.4.refs_0_), channel_id=1, source_target_pairs={{0,8},{2,10},{8,16},{10,18},{16,24},{18,26},{24,28},{26,30},{28,20... | collective-permute-start | bytes 798728 | tf_op jit(solution)/shard_map/ppermute | solution.py:163
  32.4 9.8 %collective-permute-start.9 = (bf16[1040,128]{1,0:T(8,128)(2,1)S(1)}, bf16[1040,128]{1,0:T(8,128)(2,1)S(1)}, u32[]{:S(2)}, u32[]{:S(2)}) collective-permute-start(bf16[1040,128]{1,0:T(8,128)(2,1)S(1)} %collective-permute-done.7.refs_1_), channel_id=1, source_target_pairs={{0,4},{2,6},{8,0},{10,2},{16,8},{18,10},{24,16},{26,18},{28,24},{3... | collective-permute-start | bytes 798728 | tf_op jit(solution)/shard_map/ppermute | solution.py:163
  36.5 11.4 %collective-permute-start.12 = (bf16[1040,128]{1,0:T(8,128)(2,1)S(1)}, bf16[1040,128]{1,0:T(8,128)(2,1)S(1)}, u32[]{:S(2)}, u32[]{:S(2)}) collective-permute-start(bf16[1040,128]{1,0:T(8,128)(2,1)S(1)} %collective-permute-done.11.refs_0_), channel_id=1, source_target_pairs={{0,4},{2,6},{8,0},{10,2},{16,8},{18,10},{24,16},{26,18},{28,24},{3... | collective-permute-start | bytes 798728 | tf_op jit(solution)/shard_map/ppermute | solution.py:163
  37.0 11.0 %collective-permute-start.14 = (bf16[1040,128]{1,0:T(8,128)(2,1)S(1)}, bf16[1040,128]{1,0:T(8,128)(2,1)S(1)}, u32[]{:S(2)}, u32[]{:S(2)}) collective-permute-start(bf16[1040,128]{1,0:T(8,128)(2,1)S(1)} %collective-permute-done.13.refs_1_), channel_id=1, source_target_pairs={{0,8},{2,10},{8,16},{10,18},{16,24},{18,26},{24,28},{26,30},{28,20... | collective-permute-start | bytes 798728 | tf_op jit(solution)/shard_map/ppermute | solution.py:163
  42.2 10.8 %collective-permute-start.8 = (bf16[1040,128]{1,0:T(8,128)(2,1)S(1)}, bf16[1040,128]{1,0:T(8,128)(2,1)S(1)}, u32[]{:S(2)}, u32[]{:S(2)}) collective-permute-start(bf16[1040,128]{1,0:T(8,128)(2,1)S(1)} %collective-permute-done.6.refs_0_), channel_id=1, source_target_pairs={{0,8},{2,10},{8,16},{10,18},{16,24},{18,26},{24,28},{26,30},{28,20... | collective-permute-start | bytes 798728 | tf_op jit(solution)/shard_map/ppermute | solution.py:163
  43.8 9.2 %collective-permute-start.10 = (bf16[1040,128]{1,0:T(8,128)(2,1)S(1)}, bf16[1040,128]{1,0:T(8,128)(2,1)S(1)}, u32[]{:S(2)}, u32[]{:S(2)}) collective-permute-start(bf16[1040,128]{1,0:T(8,128)(2,1)S(1)} %collective-permute-done.9.refs_1_), channel_id=1, source_target_pairs={{0,4},{2,6},{8,0},{10,2},{16,8},{18,10},{24,16},{26,18},{28,24},{3... | collective-permute-start | bytes 798728 | tf_op jit(solution)/shard_map/ppermute | solution.py:163
  50.9 8.0 %collective-permute-start.21 = (bf16[64,2048]{1,0:T(8,128)(2,1)S(1)}, bf16[64,2048]{1,0:T(8,128)(2,1)S(1)}, u32[]{:S(2)}, u32[]{:S(2)}) collective-permute-start(bf16[64,2048]{1,0:T(8,128)(2,1)S(1)} %get-tuple-element.85), channel_id=1, source_target_pairs={{0,8},{2,10},{8,16},{10,18},{16,24},{18,26},{24,28},{26,30},{28,20... | collective-permute-start | bytes 786440 | tf_op jit(solution)/shard_map/ppermute | solution.py:191
  52.5 9.1 %collective-permute-start.22 = (bf16[64,2048]{1,0:T(8,128)(2,1)S(1)}, bf16[64,2048]{1,0:T(8,128)(2,1)S(1)}, u32[]{:S(2)}, u32[]{:S(2)}) collective-permute-start(bf16[64,2048]{1,0:T(8,128)(2,1)S(1)} %get-tuple-element.98), channel_id=1, source_target_pairs={{0,4},{2,6},{8,0},{10,2},{16,8},{18,10},{24,16},{26,18},{28,24},{3... | collective-permute-start | bytes 786440 | tf_op jit(solution)/shard_map/ppermute | solution.py:191
  56.0 11.3 %collective-permute-start.15 = (bf16[64,2048]{1,0:T(8,128)(2,1)S(1)}, bf16[64,2048]{1,0:T(8,128)(2,1)S(1)}, u32[]{:S(2)}, u32[]{:S(2)}) collective-permute-start(bf16[64,2048]{1,0:T(8,128)(2,1)S(1)} %get-tuple-element.88), channel_id=1, source_target_pairs={{0,4},{2,6},{8,0},{10,2},{16,8},{18,10},{24,16},{26,18},{28,24},{3... | collective-permute-start | bytes 786440 | tf_op jit(solution)/shard_map/ppermute | solution.py:191
  56.5 10.8 %collective-permute-start.16 = (bf16[64,2048]{1,0:T(8,128)(2,1)S(1)}, bf16[64,2048]{1,0:T(8,128)(2,1)S(1)}, u32[]{:S(2)}, u32[]{:S(2)}) collective-permute-start(bf16[64,2048]{1,0:T(8,128)(2,1)S(1)} %get-tuple-element.91), channel_id=1, source_target_pairs={{0,8},{2,10},{8,16},{10,18},{16,24},{18,26},{24,28},{26,30},{28,20... | collective-permute-start | bytes 786440 | tf_op jit(solution)/shard_map/ppermute | solution.py:191
  61.7 9.7 %collective-permute-start.23 = (bf16[64,2048]{1,0:T(8,128)(2,1)S(1)}, bf16[64,2048]{1,0:T(8,128)(2,1)S(1)}, u32[]{:S(2)}, u32[]{:S(2)}) collective-permute-start(bf16[64,2048]{1,0:T(8,128)(2,1)S(1)} %add_convert_fusion.7), channel_id=1, source_target_pairs={{0,8},{2,10},{8,16},{10,18},{16,24},{18,26},{24,28},{26,30},{28,20... | collective-permute-start | bytes 786440 | tf_op jit(solution)/shard_map/ppermute | solution.py:191
  63.3 9.6 %collective-permute-start.24 = (bf16[64,2048]{1,0:T(8,128)(2,1)S(1)}, bf16[64,2048]{1,0:T(8,128)(2,1)S(1)}, u32[]{:S(2)}, u32[]{:S(2)}) collective-permute-start(bf16[64,2048]{1,0:T(8,128)(2,1)S(1)} %add_convert_fusion.6), channel_id=1, source_target_pairs={{0,4},{2,6},{8,0},{10,2},{16,8},{18,10},{24,16},{26,18},{28,24},{3... | collective-permute-start | bytes 786440 | tf_op jit(solution)/shard_map/ppermute | solution.py:191
  67.3 11.2 %collective-permute-start.17 = (bf16[64,2048]{1,0:T(8,128)(2,1)S(1)}, bf16[64,2048]{1,0:T(8,128)(2,1)S(1)}, u32[]{:S(2)}, u32[]{:S(2)}) collective-permute-start(bf16[64,2048]{1,0:T(8,128)(2,1)S(1)} %add_convert_fusion.11), channel_id=1, source_target_pairs={{0,4},{2,6},{8,0},{10,2},{16,8},{18,10},{24,16},{26,18},{28,24},{3... | collective-permute-start | bytes 786440 | tf_op jit(solution)/shard_map/ppermute | solution.py:191
  67.9 10.6 %collective-permute-start.18 = (bf16[64,2048]{1,0:T(8,128)(2,1)S(1)}, bf16[64,2048]{1,0:T(8,128)(2,1)S(1)}, u32[]{:S(2)}, u32[]{:S(2)}) collective-permute-start(bf16[64,2048]{1,0:T(8,128)(2,1)S(1)} %add_convert_fusion.10), channel_id=1, source_target_pairs={{0,8},{2,10},{8,16},{10,18},{16,24},{18,26},{24,28},{26,30},{28,20... | collective-permute-start | bytes 786440 | tf_op jit(solution)/shard_map/ppermute | solution.py:191
  72.9 10.8 %collective-permute-start.25 = (bf16[64,2048]{1,0:T(8,128)(2,1)S(1)}, bf16[64,2048]{1,0:T(8,128)(2,1)S(1)}, u32[]{:S(2)}, u32[]{:S(2)}) collective-permute-start(bf16[64,2048]{1,0:T(8,128)(2,1)S(1)} %add_convert_fusion.5), channel_id=1, source_target_pairs={{0,8},{2,10},{8,16},{10,18},{16,24},{18,26},{24,28},{26,30},{28,20... | collective-permute-start | bytes 786440 | tf_op jit(solution)/shard_map/ppermute | solution.py:191
  74.5 9.2 %collective-permute-start.26 = (bf16[64,2048]{1,0:T(8,128)(2,1)S(1)}, bf16[64,2048]{1,0:T(8,128)(2,1)S(1)}, u32[]{:S(2)}, u32[]{:S(2)}) collective-permute-start(bf16[64,2048]{1,0:T(8,128)(2,1)S(1)} %add_convert_fusion.4), channel_id=1, source_target_pairs={{0,4},{2,6},{8,0},{10,2},{16,8},{18,10},{24,16},{26,18},{28,24},{3... | collective-permute-start | bytes 786440 | tf_op jit(solution)/shard_map/ppermute | solution.py:191
  78.6 7.9 %collective-permute-start.19 = (bf16[64,2048]{1,0:T(8,128)(2,1)S(1)}, bf16[64,2048]{1,0:T(8,128)(2,1)S(1)}, u32[]{:S(2)}, u32[]{:S(2)}) collective-permute-start(bf16[64,2048]{1,0:T(8,128)(2,1)S(1)} %add_convert_fusion.9), channel_id=1, source_target_pairs={{0,4},{2,6},{8,0},{10,2},{16,8},{18,10},{24,16},{26,18},{28,24},{3... | collective-permute-start | bytes 786440 | tf_op jit(solution)/shard_map/ppermute | solution.py:191
  79.1 7.3 %collective-permute-start.20 = (bf16[64,2048]{1,0:T(8,128)(2,1)S(1)}, bf16[64,2048]{1,0:T(8,128)(2,1)S(1)}, u32[]{:S(2)}, u32[]{:S(2)}) collective-permute-start(bf16[64,2048]{1,0:T(8,128)(2,1)S(1)} %add_convert_fusion.8), channel_id=1, source_target_pairs={{0,8},{2,10},{8,16},{10,18},{16,24},{18,26},{24,28},{26,30},{28,20... | collective-permute-start | bytes 786440 | tf_op jit(solution)/shard_map/ppermute | solution.py:191
  86.5 6.4 %collective-permute-start.28 = (bf16[64,2048]{1,0:T(8,128)(2,1)S(1)}, bf16[64,2048]{1,0:T(8,128)(2,1)S(1)}, u32[]{:S(2)}, u32[]{:S(2)}) collective-permute-start(bf16[64,2048]{1,0:T(8,128)(2,1)S(1)} %add_convert_fusion.1), channel_id=1, source_target_pairs={{0,8},{2,10},{8,16},{10,18},{16,24},{18,26},{24,28},{26,30},{28,20... | collective-permute-start | bytes 786440 | tf_op jit(solution)/shard_map/ppermute | solution.py:191
  88.2 6.4 %collective-permute-start.27 = (bf16[64,2048]{1,0:T(8,128)(2,1)S(1)}, bf16[64,2048]{1,0:T(8,128)(2,1)S(1)}, u32[]{:S(2)}, u32[]{:S(2)}) collective-permute-start(bf16[64,2048]{1,0:T(8,128)(2,1)S(1)} %add_convert_fusion.3), channel_id=1, source_target_pairs={{0,4},{2,6},{8,0},{10,2},{16,8},{18,10},{24,16},{26,18},{28,24},{3... | collective-permute-start | bytes 786440 | tf_op jit(solution)/shard_map/ppermute | solution.py:191

commit v5 on v4

--- a/solution.py
+++ b/solution.py
@@ -66,6 +66,27 @@
             flops=0, bytes_accessed=sum(a.size * a.dtype.itemsize for a in arrays), transcendentals=0
         ),
     )(*arrays)
+
+
+def split_kernel(*refs):
+    n = len(refs) // 3
+    for i, block_ref in enumerate(refs[:n]):
+        size = block_ref.shape[0] // 2
+        for h in range(2):
+            refs[n + 2 * i + h][...] = block_ref[pl.ds(h * size, size), :]
+
+
+def split(blocks, flops):
+    size, width = blocks[0].shape[0] // 2, blocks[0].shape[1]
+    near = pl.BlockSpec(memory_space=pltpu.VMEM)
+    return pl.pallas_call(
+        split_kernel,
+        in_specs=[near] * len(blocks),
+        out_specs=[near] * (2 * len(blocks)),
+        out_shape=[jax.ShapeDtypeStruct((size, width), jnp.bfloat16)] * (2 * len(blocks)),
+        compiler_params=pltpu.CompilerParams(vmem_limit_bytes=6 * 2**20),
+        cost_estimate=pl.CostEstimate(flops=flops, bytes_accessed=2**20, transcendentals=0),
+    )(*blocks)
 
 
 def ffn_kernel(n_in, n_out, n_dev, *refs):
@@ -148,7 +169,7 @@
     packed = pack(tokens, expert_ids, gate_scores, partner)
     first = [lax.ppermute(packed, "ep", perm[d]) for d in range(2)]
     own = load(own)
-    held = {(d, h, 1): part for d, block in enumerate(first) for h, part in enumerate(jnp.split(block, 2))}
+    held = dict(zip([(d, h, 1) for d in range(2) for h in range(2)], split(first, 3 * 10**10)))
     last = {(d, h): far if d == h else far - 1 for d in range(2) for h in range(2)}
     done = {}
 
@@ -168,7 +189,7 @@
         return [(d, h, s) for d, h in groups[g] if s <= last[d, h]]
 
     for g in range(2):
-        send(flows(g, 2), *other, *own)
+        send(flows(g, 2), *(other if g else other[:2]), *own)
     worked = []
     for s in range(1, far):
         for g in range(2):

time: 95.8 us -> 93.9 us (0.980)
  waiting for transfers between devices: 32.9 us -> 30.7 us
    ppermute x2, waiting for transfers between devices: 7.85 us -> 6.7 us  [on_device(): first = [lax.ppermute(packed, 'ep', perm[d]) for d in range(2)]]
  transfers between devices with their start and end apart: 29 -> 29, of which waited for: 15 -> 16; matrix products, arithmetic and copies ran while one was open for 2% -> 1% of each run, Pallas kernels for 26% -> 26%
where the time goes in v5:
time: 93.9 us; the launch traced here: 93.6 us
  waiting for transfers between devices  30.7 us (33%)
  starting transfers between devices  29.1 us (31%)
  Pallas kernels  24.5 us (26%)
  local copies, waits for them, and re-layouts  6.7 us (7%)
  other arithmetic  2.36 us (3%)
    pallas_call x8, Pallas kernels, ffn(): pl.pallas_call(functools.partial(ffn_kernel, n_in, n_out, n_dev), in_spec...  23.7 us
    ppermute x14, waiting for transfers between devices, give(): back[d, h] = lax.ppermute(part, 'ep', perm[1 - d])  21.7 us
    ppermute x14, starting transfers between devices, give(): back[d, h] = lax.ppermute(part, 'ep', perm[1 - d])  15.2 us
    ppermute x10, starting transfers between devices, send(): held[d, h, s] = lax.ppermute(tie(held[d, h, s - 1], *deps), 'ep', perm[d])  10.3 us
    ppermute x2, waiting for transfers between devices, on_device(): first = [lax.ppermute(packed, 'ep', perm[d]) for d in range(2)]  6.7 us
    unnamed x8, local copies, waits for them, and re-layouts  6.7 us
    ppermute x2, starting transfers between devices, on_device(): first = [lax.ppermute(packed, 'ep', perm[d]) for d in range(2)]  3.08 us
    ppermute x10, waiting for transfers between devices, send(): held[d, h, s] = lax.ppermute(tie(held[d, h, s - 1], *deps), 'ep', perm[d])  2.3 us
  transfers between devices with their start and end apart: 29, of which 16 were waited for; matrix products, arithmetic and copies ran while one was open for 1% of the time, Pallas kernels for 26%

profile of v5, /device:TPU:0, one launch (start us, length us, event | category | flops | bytes accessed | tf_op | source)
XLA Modules:
  0.0 93.6 jit_solution(835638463972992681)
XLA Ops:
  0.0 0.8 select_reduce_fusion.scores_ref
  0.8 1.0 %copy-done.3 = bf16[128,2048]{1,0:T(8,128)(2,1)S(1)} copy-done((bf16[128,2048]{1,0:T(8,128)(2,1)S(1)}, bf16[128,2048]{1,0:T(8,128)(2,1)}, u32[]{:S(2)}) %copy-start.3) | copy-done | bytes 524312
  1.8 0.1 shard_map.73.refs_0_
  1.9 3.1 %collective-permute-start = (bf16[2080,128]{1,0:T(8,128)(2,1)S(1)}, bf16[2080,128]{1,0:T(8,128)(2,1)S(1)}, u32[]{:S(2)}, u32[]{:S(2)}) collective-permute-start(bf16[2080,128]{1,0:T(8,128)(2,1)S(1)} %shard_map.73.refs_0_), channel_id=1, source_target_pairs={{0,8},{2,10},{8,16},{10,18},{16,24},{18,26},{24,28},{26,30},{28,20... | collective-permute-start | bytes 1597448 | tf_op jit(solution)/shard_map/ppermute | solution.py:170
  5.0 0.5 collective-permute-start.3
  5.5 1.9 %copy-done = bf16[1,2048,768]{2,1,0:T(8,128)(2,1)S(1)} copy-done((bf16[1,2048,768]{2,1,0:T(8,128)(2,1)S(1)}, bf16[1,2048,768]{2,1,0:T(8,128)(2,1)}, u32[]{:S(2)}) %copy-start) | copy-done | bytes 3145752
  7.4 1.9 %copy-done.1 = bf16[1,2048,768]{2,1,0:T(8,128)(2,1)S(1)} copy-done((bf16[1,2048,768]{2,1,0:T(8,128)(2,1)S(1)}, bf16[1,2048,768]{2,1,0:T(8,128)(2,1)}, u32[]{:S(2)}) %copy-start.1) | copy-done | bytes 3145752
  9.3 1.9 %copy-done.2 = bf16[1,768,2048]{2,1,0:T(8,128)(2,1)S(1)} copy-done((bf16[1,768,2048]{2,1,0:T(8,128)(2,1)S(1)}, bf16[1,768,2048]{2,1,0:T(8,128)(2,1)}, u32[]{:S(2)}) %copy-start.2) | copy-done | bytes 3145752
  11.2 0.7 shard_map.75
  11.9 5.2 %collective-permute-done.refs_0_ = bf16[2080,128]{1,0:T(8,128)(2,1)S(1)} collective-permute-done((bf16[2080,128]{1,0:T(8,128)(2,1)S(1)}, bf16[2080,128]{1,0:T(8,128)(2,1)S(1)}, u32[]{:S(2)}, u32[]{:S(2)}) %collective-permute-start) | collective-permute-done | bytes 532512 | tf_op jit(solution)/shard_map/ppermute | solution.py:170
  17.0 1.5 %collective-permute-done.1.refs_1_ = bf16[2080,128]{1,0:T(8,128)(2,1)S(1)} collective-permute-done((bf16[2080,128]{1,0:T(8,128)(2,1)S(1)}, bf16[2080,128]{1,0:T(8,128)(2,1)S(1)}, u32[]{:S(2)}, u32[]{:S(2)}) %collective-permute-start.1) | collective-permute-done | bytes 532512 | tf_op jit(solution)/shard_map/ppermute | solution.py:170
  18.6 0.1 shard_map.74
  18.7 1.6 %collective-permute-start.4 = (bf16[1040,128]{1,0:T(8,128)(2,1)S(1)}, bf16[1040,128]{1,0:T(8,128)(2,1)S(1)}, u32[]{:S(2)}, u32[]{:S(2)}) collective-permute-start(bf16[1040,128]{1,0:T(8,128)(2,1)S(1)} %get-tuple-element.65.refs_0_), channel_id=1, source_target_pairs={{0,8},{2,10},{8,16},{10,18},{16,24},{18,26},{24,28},{26,30},{28,20... | collective-permute-start | bytes 798728 | tf_op jit(solution)/shard_map/ppermute | solution.py:184
  20.3 0.4 collective-permute-start.7
  20.8 3.0 %shard_map.76 = (f32[64,2048]{1,0:T(8,128)S(1)}, f32[64,2048]{1,0:T(8,128)S(1)}) custom-call(bf16[1040,128]{1,0:T(8,128)(2,1)S(1)} %get-tuple-element.65.refs_0_, bf16[1040,128]{1,0:T(8,128)(2,1)S(1)} %get-tuple-element.69.refs_1_, bf16[1,2048,768]{2,1,0:T(8,128)(2,1)S(1)} %get-tuple-element.62.refs_2_.refs_1_, ...), custom_call_target="tpu_custom_call" | custom-call | flops 2415919104 | bytes 20447232 | tf_op jit(solution)/shard_map/pallas_call | solution.py:134
  23.7 1.1 %collective-permute-start.11 = (bf16[1040,128]{1,0:T(8,128)(2,1)S(1)}, bf16[1040,128]{1,0:T(8,128)(2,1)S(1)}, u32[]{:S(2)}, u32[]{:S(2)}) collective-permute-start(bf16[1040,128]{1,0:T(8,128)(2,1)S(1)} %get-tuple-element.81.refs_0_), channel_id=1, source_target_pairs={{0,4},{2,6},{8,0},{10,2},{16,8},{18,10},{24,16},{26,18},{28,24},{3... | collective-permute-start | bytes 798728 | tf_op jit(solution)/shard_map/ppermute | solution.py:184
  24.9 0.9 %collective-permute-start.13 = (bf16[1040,128]{1,0:T(8,128)(2,1)S(1)}, bf16[1040,128]{1,0:T(8,128)(2,1)S(1)}, u32[]{:S(2)}, u32[]{:S(2)}) collective-permute-start(bf16[1040,128]{1,0:T(8,128)(2,1)S(1)} %get-tuple-element.83.refs_1_), channel_id=1, source_target_pairs={{0,8},{2,10},{8,16},{10,18},{16,24},{18,26},{24,28},{26,30},{28,20... | collective-permute-start | bytes 798728 | tf_op jit(solution)/shard_map/ppermute | solution.py:184
  25.8 2.9 %shard_map.77 = (f32[64,2048]{1,0:T(8,128)S(1)}, f32[64,2048]{1,0:T(8,128)S(1)}) custom-call(bf16[1040,128]{1,0:T(8,128)(2,1)S(1)} %get-tuple-element.81.refs_0_, bf16[1040,128]{1,0:T(8,128)(2,1)S(1)} %get-tuple-element.83.refs_1_, bf16[1,2048,768]{2,1,0:T(8,128)(2,1)S(1)} %get-tuple-element.62.refs_2_.refs_1_, ...), custom_call_target="tpu_custom_call" | custom-call | flops 2415919104 | bytes 20447232 | tf_op jit(solution)/shard_map/pallas_call | solution.py:134
  28.8 1.6 %collective-permute-start.6 = (bf16[1040,128]{1,0:T(8,128)(2,1)S(1)}, bf16[1040,128]{1,0:T(8,128)(2,1)S(1)}, u32[]{:S(2)}, u32[]{:S(2)}) collective-permute-start(bf16[1040,128]{1,0:T(8,128)(2,1)S(1)} %collective-permute-done.4.refs_0_), channel_id=1, source_target_pairs={{0,8},{2,10},{8,16},{10,18},{16,24},{18,26},{24,28},{26,30},{28,20... | collective-permute-start | bytes 798728 | tf_op jit(solution)/shard_map/ppermute | solution.py:184
  30.4 0.4 collective-permute-start.9
  30.9 3.0 %shard_map.78 = (f32[64,2048]{1,0:T(8,128)S(1)}, f32[64,2048]{1,0:T(8,128)S(1)}) custom-call(bf16[1040,128]{1,0:T(8,128)(2,1)S(1)} %collective-permute-done.4.refs_0_, bf16[1040,128]{1,0:T(8,128)(2,1)S(1)} %collective-permute-done.7.refs_1_, bf16[1,2048,768]{2,1,0:T(8,128)(2,1)S(1)} %get-tuple-element.62.refs_2_.refs_1_, ...), custom_call_target="tpu_custom_call" | custom-call | flops 2415919104 | bytes 20447232 | tf_op jit(solution)/shard_map/pallas_call | solution.py:134
  33.8 0.3 collective-permute-done.13.refs_1_
  34.1 1.6 %collective-permute-start.12 = (bf16[1040,128]{1,0:T(8,128)(2,1)S(1)}, bf16[1040,128]{1,0:T(8,128)(2,1)S(1)}, u32[]{:S(2)}, u32[]{:S(2)}) collective-permute-start(bf16[1040,128]{1,0:T(8,128)(2,1)S(1)} %collective-permute-done.11.refs_0_), channel_id=1, source_target_pairs={{0,4},{2,6},{8,0},{10,2},{16,8},{18,10},{24,16},{26,18},{28,24},{3... | collective-permute-start | bytes 798728 | tf_op jit(solution)/shard_map/ppermute | solution.py:184
  35.7 0.5 collective-permute-start.14
  36.2 2.9 %shard_map.79 = (f32[64,2048]{1,0:T(8,128)S(1)}, f32[64,2048]{1,0:T(8,128)S(1)}) custom-call(bf16[1040,128]{1,0:T(8,128)(2,1)S(1)} %collective-permute-done.11.refs_0_, bf16[1040,128]{1,0:T(8,128)(2,1)S(1)} %collective-permute-done.13.refs_1_, bf16[1,2048,768]{2,1,0:T(8,128)(2,1)S(1)} %get-tuple-element.62.refs_2_.refs_1_, ...), custom_call_target="tpu_custom_call" | custom-call | flops 2415919104 | bytes 20447232 | tf_op jit(solution)/shard_map/pallas_call | solution.py:134
  39.1 0.7 collective-permute-done.6.refs_0_
  39.8 1.5 %collective-permute-start.8 = (bf16[1040,128]{1,0:T(8,128)(2,1)S(1)}, bf16[1040,128]{1,0:T(8,128)(2,1)S(1)}, u32[]{:S(2)}, u32[]{:S(2)}) collective-permute-start(bf16[1040,128]{1,0:T(8,128)(2,1)S(1)} %collective-permute-done.6.refs_0_), channel_id=1, source_target_pairs={{0,8},{2,10},{8,16},{10,18},{16,24},{18,26},{24,28},{26,30},{28,20... | collective-permute-start | bytes 798728 | tf_op jit(solution)/shard_map/ppermute | solution.py:184
  41.3 0.5 collective-permute-start.10
  41.9 2.9 %shard_map.80 = (f32[64,2048]{1,0:T(8,128)S(1)}, f32[64,2048]{1,0:T(8,128)S(1)}) custom-call(bf16[1040,128]{1,0:T(8,128)(2,1)S(1)} %collective-permute-done.6.refs_0_, bf16[1040,128]{1,0:T(8,128)(2,1)S(1)} %collective-permute-done.9.refs_1_, bf16[1,2048,768]{2,1,0:T(8,128)(2,1)S(1)} %get-tuple-element.62.refs_2_.refs_1_, ...), custom_call_target="tpu_custom_call" | custom-call | flops 2415919104 | bytes 20447232 | tf_op jit(solution)/shard_map/pallas_call | solution.py:134
  44.8 0.6 collective-permute-done.12.refs_0_
  45.4 0.1 collective-permute-done.14.refs_1_
  45.5 3.0 %shard_map.81 = (bf16[64,2048]{1,0:T(8,128)(2,1)S(1)}, bf16[64,2048]{1,0:T(8,128)(2,1)S(1)}) custom-call(bf16[1040,128]{1,0:T(8,128)(2,1)S(1)} %collective-permute-done.12.refs_0_, bf16[1040,128]{1,0:T(8,128)(2,1)S(1)} %collective-permute-done.14.refs_1_, bf16[1,2048,768]{2,1,0:T(8,128)(2,1)S(1)} %get-tuple-element.62.refs_2_.refs_1_, ...), custom_call_target="tpu_custom_call" | custom-call | flops 2415919104 | bytes 20447232 | tf_op jit(solution)/shard_map/pallas_call | solution.py:134
  48.5 1.5 %collective-permute-start.21 = (bf16[64,2048]{1,0:T(8,128)(2,1)S(1)}, bf16[64,2048]{1,0:T(8,128)(2,1)S(1)}, u32[]{:S(2)}, u32[]{:S(2)}) collective-permute-start(bf16[64,2048]{1,0:T(8,128)(2,1)S(1)} %get-tuple-element.93), channel_id=1, source_target_pairs={{0,8},{2,10},{8,16},{10,18},{16,24},{18,26},{24,28},{26,30},{28,20... | collective-permute-start | bytes 786440 | tf_op jit(solution)/shard_map/ppermute | solution.py:212
  50.1 0.5 collective-permute-start.22
  50.6 0.5 collective-permute-done.8.refs_0_
  51.2 3.0 %shard_map.82 = (bf16[64,2048]{1,0:T(8,128)(2,1)S(1)}, bf16[64,2048]{1,0:T(8,128)(2,1)S(1)}) custom-call(bf16[1040,128]{1,0:T(8,128)(2,1)S(1)} %collective-permute-done.8.refs_0_, bf16[1040,128]{1,0:T(8,128)(2,1)S(1)} %collective-permute-done.10.refs_1_, bf16[1,2048,768]{2,1,0:T(8,128)(2,1)S(1)} %get-tuple-element.62.refs_2_.refs_1_, ...), custom_call_target="tpu_custom_call" | custom-call | flops 2415919104 | bytes 20447232 | tf_op jit(solution)/shard_map/pallas_call | solution.py:134
  54.1 1.6 %collective-permute-start.15 = (bf16[64,2048]{1,0:T(8,128)(2,1)S(1)}, bf16[64,2048]{1,0:T(8,128)(2,1)S(1)}, u32[]{:S(2)}, u32[]{:S(2)}) collective-permute-start(bf16[64,2048]{1,0:T(8,128)(2,1)S(1)} %get-tuple-element.96), channel_id=1, source_target_pairs={{0,4},{2,6},{8,0},{10,2},{16,8},{18,10},{24,16},{26,18},{28,24},{3... | collective-permute-start | bytes 786440 | tf_op jit(solution)/shard_map/ppermute | solution.py:212
  55.8 0.5 collective-permute-start.16
  56.2 1.9 %collective-permute-done.22 = bf16[64,2048]{1,0:T(8,128)(2,1)S(1)} collective-permute-done((bf16[64,2048]{1,0:T(8,128)(2,1)S(1)}, bf16[64,2048]{1,0:T(8,128)(2,1)S(1)}, u32[]{:S(2)}, u32[]{:S(2)}) %collective-permute-start.22) | collective-permute-done | bytes 262176 | tf_op jit(solution)/shard_map/ppermute | solution.py:212
  58.1 0.1 add_convert_fusion.7
  58.2 2.1 %collective-permute-start.23 = (bf16[64,2048]{1,0:T(8,128)(2,1)S(1)}, bf16[64,2048]{1,0:T(8,128)(2,1)S(1)}, u32[]{:S(2)}, u32[]{:S(2)}) collective-permute-start(bf16[64,2048]{1,0:T(8,128)(2,1)S(1)} %add_convert_fusion.7), channel_id=1, source_target_pairs={{0,8},{2,10},{8,16},{10,18},{16,24},{18,26},{24,28},{26,30},{28,20... | collective-permute-start | bytes 786440 | tf_op jit(solution)/shard_map/ppermute | solution.py:212
  60.3 0.1 add_convert_fusion.6
  60.4 0.3 collective-permute-start.24
  60.7 3.1 %collective-permute-done.15 = bf16[64,2048]{1,0:T(8,128)(2,1)S(1)} collective-permute-done((bf16[64,2048]{1,0:T(8,128)(2,1)S(1)}, bf16[64,2048]{1,0:T(8,128)(2,1)S(1)}, u32[]{:S(2)}, u32[]{:S(2)}) %collective-permute-start.15) | collective-permute-done | bytes 262176 | tf_op jit(solution)/shard_map/ppermute | solution.py:212
  63.8 1.2 %collective-permute-done.16 = bf16[64,2048]{1,0:T(8,128)(2,1)S(1)} collective-permute-done((bf16[64,2048]{1,0:T(8,128)(2,1)S(1)}, bf16[64,2048]{1,0:T(8,128)(2,1)S(1)}, u32[]{:S(2)}, u32[]{:S(2)}) %collective-permute-start.16) | collective-permute-done | bytes 262176 | tf_op jit(solution)/shard_map/ppermute | solution.py:212
  65.0 0.1 add_convert_fusion.11
  65.1 1.6 %collective-permute-start.17 = (bf16[64,2048]{1,0:T(8,128)(2,1)S(1)}, bf16[64,2048]{1,0:T(8,128)(2,1)S(1)}, u32[]{:S(2)}, u32[]{:S(2)}) collective-permute-start(bf16[64,2048]{1,0:T(8,128)(2,1)S(1)} %add_convert_fusion.11), channel_id=1, source_target_pairs={{0,4},{2,6},{8,0},{10,2},{16,8},{18,10},{24,16},{26,18},{28,24},{3... | collective-permute-start | bytes 786440 | tf_op jit(solution)/shard_map/ppermute | solution.py:212
  66.8 0.5 collective-permute-start.18
  67.3 3.4 %collective-permute-done.23 = bf16[64,2048]{1,0:T(8,128)(2,1)S(1)} collective-permute-done((bf16[64,2048]{1,0:T(8,128)(2,1)S(1)}, bf16[64,2048]{1,0:T(8,128)(2,1)S(1)}, u32[]{:S(2)}, u32[]{:S(2)}) %collective-permute-start.23) | collective-permute-done | bytes 262176 | tf_op jit(solution)/shard_map/ppermute | solution.py:212
  70.7 0.9 collective-permute-start.25
  71.6 1.3 %collective-permute-start.26 = (bf16[64,2048]{1,0:T(8,128)(2,1)S(1)}, bf16[64,2048]{1,0:T(8,128)(2,1)S(1)}, u32[]{:S(2)}, u32[]{:S(2)}) collective-permute-start(bf16[64,2048]{1,0:T(8,128)(2,1)S(1)} %add_convert_fusion.4), channel_id=1, source_target_pairs={{0,4},{2,6},{8,0},{10,2},{16,8},{18,10},{24,16},{26,18},{28,24},{3... | collective-permute-start | bytes 786440 | tf_op jit(solution)/shard_map/ppermute | solution.py:212
  72.9 2.7 %collective-permute-done.17 = bf16[64,2048]{1,0:T(8,128)(2,1)S(1)} collective-permute-done((bf16[64,2048]{1,0:T(8,128)(2,1)S(1)}, bf16[64,2048]{1,0:T(8,128)(2,1)S(1)}, u32[]{:S(2)}, u32[]{:S(2)}) %collective-permute-start.17) | collective-permute-done | bytes 262176 | tf_op jit(solution)/shard_map/ppermute | solution.py:212
  75.5 0.7 collective-permute-done.18
  76.3 1.6 %collective-permute-start.19 = (bf16[64,2048]{1,0:T(8,128)(2,1)S(1)}, bf16[64,2048]{1,0:T(8,128)(2,1)S(1)}, u32[]{:S(2)}, u32[]{:S(2)}) collective-permute-start(bf16[64,2048]{1,0:T(8,128)(2,1)S(1)} %add_convert_fusion.9), channel_id=1, source_target_pairs={{0,4},{2,6},{8,0},{10,2},{16,8},{18,10},{24,16},{26,18},{28,24},{3... | collective-permute-start | bytes 786440 | tf_op jit(solution)/shard_map/ppermute | solution.py:212
  78.0 0.5 collective-permute-start.20
  78.5 3.0 %shard_map.83 = (f32[64,2048]{1,0:T(8,128)S(1)}, f32[64,2048]{1,0:T(8,128)S(1)}) custom-call(bf16[2080,128]{1,0:T(8,128)(2,1)S(1)} %shard_map.73.refs_0_, bf16[1,2048,768]{2,1,0:T(8,128)(2,1)S(1)} %get-tuple-element.62.refs_2_.refs_1_, bf16[1,2048,768]{2,1,0:T(8,128)(2,1)S(1)} %get-tuple-element.63.refs_3_.refs_2_, ...), custom_call_target="tpu_custom_call" | custom-call | flops 2415919104 | bytes 20447232 | tf_op jit(solution)/shard_map/pallas_call | solution.py:134
  81.5 3.1 %collective-permute-done.19 = bf16[64,2048]{1,0:T(8,128)(2,1)S(1)} collective-permute-done((bf16[64,2048]{1,0:T(8,128)(2,1)S(1)}, bf16[64,2048]{1,0:T(8,128)(2,1)S(1)}, u32[]{:S(2)}, u32[]{:S(2)}) %collective-permute-start.19) | collective-permute-done | bytes 262176 | tf_op jit(solution)/shard_map/ppermute | solution.py:212
  84.6 1.5 %collective-permute-start.28 = (bf16[64,2048]{1,0:T(8,128)(2,1)S(1)}, bf16[64,2048]{1,0:T(8,128)(2,1)S(1)}, u32[]{:S(2)}, u32[]{:S(2)}) collective-permute-start(bf16[64,2048]{1,0:T(8,128)(2,1)S(1)} %add_convert_fusion.1), channel_id=1, source_target_pairs={{0,8},{2,10},{8,16},{10,18},{16,24},{18,26},{24,28},{26,30},{28,20... | collective-permute-start | bytes 786440 | tf_op jit(solution)/shard_map/ppermute | solution.py:212
  86.2 0.7 collective-permute-start.27
  86.9 4.2 %collective-permute-done.28 = bf16[64,2048]{1,0:T(8,128)(2,1)S(1)} collective-permute-done((bf16[64,2048]{1,0:T(8,128)(2,1)S(1)}, bf16[64,2048]{1,0:T(8,128)(2,1)S(1)}, u32[]{:S(2)}, u32[]{:S(2)}) %collective-permute-start.28) | collective-permute-done | bytes 262176 | tf_op jit(solution)/shard_map/ppermute | solution.py:212
  91.1 0.1 add_convert_fusion
  91.2 1.4 %collective-permute-done.27 = bf16[64,2048]{1,0:T(8,128)(2,1)S(1)} collective-permute-done((bf16[64,2048]{1,0:T(8,128)(2,1)S(1)}, bf16[64,2048]{1,0:T(8,128)(2,1)S(1)}, u32[]{:S(2)}, u32[]{:S(2)}) %collective-permute-start.27) | collective-permute-done | bytes 262176 | tf_op jit(solution)/shard_map/ppermute | solution.py:212
  92.6 0.1 add_convert_fusion.2
  92.7 0.8 pad_maximum_fusion
  (27 shorter events, 0.4 us)
Async XLA Ops:
  0.8 1.0 %copy-start.3 = (bf16[128,2048]{1,0:T(8,128)(2,1)S(1)}, bf16[128,2048]{1,0:T(8,128)(2,1)}, u32[]{:S(2)}) copy-start(bf16[128,2048]{1,0:T(8,128)(2,1)} %tokens_ref.1) | copy-start | bytes 1572868
  1.9 15.1 %collective-permute-start = (bf16[2080,128]{1,0:T(8,128)(2,1)S(1)}, bf16[2080,128]{1,0:T(8,128)(2,1)S(1)}, u32[]{:S(2)}, u32[]{:S(2)}) collective-permute-start(bf16[2080,128]{1,0:T(8,128)(2,1)S(1)} %shard_map.73.refs_0_), channel_id=1, source_target_pairs={{0,8},{2,10},{8,16},{10,18},{16,24},{18,26},{24,28},{26,30},{28,20... | collective-permute-start | bytes 1597448 | tf_op jit(solution)/shard_map/ppermute | solution.py:170
  5.0 13.6 %collective-permute-start.1 = (bf16[2080,128]{1,0:T(8,128)(2,1)S(1)}, bf16[2080,128]{1,0:T(8,128)(2,1)S(1)}, u32[]{:S(2)}, u32[]{:S(2)}) collective-permute-start(bf16[2080,128]{1,0:T(8,128)(2,1)S(1)} %shard_map.73.refs_0_), channel_id=1, source_target_pairs={{0,4},{2,6},{8,0},{10,2},{16,8},{18,10},{24,16},{26,18},{28,24},{3... | collective-permute-start | bytes 1597448 | tf_op jit(solution)/shard_map/ppermute | solution.py:170
  5.0 13.6 %collective-permute-start.2 = (bf16[1,2048,768]{2,1,0:T(8,128)(2,1)}, bf16[1,2048,768]{2,1,0:T(8,128)(2,1)S(1)}, u32[]{:S(2)}, u32[]{:S(2)}) collective-permute-start(bf16[1,2048,768]{2,1,0:T(8,128)(2,1)} %refs_0_.1), channel_id=1, source_target_pairs={{0,2},{2,0},{4,6},{6,4},{8,10},{10,8},{12,14},{14,12},{16,18},{18,... | collective-permute-start | bytes 9437192 | tf_op jit(solution)/shard_map/ppermute | solution.py:168
  5.0 13.6 %collective-permute-start.3 = (bf16[1,2048,768]{2,1,0:T(8,128)(2,1)}, bf16[1,2048,768]{2,1,0:T(8,128)(2,1)S(1)}, u32[]{:S(2)}, u32[]{:S(2)}) collective-permute-start(bf16[1,2048,768]{2,1,0:T(8,128)(2,1)} %refs_1_.1), channel_id=1, source_target_pairs={{0,2},{2,0},{4,6},{6,4},{8,10},{10,8},{12,14},{14,12},{16,18},{18,... | collective-permute-start | bytes 9437192 | tf_op jit(solution)/shard_map/ppermute | solution.py:168
  5.5 15.2 %collective-permute-start.5 = (bf16[1,768,2048]{2,1,0:T(8,128)(2,1)}, bf16[1,768,2048]{2,1,0:T(8,128)(2,1)S(1)}, u32[]{:S(2)}, u32[]{:S(2)}) collective-permute-start(bf16[1,768,2048]{2,1,0:T(8,128)(2,1)} %refs_2_.1), channel_id=1, source_target_pairs={{0,2},{2,0},{4,6},{6,4},{8,10},{10,8},{12,14},{14,12},{16,18},{18,... | collective-permute-start | bytes 9437192 | tf_op jit(solution)/shard_map/ppermute | solution.py:168
  5.5 1.9 %copy-start = (bf16[1,2048,768]{2,1,0:T(8,128)(2,1)S(1)}, bf16[1,2048,768]{2,1,0:T(8,128)(2,1)}, u32[]{:S(2)}) copy-start(bf16[1,2048,768]{2,1,0:T(8,128)(2,1)} %refs_0_.1) | copy-start | bytes 9437188
  7.4 1.9 %copy-start.1 = (bf16[1,2048,768]{2,1,0:T(8,128)(2,1)S(1)}, bf16[1,2048,768]{2,1,0:T(8,128)(2,1)}, u32[]{:S(2)}) copy-start(bf16[1,2048,768]{2,1,0:T(8,128)(2,1)} %refs_1_.1) | copy-start | bytes 9437188
  9.3 1.9 %copy-start.2 = (bf16[1,768,2048]{2,1,0:T(8,128)(2,1)S(1)}, bf16[1,768,2048]{2,1,0:T(8,128)(2,1)}, u32[]{:S(2)}) copy-start(bf16[1,768,2048]{2,1,0:T(8,128)(2,1)} %refs_2_.1) | copy-start | bytes 9437188
  18.7 10.1 %collective-permute-start.4 = (bf16[1040,128]{1,0:T(8,128)(2,1)S(1)}, bf16[1040,128]{1,0:T(8,128)(2,1)S(1)}, u32[]{:S(2)}, u32[]{:S(2)}) collective-permute-start(bf16[1040,128]{1,0:T(8,128)(2,1)S(1)} %get-tuple-element.65.refs_0_), channel_id=1, source_target_pairs={{0,8},{2,10},{8,16},{10,18},{16,24},{18,26},{24,28},{26,30},{28,20... | collective-permute-start | bytes 798728 | tf_op jit(solution)/shard_map/ppermute | solution.py:184
  20.3 8.5 %collective-permute-start.7 = (bf16[1040,128]{1,0:T(8,128)(2,1)S(1)}, bf16[1040,128]{1,0:T(8,128)(2,1)S(1)}, u32[]{:S(2)}, u32[]{:S(2)}) collective-permute-start(bf16[1040,128]{1,0:T(8,128)(2,1)S(1)} %get-tuple-element.69.refs_1_), channel_id=1, source_target_pairs={{0,4},{2,6},{8,0},{10,2},{16,8},{18,10},{24,16},{26,18},{28,24},{3... | collective-permute-start | bytes 798728 | tf_op jit(solution)/shard_map/ppermute | solution.py:184
  23.7 10.1 %collective-permute-start.11 = (bf16[1040,128]{1,0:T(8,128)(2,1)S(1)}, bf16[1040,128]{1,0:T(8,128)(2,1)S(1)}, u32[]{:S(2)}, u32[]{:S(2)}) collective-permute-start(bf16[1040,128]{1,0:T(8,128)(2,1)S(1)} %get-tuple-element.81.refs_0_), channel_id=1, source_target_pairs={{0,4},{2,6},{8,0},{10,2},{16,8},{18,10},{24,16},{26,18},{28,24},{3... | collective-permute-start | bytes 798728 | tf_op jit(solution)/shard_map/ppermute | solution.py:184
  24.9 9.3 %collective-permute-start.13 = (bf16[1040,128]{1,0:T(8,128)(2,1)S(1)}, bf16[1040,128]{1,0:T(8,128)(2,1)S(1)}, u32[]{:S(2)}, u32[]{:S(2)}) collective-permute-start(bf16[1040,128]{1,0:T(8,128)(2,1)S(1)} %get-tuple-element.83.refs_1_), channel_id=1, source_target_pairs={{0,8},{2,10},{8,16},{10,18},{16,24},{18,26},{24,28},{26,30},{28,20... | collective-permute-start | bytes 798728 | tf_op jit(solution)/shard_map/ppermute | solution.py:184
  28.8 11.1 %collective-permute-start.6 = (bf16[1040,128]{1,0:T(8,128)(2,1)S(1)}, bf16[1040,128]{1,0:T(8,128)(2,1)S(1)}, u32[]{:S(2)}, u32[]{:S(2)}) collective-permute-start(bf16[1040,128]{1,0:T(8,128)(2,1)S(1)} %collective-permute-done.4.refs_0_), channel_id=1, source_target_pairs={{0,8},{2,10},{8,16},{10,18},{16,24},{18,26},{24,28},{26,30},{28,20... | collective-permute-start | bytes 798728 | tf_op jit(solution)/shard_map/ppermute | solution.py:184
  30.4 9.4 %collective-permute-start.9 = (bf16[1040,128]{1,0:T(8,128)(2,1)S(1)}, bf16[1040,128]{1,0:T(8,128)(2,1)S(1)}, u32[]{:S(2)}, u32[]{:S(2)}) collective-permute-start(bf16[1040,128]{1,0:T(8,128)(2,1)S(1)} %collective-permute-done.7.refs_1_), channel_id=1, source_target_pairs={{0,4},{2,6},{8,0},{10,2},{16,8},{18,10},{24,16},{26,18},{28,24},{3... | collective-permute-start | bytes 798728 | tf_op jit(solution)/shard_map/ppermute | solution.py:184
  34.1 11.3 %collective-permute-start.12 = (bf16[1040,128]{1,0:T(8,128)(2,1)S(1)}, bf16[1040,128]{1,0:T(8,128)(2,1)S(1)}, u32[]{:S(2)}, u32[]{:S(2)}) collective-permute-start(bf16[1040,128]{1,0:T(8,128)(2,1)S(1)} %collective-permute-done.11.refs_0_), channel_id=1, source_target_pairs={{0,4},{2,6},{8,0},{10,2},{16,8},{18,10},{24,16},{26,18},{28,24},{3... | collective-permute-start | bytes 798728 | tf_op jit(solution)/shard_map/ppermute | solution.py:184
  35.7 9.8 %collective-permute-start.14 = (bf16[1040,128]{1,0:T(8,128)(2,1)S(1)}, bf16[1040,128]{1,0:T(8,128)(2,1)S(1)}, u32[]{:S(2)}, u32[]{:S(2)}) collective-permute-start(bf16[1040,128]{1,0:T(8,128)(2,1)S(1)} %collective-permute-done.13.refs_1_), channel_id=1, source_target_pairs={{0,8},{2,10},{8,16},{10,18},{16,24},{18,26},{24,28},{26,30},{28,20... | collective-permute-start | bytes 798728 | tf_op jit(solution)/shard_map/ppermute | solution.py:184
  39.8 11.3 %collective-permute-start.8 = (bf16[1040,128]{1,0:T(8,128)(2,1)S(1)}, bf16[1040,128]{1,0:T(8,128)(2,1)S(1)}, u32[]{:S(2)}, u32[]{:S(2)}) collective-permute-start(bf16[1040,128]{1,0:T(8,128)(2,1)S(1)} %collective-permute-done.6.refs_0_), channel_id=1, source_target_pairs={{0,8},{2,10},{8,16},{10,18},{16,24},{18,26},{24,28},{26,30},{28,20... | collective-permute-start | bytes 798728 | tf_op jit(solution)/shard_map/ppermute | solution.py:184
  41.3 9.8 %collective-permute-start.10 = (bf16[1040,128]{1,0:T(8,128)(2,1)S(1)}, bf16[1040,128]{1,0:T(8,128)(2,1)S(1)}, u32[]{:S(2)}, u32[]{:S(2)}) collective-permute-start(bf16[1040,128]{1,0:T(8,128)(2,1)S(1)} %collective-permute-done.9.refs_1_), channel_id=1, source_target_pairs={{0,4},{2,6},{8,0},{10,2},{16,8},{18,10},{24,16},{26,18},{28,24},{3... | collective-permute-start | bytes 798728 | tf_op jit(solution)/shard_map/ppermute | solution.py:184
  48.5 7.7 %collective-permute-start.21 = (bf16[64,2048]{1,0:T(8,128)(2,1)S(1)}, bf16[64,2048]{1,0:T(8,128)(2,1)S(1)}, u32[]{:S(2)}, u32[]{:S(2)}) collective-permute-start(bf16[64,2048]{1,0:T(8,128)(2,1)S(1)} %get-tuple-element.93), channel_id=1, source_target_pairs={{0,8},{2,10},{8,16},{10,18},{16,24},{18,26},{24,28},{26,30},{28,20... | collective-permute-start | bytes 786440 | tf_op jit(solution)/shard_map/ppermute | solution.py:212
  50.1 8.1 %collective-permute-start.22 = (bf16[64,2048]{1,0:T(8,128)(2,1)S(1)}, bf16[64,2048]{1,0:T(8,128)(2,1)S(1)}, u32[]{:S(2)}, u32[]{:S(2)}) collective-permute-start(bf16[64,2048]{1,0:T(8,128)(2,1)S(1)} %get-tuple-element.106), channel_id=1, source_target_pairs={{0,4},{2,6},{8,0},{10,2},{16,8},{18,10},{24,16},{26,18},{28,24},{3... | collective-permute-start | bytes 786440 | tf_op jit(solution)/shard_map/ppermute | solution.py:212
  54.1 9.6 %collective-permute-start.15 = (bf16[64,2048]{1,0:T(8,128)(2,1)S(1)}, bf16[64,2048]{1,0:T(8,128)(2,1)S(1)}, u32[]{:S(2)}, u32[]{:S(2)}) collective-permute-start(bf16[64,2048]{1,0:T(8,128)(2,1)S(1)} %get-tuple-element.96), channel_id=1, source_target_pairs={{0,4},{2,6},{8,0},{10,2},{16,8},{18,10},{24,16},{26,18},{28,24},{3... | collective-permute-start | bytes 786440 | tf_op jit(solution)/shard_map/ppermute | solution.py:212
  55.8 9.2 %collective-permute-start.16 = (bf16[64,2048]{1,0:T(8,128)(2,1)S(1)}, bf16[64,2048]{1,0:T(8,128)(2,1)S(1)}, u32[]{:S(2)}, u32[]{:S(2)}) collective-permute-start(bf16[64,2048]{1,0:T(8,128)(2,1)S(1)} %get-tuple-element.99), channel_id=1, source_target_pairs={{0,8},{2,10},{8,16},{10,18},{16,24},{18,26},{24,28},{26,30},{28,20... | collective-permute-start | bytes 786440 | tf_op jit(solution)/shard_map/ppermute | solution.py:212
  58.2 12.4 %collective-permute-start.23 = (bf16[64,2048]{1,0:T(8,128)(2,1)S(1)}, bf16[64,2048]{1,0:T(8,128)(2,1)S(1)}, u32[]{:S(2)}, u32[]{:S(2)}) collective-permute-start(bf16[64,2048]{1,0:T(8,128)(2,1)S(1)} %add_convert_fusion.7), channel_id=1, source_target_pairs={{0,8},{2,10},{8,16},{10,18},{16,24},{18,26},{24,28},{26,30},{28,20... | collective-permute-start | bytes 786440 | tf_op jit(solution)/shard_map/ppermute | solution.py:212
  60.4 10.2 %collective-permute-start.24 = (bf16[64,2048]{1,0:T(8,128)(2,1)S(1)}, bf16[64,2048]{1,0:T(8,128)(2,1)S(1)}, u32[]{:S(2)}, u32[]{:S(2)}) collective-permute-start(bf16[64,2048]{1,0:T(8,128)(2,1)S(1)} %add_convert_fusion.6), channel_id=1, source_target_pairs={{0,4},{2,6},{8,0},{10,2},{16,8},{18,10},{24,16},{26,18},{28,24},{3... | collective-permute-start | bytes 786440 | tf_op jit(solution)/shard_map/ppermute | solution.py:212
  65.1 10.5 %collective-permute-start.17 = (bf16[64,2048]{1,0:T(8,128)(2,1)S(1)}, bf16[64,2048]{1,0:T(8,128)(2,1)S(1)}, u32[]{:S(2)}, u32[]{:S(2)}) collective-permute-start(bf16[64,2048]{1,0:T(8,128)(2,1)S(1)} %add_convert_fusion.11), channel_id=1, source_target_pairs={{0,4},{2,6},{8,0},{10,2},{16,8},{18,10},{24,16},{26,18},{28,24},{3... | collective-permute-start | bytes 786440 | tf_op jit(solution)/shard_map/ppermute | solution.py:212
  66.8 9.5 %collective-permute-start.18 = (bf16[64,2048]{1,0:T(8,128)(2,1)S(1)}, bf16[64,2048]{1,0:T(8,128)(2,1)S(1)}, u32[]{:S(2)}, u32[]{:S(2)}) collective-permute-start(bf16[64,2048]{1,0:T(8,128)(2,1)S(1)} %add_convert_fusion.10), channel_id=1, source_target_pairs={{0,8},{2,10},{8,16},{10,18},{16,24},{18,26},{24,28},{26,30},{28,20... | collective-permute-start | bytes 786440 | tf_op jit(solution)/shard_map/ppermute | solution.py:212
  70.7 10.8 %collective-permute-start.25 = (bf16[64,2048]{1,0:T(8,128)(2,1)S(1)}, bf16[64,2048]{1,0:T(8,128)(2,1)S(1)}, u32[]{:S(2)}, u32[]{:S(2)}) collective-permute-start(bf16[64,2048]{1,0:T(8,128)(2,1)S(1)} %add_convert_fusion.5), channel_id=1, source_target_pairs={{0,8},{2,10},{8,16},{10,18},{16,24},{18,26},{24,28},{26,30},{28,20... | collective-permute-start | bytes 786440 | tf_op jit(solution)/shard_map/ppermute | solution.py:212
  71.6 9.9 %collective-permute-start.26 = (bf16[64,2048]{1,0:T(8,128)(2,1)S(1)}, bf16[64,2048]{1,0:T(8,128)(2,1)S(1)}, u32[]{:S(2)}, u32[]{:S(2)}) collective-permute-start(bf16[64,2048]{1,0:T(8,128)(2,1)S(1)} %add_convert_fusion.4), channel_id=1, source_target_pairs={{0,4},{2,6},{8,0},{10,2},{16,8},{18,10},{24,16},{26,18},{28,24},{3... | collective-permute-start | bytes 786440 | tf_op jit(solution)/shard_map/ppermute | solution.py:212
  76.3 8.2 %collective-permute-start.19 = (bf16[64,2048]{1,0:T(8,128)(2,1)S(1)}, bf16[64,2048]{1,0:T(8,128)(2,1)S(1)}, u32[]{:S(2)}, u32[]{:S(2)}) collective-permute-start(bf16[64,2048]{1,0:T(8,128)(2,1)S(1)} %add_convert_fusion.9), channel_id=1, source_target_pairs={{0,4},{2,6},{8,0},{10,2},{16,8},{18,10},{24,16},{26,18},{28,24},{3... | collective-permute-start | bytes 786440 | tf_op jit(solution)/shard_map/ppermute | solution.py:212
  78.0 6.6 %collective-permute-start.20 = (bf16[64,2048]{1,0:T(8,128)(2,1)S(1)}, bf16[64,2048]{1,0:T(8,128)(2,1)S(1)}, u32[]{:S(2)}, u32[]{:S(2)}) collective-permute-start(bf16[64,2048]{1,0:T(8,128)(2,1)S(1)} %add_convert_fusion.8), channel_id=1, source_target_pairs={{0,8},{2,10},{8,16},{10,18},{16,24},{18,26},{24,28},{26,30},{28,20... | collective-permute-start | bytes 786440 | tf_op jit(solution)/shard_map/ppermute | solution.py:212
  84.6 6.5 %collective-permute-start.28 = (bf16[64,2048]{1,0:T(8,128)(2,1)S(1)}, bf16[64,2048]{1,0:T(8,128)(2,1)S(1)}, u32[]{:S(2)}, u32[]{:S(2)}) collective-permute-start(bf16[64,2048]{1,0:T(8,128)(2,1)S(1)} %add_convert_fusion.1), channel_id=1, source_target_pairs={{0,8},{2,10},{8,16},{10,18},{16,24},{18,26},{24,28},{26,30},{28,20... | collective-permute-start | bytes 786440 | tf_op jit(solution)/shard_map/ppermute | solution.py:212
  86.2 6.4 %collective-permute-start.27 = (bf16[64,2048]{1,0:T(8,128)(2,1)S(1)}, bf16[64,2048]{1,0:T(8,128)(2,1)S(1)}, u32[]{:S(2)}, u32[]{:S(2)}) collective-permute-start(bf16[64,2048]{1,0:T(8,128)(2,1)S(1)} %add_convert_fusion.3), channel_id=1, source_target_pairs={{0,4},{2,6},{8,0},{10,2},{16,8},{18,10},{24,16},{26,18},{28,24},{3... | collective-permute-start | bytes 786440 | tf_op jit(solution)/shard_map/ppermute | solution.py:212

commit v6 on v4

--- a/solution.py
+++ b/solution.py
@@ -11,37 +11,57 @@
 TILE = 16
 
 
-def pack_kernel(tokens_ref, scores_ref, out_ref):
-    rows, width = tokens_ref.shape
-    chips = scores_ref.shape[0] // 2
+def tail_kernel(scores_ref, out_ref):
+    chips, rows = scores_ref.shape[0] // 2, scores_ref.shape[1]
     half = rows // 2
     lane = lax.broadcasted_iota(jnp.int32, (chips, LANES), 1)
     even, odd = (scores_ref[pl.ds(i, chips, stride=2), :] for i in range(2))
-    at = 0
     for h in range(2):
-        for g in range(0, half, TILE):
-            for j in range(0, width, LANES):
-                out_ref[pl.ds(at, TILE), :] = tokens_ref[pl.ds(h * half + g, TILE), pl.ds(j, LANES)]
-                at += TILE
         first, second = (even, pltpu.roll(odd, half, 1)) if h == 0 else (pltpu.roll(even, half, 1), odd)
         scores = jnp.where(lane < half, first, second)
         high = scores.astype(jnp.bfloat16).astype(jnp.float32)
         tail = jnp.concatenate([high, scores - high], axis=0).astype(jnp.bfloat16)
-        out_ref[pl.ds(at, 2 * chips), :] = tail
-        at += 2 * chips
-
-
-def pack(tokens, expert_ids, gate_scores, partner):
+        out_ref[pl.ds(h * 2 * chips, 2 * chips), :] = tail
+
+
+def tail_of(expert_ids, gate_scores, partner):
     scores = jnp.sum(jnp.where(expert_ids.T[None] == partner[:, None, None], gate_scores.T[None], 0.0), axis=1)
-    rows, width = tokens.shape
     near = pl.BlockSpec(memory_space=pltpu.VMEM)
     return pl.pallas_call(
-        pack_kernel,
-        in_specs=[near, near],
+        tail_kernel,
+        in_specs=[near],
         out_specs=near,
-        out_shape=jax.ShapeDtypeStruct((rows * width // LANES + 2 * scores.shape[0], LANES), jnp.bfloat16),
-        compiler_params=pltpu.CompilerParams(vmem_limit_bytes=4 * 2**20),
-    )(tokens, scores)
+        out_shape=jax.ShapeDtypeStruct((2 * scores.shape[0], LANES), jnp.bfloat16),
+        compiler_params=pltpu.CompilerParams(vmem_limit_bytes=2 * 2**20),
+    )(scores)
+
+
+def pack_kernel(n, *refs):
+    block_refs, tail_refs, out_refs = refs[:n], refs[n : 2 * n], refs[2 * n :]
+    for i, (block_ref, tail_ref) in enumerate(zip(block_refs, tail_refs)):
+        half, extra = block_ref.shape[0] // 2, tail_ref.shape[0] // 2
+        for h in range(2):
+            out_ref = out_refs[2 * i + h]
+            at = 0
+            for g in range(0, half, TILE):
+                for j in range(0, block_ref.shape[1], LANES):
+                    out_ref[pl.ds(at, TILE), :] = block_ref[pl.ds(h * half + g, TILE), pl.ds(j, LANES)]
+                    at += TILE
+            out_ref[pl.ds(at, extra), :] = tail_ref[pl.ds(h * extra, extra), :]
+
+
+def pack(blocks, tails, flops):
+    rows, width = blocks[0].shape
+    near = pl.BlockSpec(memory_space=pltpu.VMEM)
+    size = rows // 2 * width // LANES + tails[0].shape[0] // 2
+    return pl.pallas_call(
+        functools.partial(pack_kernel, len(blocks)),
+        in_specs=[near] * (2 * len(blocks)),
+        out_specs=[near] * (2 * len(blocks)),
+        out_shape=[jax.ShapeDtypeStruct((size, LANES), jnp.bfloat16)] * (2 * len(blocks)),
+        compiler_params=pltpu.CompilerParams(vmem_limit_bytes=6 * 2**20),
+        cost_estimate=pl.CostEstimate(flops=flops, bytes_accessed=2**20, transcendentals=0),
+    )(*blocks, *tails)
 
 
 def load_kernel(*refs):
@@ -144,11 +164,12 @@
         return lax.optimization_barrier((value, deps))[0]
 
     half = tokens.shape[0] // 2
-    other = [lax.ppermute(w, "ep", swap) for w in own]
-    packed = pack(tokens, expert_ids, gate_scores, partner)
-    first = [lax.ppermute(packed, "ep", perm[d]) for d in range(2)]
+    first = [lax.ppermute(tokens, "ep", perm[d]) for d in range(2)]
+    tail = tail_of(expert_ids, gate_scores, partner)
+    tails = [lax.ppermute(tail, "ep", perm[d]) for d in range(2)]
+    other = [lax.ppermute(w if i == 0 else tie(w, *tails), "ep", swap) for i, w in enumerate(own)]
     own = load(own)
-    held = {(d, h, 1): part for d, block in enumerate(first) for h, part in enumerate(jnp.split(block, 2))}
+    held = dict(zip([(d, h, 1) for d in range(2) for h in range(2)], pack(first, tails, 5 * 10**10)))
     last = {(d, h): far if d == h else far - 1 for d in range(2) for h in range(2)}
     done = {}
 
@@ -168,16 +189,21 @@
         return [(d, h, s) for d, h in groups[g] if s <= last[d, h]]
 
     for g in range(2):
-        send(flows(g, 2), *other, *own)
+        send(flows(g, 2), *([other[0], *own] if g == 0 else other[:2]))
     worked = []
     for s in range(1, far):
         for g in range(2):
             names = flows(g, s)
-            worked.append(compute(names, [held[n] for n in names], *worked[-1:]))
+            if s > 1:
+                worked.append(compute(names, [held[n] for n in names], *worked[-1:]))
             if s + 2 <= far:
-                send(flows(g, s + 2), worked[-1])
+                send(flows(g, s + 2), *worked[-1:])
     names = flows(0, far)
     worked.append(compute(names, [held[n] for n in names], worked[-1]))
+    for g in (1, 0):
+        names = flows(g, 1)
+        worked.append(compute(names, [held[n] for n in names], worked[-1]))
+    k_far = worked[-3]
 
     back = {}
 
@@ -194,9 +220,9 @@
     give(flows(0, far))
     for s in range(far - 1, 0, -1):
         if s > 1:
-            give(flows(1, s - 1), worked[-1])
+            give(flows(1, s - 1), k_far)
         give(flows(0, s), *([back[f] for f in groups[1]] if s == 1 else []))
-    compute([(0, 0, 0), (0, 1, 0)], [packed], worked[-1])
+    compute([(0, 0, 0), (0, 1, 0)], pack([tokens], [tail], 0), worked[-1])
     out = [
         (done[0, h, 0] + back[0, h].astype(jnp.float32) + back[1, h].astype(jnp.float32)).astype(jnp.bfloat16)
         for h in range(2)

time: 95.8 us -> 92.6 us (0.967)
  waiting for transfers between devices: 32.9 us -> 28.7 us
  starting transfers between devices: 28.9 us -> 30.8 us
  local copies, waits for them, and re-layouts: 6.77 us -> 5.68 us
    ppermute x14, waiting for transfers between devices: 22 us -> 16.5 us  [give(): back[d, h] = lax.ppermute(part, 'ep', perm[1 - d])]
    ppermute x5 -> x7, starting transfers between devices: 3.59 us -> 5.56 us  [the longest x2 3.03 us: on_device(): first = [lax.ppermute(tokens, 'ep', perm[d]) for d in range(2)]]
    ppermute x10, waiting for transfers between devices: 2.99 us -> 4.81 us  [send(): held[d, h, s] = lax.ppermute(tie(held[d, h, s - 1], *deps), 'ep', perm[d])]
    unnamed x8 -> x12, local copies, waits for them, and re-layouts: 6.7 us -> 5.68 us
    ppermute x5 -> x7, waiting for transfers between devices: 7.86 us -> 7.38 us  [the longest x2 4.5 us: on_device(): tails = [lax.ppermute(tail, 'ep', perm[d]) for d in range(2)]]
  transfers between devices with their start and end apart: 29 -> 31, of which waited for: 15 -> 18; matrix products, arithmetic and copies ran while one was open for 2% -> 1% of each run, Pallas kernels for 26% -> 27%
where the time goes in v6:
time: 92.6 us; the launch traced here: 92.4 us
  starting transfers between devices  30.8 us (33%)
  waiting for transfers between devices  28.7 us (31%)
  Pallas kernels  24.7 us (27%)
  local copies, waits for them, and re-layouts  5.68 us (6%)
  other arithmetic  2.35 us (3%)
    pallas_call x8, Pallas kernels, ffn(): pl.pallas_call(functools.partial(ffn_kernel, n_in, n_out, n_dev), in_spec...  23.7 us
    ppermute x14, waiting for transfers between devices, give(): back[d, h] = lax.ppermute(part, 'ep', perm[1 - d])  16.5 us
    ppermute x14, starting transfers between devices, give(): back[d, h] = lax.ppermute(part, 'ep', perm[1 - d])  15 us
    ppermute x10, starting transfers between devices, send(): held[d, h, s] = lax.ppermute(tie(held[d, h, s - 1], *deps), 'ep', perm[d])  10.2 us
    unnamed x12, local copies, waits for them, and re-layouts  5.68 us
    ppermute x10, waiting for transfers between devices, send(): held[d, h, s] = lax.ppermute(tie(held[d, h, s - 1], *deps), 'ep', perm[d])  4.81 us
    ppermute x2, waiting for transfers between devices, on_device(): tails = [lax.ppermute(tail, 'ep', perm[d]) for d in range(2)]  4.5 us
    ppermute x2, starting transfers between devices, on_device(): first = [lax.ppermute(tokens, 'ep', perm[d]) for d in range(2)]  3.03 us
  transfers between devices with their start and end apart: 31, of which 18 were waited for; matrix products, arithmetic and copies ran while one was open for 1% of the time, Pallas kernels for 27%

profile of v6, /device:TPU:0, one launch (start us, length us, event | category | flops | bytes accessed | tf_op | source)
XLA Modules:
  0.0 92.4 jit_solution(10986154418804034566)
XLA Ops:
  0.0 3.0 %collective-permute-start = (bf16[128,2048]{1,0:T(8,128)(2,1)}, bf16[128,2048]{1,0:T(8,128)(2,1)S(1)}, u32[]{:S(2)}, u32[]{:S(2)}) collective-permute-start(bf16[128,2048]{1,0:T(8,128)(2,1)} %refs_0_.2), channel_id=1, source_target_pairs={{0,8},{2,10},{8,16},{10,18},{16,24},{18,26},{24,28},{26,30},{28,20... | collective-permute-start | bytes 1572872 | tf_op jit(solution)/shard_map/ppermute | solution.py:167
  3.0 0.8 select_reduce_fusion.scores_ref
  3.8 0.1 shard_map.73.refs_1_
  3.9 2.0 %collective-permute-start.2 = (bf16[32,128]{1,0:T(8,128)(2,1)S(1)}, bf16[32,128]{1,0:T(8,128)(2,1)S(1)}, u32[]{:S(2)}, u32[]{:S(2)}) collective-permute-start(bf16[32,128]{1,0:T(8,128)(2,1)S(1)} %shard_map.73.refs_1_), channel_id=1, source_target_pairs={{0,8},{2,10},{8,16},{10,18},{16,24},{18,26},{24,28},{26,30},{28,20... | collective-permute-start | bytes 24584 | tf_op jit(solution)/shard_map/ppermute | solution.py:169
  5.9 1.9 %copy-done = bf16[1,2048,768]{2,1,0:T(8,128)(2,1)S(1)} copy-done((bf16[1,2048,768]{2,1,0:T(8,128)(2,1)S(1)}, bf16[1,2048,768]{2,1,0:T(8,128)(2,1)}, u32[]{:S(2)}) %copy-start) | copy-done | bytes 3145752
  7.8 1.9 %copy-done.1 = bf16[1,2048,768]{2,1,0:T(8,128)(2,1)S(1)} copy-done((bf16[1,2048,768]{2,1,0:T(8,128)(2,1)S(1)}, bf16[1,2048,768]{2,1,0:T(8,128)(2,1)}, u32[]{:S(2)}) %copy-start.1) | copy-done | bytes 3145752
  9.7 1.9 %copy-done.3 = bf16[1,768,2048]{2,1,0:T(8,128)(2,1)S(1)} copy-done((bf16[1,768,2048]{2,1,0:T(8,128)(2,1)S(1)}, bf16[1,768,2048]{2,1,0:T(8,128)(2,1)}, u32[]{:S(2)}) %copy-start.3) | copy-done | bytes 3145752
  11.6 0.7 shard_map.76
  12.3 3.0 %collective-permute-done.2.refs_2_ = bf16[32,128]{1,0:T(8,128)(2,1)S(1)} collective-permute-done((bf16[32,128]{1,0:T(8,128)(2,1)S(1)}, bf16[32,128]{1,0:T(8,128)(2,1)S(1)}, u32[]{:S(2)}, u32[]{:S(2)}) %collective-permute-start.2) | collective-permute-done | bytes 8224 | tf_op jit(solution)/shard_map/ppermute | solution.py:169
  15.2 1.5 %collective-permute-done.3.refs_3_ = bf16[32,128]{1,0:T(8,128)(2,1)S(1)} collective-permute-done((bf16[32,128]{1,0:T(8,128)(2,1)S(1)}, bf16[32,128]{1,0:T(8,128)(2,1)S(1)}, u32[]{:S(2)}, u32[]{:S(2)}) %collective-permute-start.3) | collective-permute-done | bytes 8224 | tf_op jit(solution)/shard_map/ppermute | solution.py:169
  16.8 0.5 collective-permute-start.9
  17.3 0.2 shard_map.75
  17.5 0.4 collective-permute-start.7
  17.9 1.7 %collective-permute-start.5 = (bf16[1040,128]{1,0:T(8,128)(2,1)S(1)}, bf16[1040,128]{1,0:T(8,128)(2,1)S(1)}, u32[]{:S(2)}, u32[]{:S(2)}) collective-permute-start(bf16[1040,128]{1,0:T(8,128)(2,1)S(1)} %get-tuple-element.95.refs_0_), channel_id=1, source_target_pairs={{0,8},{2,10},{8,16},{10,18},{16,24},{18,26},{24,28},{26,30},{28,20... | collective-permute-start | bytes 798728 | tf_op jit(solution)/shard_map/ppermute | solution.py:184
  19.6 2.9 %collective-permute-done.8.refs_6_ = bf16[1,2048,768]{2,1,0:T(8,128)(2,1)S(1)} collective-permute-done((bf16[1,2048,768]{2,1,0:T(8,128)(2,1)S(1)}, bf16[1,2048,768]{2,1,0:T(8,128)(2,1)S(1)}, u32[]{:S(2)}, u32[]{:S(2)}) %collective-permute-start.8) | collective-permute-done | bytes 3145760 | tf_op jit(solution)/shard_map/ppermute | solution.py:170
  22.5 0.3 collective-permute-start.13
  22.8 1.7 %collective-permute-start.15 = (bf16[1040,128]{1,0:T(8,128)(2,1)S(1)}, bf16[1040,128]{1,0:T(8,128)(2,1)S(1)}, u32[]{:S(2)}, u32[]{:S(2)}) collective-permute-start(bf16[1040,128]{1,0:T(8,128)(2,1)S(1)} %get-tuple-element.93.refs_1_), channel_id=1, source_target_pairs={{0,8},{2,10},{8,16},{10,18},{16,24},{18,26},{24,28},{26,30},{28,20... | collective-permute-start | bytes 798728 | tf_op jit(solution)/shard_map/ppermute | solution.py:184
  24.5 0.1 shard_map.74
  24.6 2.0 %collective-permute-done.7.refs_1_ = bf16[1040,128]{1,0:T(8,128)(2,1)S(1)} collective-permute-done((bf16[1040,128]{1,0:T(8,128)(2,1)S(1)}, bf16[1040,128]{1,0:T(8,128)(2,1)S(1)}, u32[]{:S(2)}, u32[]{:S(2)}) %collective-permute-start.7) | collective-permute-done | bytes 266272 | tf_op jit(solution)/shard_map/ppermute | solution.py:184
  26.6 0.3 collective-permute-start.11
  26.9 1.7 %collective-permute-start.6 = (bf16[1040,128]{1,0:T(8,128)(2,1)S(1)}, bf16[1040,128]{1,0:T(8,128)(2,1)S(1)}, u32[]{:S(2)}, u32[]{:S(2)}) collective-permute-start(bf16[1040,128]{1,0:T(8,128)(2,1)S(1)} %collective-permute-done.5.refs_0_), channel_id=1, source_target_pairs={{0,8},{2,10},{8,16},{10,18},{16,24},{18,26},{24,28},{26,30},{28,20... | collective-permute-start | bytes 798728 | tf_op jit(solution)/shard_map/ppermute | solution.py:184
  28.6 3.0 %shard_map.77 = (f32[64,2048]{1,0:T(8,128)S(1)}, f32[64,2048]{1,0:T(8,128)S(1)}) custom-call(bf16[1040,128]{1,0:T(8,128)(2,1)S(1)} %collective-permute-done.5.refs_0_, bf16[1040,128]{1,0:T(8,128)(2,1)S(1)} %collective-permute-done.7.refs_1_, bf16[1,2048,768]{2,1,0:T(8,128)(2,1)S(1)} %get-tuple-element.68.refs_2_, ...), custom_call_target="tpu_custom_call" | custom-call | flops 2415919104 | bytes 20447232 | tf_op jit(solution)/shard_map/pallas_call | solution.py:133
  31.6 0.7 collective-permute-done.13.refs_0_
  32.3 0.1 collective-permute-done.15.refs_1_
  32.4 1.6 %collective-permute-start.14 = (bf16[1040,128]{1,0:T(8,128)(2,1)S(1)}, bf16[1040,128]{1,0:T(8,128)(2,1)S(1)}, u32[]{:S(2)}, u32[]{:S(2)}) collective-permute-start(bf16[1040,128]{1,0:T(8,128)(2,1)S(1)} %collective-permute-done.13.refs_0_), channel_id=1, source_target_pairs={{0,4},{2,6},{8,0},{10,2},{16,8},{18,10},{24,16},{26,18},{28,24},{3... | collective-permute-start | bytes 798728 | tf_op jit(solution)/shard_map/ppermute | solution.py:184
  34.0 0.5 collective-permute-start.16
  34.4 3.0 %shard_map.78 = (f32[64,2048]{1,0:T(8,128)S(1)}, f32[64,2048]{1,0:T(8,128)S(1)}) custom-call(bf16[1040,128]{1,0:T(8,128)(2,1)S(1)} %collective-permute-done.13.refs_0_, bf16[1040,128]{1,0:T(8,128)(2,1)S(1)} %collective-permute-done.15.refs_1_, bf16[1,2048,768]{2,1,0:T(8,128)(2,1)S(1)} %get-tuple-element.68.refs_2_, ...), custom_call_target="tpu_custom_call" | custom-call | flops 2415919104 | bytes 20447232 | tf_op jit(solution)/shard_map/pallas_call | solution.py:133
  37.4 0.6 collective-permute-done.11.refs_1_
  38.0 0.1 collective-permute-done.6.refs_0_
  38.1 1.6 %collective-permute-start.12 = (bf16[1040,128]{1,0:T(8,128)(2,1)S(1)}, bf16[1040,128]{1,0:T(8,128)(2,1)S(1)}, u32[]{:S(2)}, u32[]{:S(2)}) collective-permute-start(bf16[1040,128]{1,0:T(8,128)(2,1)S(1)} %collective-permute-done.11.refs_1_), channel_id=1, source_target_pairs={{0,4},{2,6},{8,0},{10,2},{16,8},{18,10},{24,16},{26,18},{28,24},{3... | collective-permute-start | bytes 798728 | tf_op jit(solution)/shard_map/ppermute | solution.py:184
  39.7 0.5 collective-permute-start.10
  40.1 3.0 %shard_map.79 = (f32[64,2048]{1,0:T(8,128)S(1)}, f32[64,2048]{1,0:T(8,128)S(1)}) custom-call(bf16[1040,128]{1,0:T(8,128)(2,1)S(1)} %collective-permute-done.6.refs_0_, bf16[1040,128]{1,0:T(8,128)(2,1)S(1)} %collective-permute-done.11.refs_1_, bf16[1,2048,768]{2,1,0:T(8,128)(2,1)S(1)} %get-tuple-element.68.refs_2_, ...), custom_call_target="tpu_custom_call" | custom-call | flops 2415919104 | bytes 20447232 | tf_op jit(solution)/shard_map/pallas_call | solution.py:133
  43.1 0.6 collective-permute-done.14.refs_0_
  43.7 0.1 collective-permute-done.16.refs_1_
  43.8 3.0 %shard_map.80 = (bf16[64,2048]{1,0:T(8,128)(2,1)S(1)}, bf16[64,2048]{1,0:T(8,128)(2,1)S(1)}) custom-call(bf16[1040,128]{1,0:T(8,128)(2,1)S(1)} %collective-permute-done.14.refs_0_, bf16[1040,128]{1,0:T(8,128)(2,1)S(1)} %collective-permute-done.16.refs_1_, bf16[1,2048,768]{2,1,0:T(8,128)(2,1)S(1)} %get-tuple-element.68.refs_2_, ...), custom_call_target="tpu_custom_call" | custom-call | flops 2415919104 | bytes 20447232 | tf_op jit(solution)/shard_map/pallas_call | solution.py:133
  46.8 1.7 %collective-permute-start.23 = (bf16[64,2048]{1,0:T(8,128)(2,1)S(1)}, bf16[64,2048]{1,0:T(8,128)(2,1)S(1)}, u32[]{:S(2)}, u32[]{:S(2)}) collective-permute-start(bf16[64,2048]{1,0:T(8,128)(2,1)S(1)} %get-tuple-element.88), channel_id=1, source_target_pairs={{0,8},{2,10},{8,16},{10,18},{16,24},{18,26},{24,28},{26,30},{28,20... | collective-permute-start | bytes 786440 | tf_op jit(solution)/shard_map/ppermute | solution.py:217
  48.5 0.4 collective-permute-start.24
  48.9 0.6 collective-permute-done.10.refs_0_
  49.4 3.0 %shard_map.81 = (bf16[64,2048]{1,0:T(8,128)(2,1)S(1)}, bf16[64,2048]{1,0:T(8,128)(2,1)S(1)}) custom-call(bf16[1040,128]{1,0:T(8,128)(2,1)S(1)} %collective-permute-done.10.refs_0_, bf16[1040,128]{1,0:T(8,128)(2,1)S(1)} %collective-permute-done.12.refs_1_, bf16[1,2048,768]{2,1,0:T(8,128)(2,1)S(1)} %get-tuple-element.68.refs_2_, ...), custom_call_target="tpu_custom_call" | custom-call | flops 2415919104 | bytes 20447232 | tf_op jit(solution)/shard_map/pallas_call | solution.py:133
  52.4 1.6 %collective-permute-start.17 = (bf16[64,2048]{1,0:T(8,128)(2,1)S(1)}, bf16[64,2048]{1,0:T(8,128)(2,1)S(1)}, u32[]{:S(2)}, u32[]{:S(2)}) collective-permute-start(bf16[64,2048]{1,0:T(8,128)(2,1)S(1)} %get-tuple-element.91), channel_id=1, source_target_pairs={{0,4},{2,6},{8,0},{10,2},{16,8},{18,10},{24,16},{26,18},{28,24},{3... | collective-permute-start | bytes 786440 | tf_op jit(solution)/shard_map/ppermute | solution.py:217
  54.0 0.5 collective-permute-start.18
  54.5 3.0 %shard_map.82 = (f32[64,2048]{1,0:T(8,128)S(1)}, f32[64,2048]{1,0:T(8,128)S(1)}) custom-call(bf16[1040,128]{1,0:T(8,128)(2,1)S(1)} %get-tuple-element.92.refs_0_, bf16[1040,128]{1,0:T(8,128)(2,1)S(1)} %get-tuple-element.93.refs_1_, bf16[1,2048,768]{2,1,0:T(8,128)(2,1)S(1)} %get-tuple-element.68.refs_2_, bf16[1,2048,768]{2,1,0:T(8,128)(2,1)S(1)} %get-tuple-element.69.refs_3_, ...), custom_call_target="tpu_custom_call" | custom-call | flops 2415919104 | bytes 20447232 | tf_op jit(solution)/shard_map/pallas_call | solution.py:133
  57.5 1.6 %collective-permute-start.26 = (bf16[64,2048]{1,0:T(8,128)(2,1)S(1)}, bf16[64,2048]{1,0:T(8,128)(2,1)S(1)}, u32[]{:S(2)}, u32[]{:S(2)}) collective-permute-start(bf16[64,2048]{1,0:T(8,128)(2,1)S(1)} %add_convert_fusion.6), channel_id=1, source_target_pairs={{0,4},{2,6},{8,0},{10,2},{16,8},{18,10},{24,16},{26,18},{28,24},{3... | collective-permute-start | bytes 786440 | tf_op jit(solution)/shard_map/ppermute | solution.py:217
  59.2 0.5 collective-permute-start.25
  59.7 2.3 %collective-permute-done.17 = bf16[64,2048]{1,0:T(8,128)(2,1)S(1)} collective-permute-done((bf16[64,2048]{1,0:T(8,128)(2,1)S(1)}, bf16[64,2048]{1,0:T(8,128)(2,1)S(1)}, u32[]{:S(2)}, u32[]{:S(2)}) %collective-permute-start.17) | collective-permute-done | bytes 262176 | tf_op jit(solution)/shard_map/ppermute | solution.py:217
  62.1 1.5 %collective-permute-start.20 = (bf16[64,2048]{1,0:T(8,128)(2,1)S(1)}, bf16[64,2048]{1,0:T(8,128)(2,1)S(1)}, u32[]{:S(2)}, u32[]{:S(2)}) collective-permute-start(bf16[64,2048]{1,0:T(8,128)(2,1)S(1)} %add_convert_fusion.10), channel_id=1, source_target_pairs={{0,8},{2,10},{8,16},{10,18},{16,24},{18,26},{24,28},{26,30},{28,20... | collective-permute-start | bytes 786440 | tf_op jit(solution)/shard_map/ppermute | solution.py:217
  63.7 0.8 collective-permute-start.19
  64.5 3.1 %collective-permute-done.26 = bf16[64,2048]{1,0:T(8,128)(2,1)S(1)} collective-permute-done((bf16[64,2048]{1,0:T(8,128)(2,1)S(1)}, bf16[64,2048]{1,0:T(8,128)(2,1)S(1)}, u32[]{:S(2)}, u32[]{:S(2)}) %collective-permute-start.26) | collective-permute-done | bytes 262176 | tf_op jit(solution)/shard_map/ppermute | solution.py:217
  67.7 0.8 collective-permute-done.25
  68.6 1.6 %collective-permute-start.28 = (bf16[64,2048]{1,0:T(8,128)(2,1)S(1)}, bf16[64,2048]{1,0:T(8,128)(2,1)S(1)}, u32[]{:S(2)}, u32[]{:S(2)}) collective-permute-start(bf16[64,2048]{1,0:T(8,128)(2,1)S(1)} %add_convert_fusion.4), channel_id=1, source_target_pairs={{0,4},{2,6},{8,0},{10,2},{16,8},{18,10},{24,16},{26,18},{28,24},{3... | collective-permute-start | bytes 786440 | tf_op jit(solution)/shard_map/ppermute | solution.py:217
  70.3 0.5 collective-permute-start.27
  70.8 3.4 %collective-permute-done.20 = bf16[64,2048]{1,0:T(8,128)(2,1)S(1)} collective-permute-done((bf16[64,2048]{1,0:T(8,128)(2,1)S(1)}, bf16[64,2048]{1,0:T(8,128)(2,1)S(1)}, u32[]{:S(2)}, u32[]{:S(2)}) %collective-permute-start.20) | collective-permute-done | bytes 262176 | tf_op jit(solution)/shard_map/ppermute | solution.py:217
  74.2 0.7 collective-permute-start.22
  74.9 1.4 %collective-permute-start.21 = (bf16[64,2048]{1,0:T(8,128)(2,1)S(1)}, bf16[64,2048]{1,0:T(8,128)(2,1)S(1)}, u32[]{:S(2)}, u32[]{:S(2)}) collective-permute-start(bf16[64,2048]{1,0:T(8,128)(2,1)S(1)} %add_convert_fusion.9), channel_id=1, source_target_pairs={{0,4},{2,6},{8,0},{10,2},{16,8},{18,10},{24,16},{26,18},{28,24},{3... | collective-permute-start | bytes 786440 | tf_op jit(solution)/shard_map/ppermute | solution.py:217
  76.4 3.0 %shard_map.83 = (f32[64,2048]{1,0:T(8,128)S(1)}, f32[64,2048]{1,0:T(8,128)S(1)}) custom-call(bf16[1040,128]{1,0:T(8,128)(2,1)S(1)} %get-tuple-element.95.refs_0_, bf16[1040,128]{1,0:T(8,128)(2,1)S(1)} %get-tuple-element.96.refs_1_, bf16[1,2048,768]{2,1,0:T(8,128)(2,1)S(1)} %get-tuple-element.68.refs_2_, bf16[1,2048,768]{2,1,0:T(8,128)(2,1)S(1)} %get-tuple-element.69.refs_3_, ...), custom_call_target="tpu_custom_call" | custom-call | flops 2415919104 | bytes 20447232 | tf_op jit(solution)/shard_map/pallas_call | solution.py:133
  79.3 3.0 %shard_map.84 = (f32[64,2048]{1,0:T(8,128)S(1)}, f32[64,2048]{1,0:T(8,128)S(1)}) custom-call(bf16[1040,128]{1,0:T(8,128)(2,1)S(1)} %get-tuple-element.98.refs_0_, bf16[1040,128]{1,0:T(8,128)(2,1)S(1)} %get-tuple-element.99.refs_1_, bf16[1,2048,768]{2,1,0:T(8,128)(2,1)S(1)} %get-tuple-element.68.refs_2_, bf16[1,2048,768]{2,1,0:T(8,128)(2,1)S(1)} %get-tuple-element.69.refs_3_, ...), custom_call_target="tpu_custom_call" | custom-call | flops 2415919104 | bytes 20447232 | tf_op jit(solution)/shard_map/pallas_call | solution.py:133
  82.3 1.0 %collective-permute-done.22 = bf16[64,2048]{1,0:T(8,128)(2,1)S(1)} collective-permute-done((bf16[64,2048]{1,0:T(8,128)(2,1)S(1)}, bf16[64,2048]{1,0:T(8,128)(2,1)S(1)}, u32[]{:S(2)}, u32[]{:S(2)}) %collective-permute-start.22) | collective-permute-done | bytes 262176 | tf_op jit(solution)/shard_map/ppermute | solution.py:217
  83.3 1.6 %collective-permute-start.29 = (bf16[64,2048]{1,0:T(8,128)(2,1)S(1)}, bf16[64,2048]{1,0:T(8,128)(2,1)S(1)}, u32[]{:S(2)}, u32[]{:S(2)}) collective-permute-start(bf16[64,2048]{1,0:T(8,128)(2,1)S(1)} %add_convert_fusion.3), channel_id=1, source_target_pairs={{0,4},{2,6},{8,0},{10,2},{16,8},{18,10},{24,16},{26,18},{28,24},{3... | collective-permute-start | bytes 786440 | tf_op jit(solution)/shard_map/ppermute | solution.py:217
  85.0 0.5 collective-permute-start.30
  85.5 4.9 %collective-permute-done.29 = bf16[64,2048]{1,0:T(8,128)(2,1)S(1)} collective-permute-done((bf16[64,2048]{1,0:T(8,128)(2,1)S(1)}, bf16[64,2048]{1,0:T(8,128)(2,1)S(1)}, u32[]{:S(2)}, u32[]{:S(2)}) %collective-permute-start.29) | collective-permute-done | bytes 262176 | tf_op jit(solution)/shard_map/ppermute | solution.py:217
  90.4 0.1 add_convert_fusion.2
  90.5 0.9 collective-permute-done.30
  91.4 0.1 add_convert_fusion
  91.5 0.8 pad_maximum_fusion
  (36 shorter events, 0.6 us)
Async XLA Ops:
  0.0 17.3 %collective-permute-start = (bf16[128,2048]{1,0:T(8,128)(2,1)}, bf16[128,2048]{1,0:T(8,128)(2,1)S(1)}, u32[]{:S(2)}, u32[]{:S(2)}) collective-permute-start(bf16[128,2048]{1,0:T(8,128)(2,1)} %refs_0_.2), channel_id=1, source_target_pairs={{0,8},{2,10},{8,16},{10,18},{16,24},{18,26},{24,28},{26,30},{28,20... | collective-permute-start | bytes 1572872 | tf_op jit(solution)/shard_map/ppermute | solution.py:167
  3.0 14.3 %collective-permute-start.1 = (bf16[128,2048]{1,0:T(8,128)(2,1)}, bf16[128,2048]{1,0:T(8,128)(2,1)S(1)}, u32[]{:S(2)}, u32[]{:S(2)}) collective-permute-start(bf16[128,2048]{1,0:T(8,128)(2,1)} %refs_0_.2), channel_id=1, source_target_pairs={{0,4},{2,6},{8,0},{10,2},{16,8},{18,10},{24,16},{26,18},{28,24},{3... | collective-permute-start | bytes 1572872 | tf_op jit(solution)/shard_map/ppermute | solution.py:167
  3.9 11.3 %collective-permute-start.2 = (bf16[32,128]{1,0:T(8,128)(2,1)S(1)}, bf16[32,128]{1,0:T(8,128)(2,1)S(1)}, u32[]{:S(2)}, u32[]{:S(2)}) collective-permute-start(bf16[32,128]{1,0:T(8,128)(2,1)S(1)} %shard_map.73.refs_1_), channel_id=1, source_target_pairs={{0,8},{2,10},{8,16},{10,18},{16,24},{18,26},{24,28},{26,30},{28,20... | collective-permute-start | bytes 24584 | tf_op jit(solution)/shard_map/ppermute | solution.py:169
  5.9 10.9 %collective-permute-start.3 = (bf16[32,128]{1,0:T(8,128)(2,1)S(1)}, bf16[32,128]{1,0:T(8,128)(2,1)S(1)}, u32[]{:S(2)}, u32[]{:S(2)}) collective-permute-start(bf16[32,128]{1,0:T(8,128)(2,1)S(1)} %shard_map.73.refs_1_), channel_id=1, source_target_pairs={{0,4},{2,6},{8,0},{10,2},{16,8},{18,10},{24,16},{26,18},{28,24},{3... | collective-permute-start | bytes 24584 | tf_op jit(solution)/shard_map/ppermute | solution.py:169
  5.9 11.6 %collective-permute-start.4 = (bf16[1,2048,768]{2,1,0:T(8,128)(2,1)}, bf16[1,2048,768]{2,1,0:T(8,128)(2,1)S(1)}, u32[]{:S(2)}, u32[]{:S(2)}) collective-permute-start(bf16[1,2048,768]{2,1,0:T(8,128)(2,1)} %refs_0_.3), channel_id=1, source_target_pairs={{0,2},{2,0},{4,6},{6,4},{8,10},{10,8},{12,14},{14,12},{16,18},{18,... | collective-permute-start | bytes 9437192 | tf_op jit(solution)/shard_map/ppermute | solution.py:170
  5.9 1.9 %copy-start = (bf16[1,2048,768]{2,1,0:T(8,128)(2,1)S(1)}, bf16[1,2048,768]{2,1,0:T(8,128)(2,1)}, u32[]{:S(2)}) copy-start(bf16[1,2048,768]{2,1,0:T(8,128)(2,1)} %refs_0_.3) | copy-start | bytes 9437188
  7.8 1.9 %copy-start.1 = (bf16[1,2048,768]{2,1,0:T(8,128)(2,1)S(1)}, bf16[1,2048,768]{2,1,0:T(8,128)(2,1)}, u32[]{:S(2)}) copy-start(bf16[1,2048,768]{2,1,0:T(8,128)(2,1)} %refs_1_.1) | copy-start | bytes 9437188
  9.7 1.9 %copy-start.3 = (bf16[1,768,2048]{2,1,0:T(8,128)(2,1)S(1)}, bf16[1,768,2048]{2,1,0:T(8,128)(2,1)}, u32[]{:S(2)}) copy-start(bf16[1,768,2048]{2,1,0:T(8,128)(2,1)} %refs_2_.1) | copy-start | bytes 9437188
  11.6 5.2 %copy-start.2 = (bf16[1,2048,768]{2,1,0:T(8,128)(2,1)S(1)}, bf16[1,2048,768]{2,1,0:T(8,128)(2,1)}, u32[]{:S(2)}) copy-start(bf16[1,2048,768]{2,1,0:T(8,128)(2,1)} %refs_1_.1) | copy-start | bytes 9437188
  11.6 5.2 %copy-start.4 = (bf16[1,768,2048]{2,1,0:T(8,128)(2,1)S(1)}, bf16[1,768,2048]{2,1,0:T(8,128)(2,1)}, u32[]{:S(2)}) copy-start(bf16[1,768,2048]{2,1,0:T(8,128)(2,1)} %refs_2_.1) | copy-start | bytes 9437188
  12.3 12.2 %copy-start.5 = (bf16[128,2048]{1,0:T(8,128)(2,1)S(1)}, bf16[128,2048]{1,0:T(8,128)(2,1)}, u32[]{:S(2)}) copy-start(bf16[128,2048]{1,0:T(8,128)(2,1)} %refs_0_.2) | copy-start | bytes 1572868
  16.8 5.7 %collective-permute-start.8 = (bf16[1,2048,768]{2,1,0:T(8,128)(2,1)S(1)}, bf16[1,2048,768]{2,1,0:T(8,128)(2,1)S(1)}, u32[]{:S(2)}, u32[]{:S(2)}) collective-permute-start(bf16[1,2048,768]{2,1,0:T(8,128)(2,1)S(1)} %copy-done.2), channel_id=1, source_target_pairs={{0,2},{2,0},{4,6},{6,4},{8,10},{10,8},{12,14},{14,12},{16,18},{18,... | collective-permute-start | bytes 9437192 | tf_op jit(solution)/shard_map/ppermute | solution.py:170
  16.8 11.8 %collective-permute-start.9 = (bf16[1,768,2048]{2,1,0:T(8,128)(2,1)S(1)}, bf16[1,768,2048]{2,1,0:T(8,128)(2,1)S(1)}, u32[]{:S(2)}, u32[]{:S(2)}) collective-permute-start(bf16[1,768,2048]{2,1,0:T(8,128)(2,1)S(1)} %copy-done.4), channel_id=1, source_target_pairs={{0,2},{2,0},{4,6},{6,4},{8,10},{10,8},{12,14},{14,12},{16,18},{18,... | collective-permute-start | bytes 9437192 | tf_op jit(solution)/shard_map/ppermute | solution.py:170
  17.5 9.1 %collective-permute-start.7 = (bf16[1040,128]{1,0:T(8,128)(2,1)S(1)}, bf16[1040,128]{1,0:T(8,128)(2,1)S(1)}, u32[]{:S(2)}, u32[]{:S(2)}) collective-permute-start(bf16[1040,128]{1,0:T(8,128)(2,1)S(1)} %get-tuple-element.96.refs_1_), channel_id=1, source_target_pairs={{0,4},{2,6},{8,0},{10,2},{16,8},{18,10},{24,16},{26,18},{28,24},{3... | collective-permute-start | bytes 798728 | tf_op jit(solution)/shard_map/ppermute | solution.py:184
  17.9 9.0 %collective-permute-start.5 = (bf16[1040,128]{1,0:T(8,128)(2,1)S(1)}, bf16[1040,128]{1,0:T(8,128)(2,1)S(1)}, u32[]{:S(2)}, u32[]{:S(2)}) collective-permute-start(bf16[1040,128]{1,0:T(8,128)(2,1)S(1)} %get-tuple-element.95.refs_0_), channel_id=1, source_target_pairs={{0,8},{2,10},{8,16},{10,18},{16,24},{18,26},{24,28},{26,30},{28,20... | collective-permute-start | bytes 798728 | tf_op jit(solution)/shard_map/ppermute | solution.py:184
  22.5 9.9 %collective-permute-start.13 = (bf16[1040,128]{1,0:T(8,128)(2,1)S(1)}, bf16[1040,128]{1,0:T(8,128)(2,1)S(1)}, u32[]{:S(2)}, u32[]{:S(2)}) collective-permute-start(bf16[1040,128]{1,0:T(8,128)(2,1)S(1)} %get-tuple-element.92.refs_0_), channel_id=1, source_target_pairs={{0,4},{2,6},{8,0},{10,2},{16,8},{18,10},{24,16},{26,18},{28,24},{3... | collective-permute-start | bytes 798728 | tf_op jit(solution)/shard_map/ppermute | solution.py:184
  22.8 9.6 %collective-permute-start.15 = (bf16[1040,128]{1,0:T(8,128)(2,1)S(1)}, bf16[1040,128]{1,0:T(8,128)(2,1)S(1)}, u32[]{:S(2)}, u32[]{:S(2)}) collective-permute-start(bf16[1040,128]{1,0:T(8,128)(2,1)S(1)} %get-tuple-element.93.refs_1_), channel_id=1, source_target_pairs={{0,8},{2,10},{8,16},{10,18},{16,24},{18,26},{24,28},{26,30},{28,20... | collective-permute-start | bytes 798728 | tf_op jit(solution)/shard_map/ppermute | solution.py:184
  26.6 11.4 %collective-permute-start.11 = (bf16[1040,128]{1,0:T(8,128)(2,1)S(1)}, bf16[1040,128]{1,0:T(8,128)(2,1)S(1)}, u32[]{:S(2)}, u32[]{:S(2)}) collective-permute-start(bf16[1040,128]{1,0:T(8,128)(2,1)S(1)} %collective-permute-done.7.refs_1_), channel_id=1, source_target_pairs={{0,4},{2,6},{8,0},{10,2},{16,8},{18,10},{24,16},{26,18},{28,24},{3... | collective-permute-start | bytes 798728 | tf_op jit(solution)/shard_map/ppermute | solution.py:184
  26.9 11.2 %collective-permute-start.6 = (bf16[1040,128]{1,0:T(8,128)(2,1)S(1)}, bf16[1040,128]{1,0:T(8,128)(2,1)S(1)}, u32[]{:S(2)}, u32[]{:S(2)}) collective-permute-start(bf16[1040,128]{1,0:T(8,128)(2,1)S(1)} %collective-permute-done.5.refs_0_), channel_id=1, source_target_pairs={{0,8},{2,10},{8,16},{10,18},{16,24},{18,26},{24,28},{26,30},{28,20... | collective-permute-start | bytes 798728 | tf_op jit(solution)/shard_map/ppermute | solution.py:184
  32.4 11.3 %collective-permute-start.14 = (bf16[1040,128]{1,0:T(8,128)(2,1)S(1)}, bf16[1040,128]{1,0:T(8,128)(2,1)S(1)}, u32[]{:S(2)}, u32[]{:S(2)}) collective-permute-start(bf16[1040,128]{1,0:T(8,128)(2,1)S(1)} %collective-permute-done.13.refs_0_), channel_id=1, source_target_pairs={{0,4},{2,6},{8,0},{10,2},{16,8},{18,10},{24,16},{26,18},{28,24},{3... | collective-permute-start | bytes 798728 | tf_op jit(solution)/shard_map/ppermute | solution.py:184
  34.0 9.8 %collective-permute-start.16 = (bf16[1040,128]{1,0:T(8,128)(2,1)S(1)}, bf16[1040,128]{1,0:T(8,128)(2,1)S(1)}, u32[]{:S(2)}, u32[]{:S(2)}) collective-permute-start(bf16[1040,128]{1,0:T(8,128)(2,1)S(1)} %collective-permute-done.15.refs_1_), channel_id=1, source_target_pairs={{0,8},{2,10},{8,16},{10,18},{16,24},{18,26},{24,28},{26,30},{28,20... | collective-permute-start | bytes 798728 | tf_op jit(solution)/shard_map/ppermute | solution.py:184
  38.1 10.8 %collective-permute-start.12 = (bf16[1040,128]{1,0:T(8,128)(2,1)S(1)}, bf16[1040,128]{1,0:T(8,128)(2,1)S(1)}, u32[]{:S(2)}, u32[]{:S(2)}) collective-permute-start(bf16[1040,128]{1,0:T(8,128)(2,1)S(1)} %collective-permute-done.11.refs_1_), channel_id=1, source_target_pairs={{0,4},{2,6},{8,0},{10,2},{16,8},{18,10},{24,16},{26,18},{28,24},{3... | collective-permute-start | bytes 798728 | tf_op jit(solution)/shard_map/ppermute | solution.py:184
  39.7 9.7 %collective-permute-start.10 = (bf16[1040,128]{1,0:T(8,128)(2,1)S(1)}, bf16[1040,128]{1,0:T(8,128)(2,1)S(1)}, u32[]{:S(2)}, u32[]{:S(2)}) collective-permute-start(bf16[1040,128]{1,0:T(8,128)(2,1)S(1)} %collective-permute-done.6.refs_0_), channel_id=1, source_target_pairs={{0,8},{2,10},{8,16},{10,18},{16,24},{18,26},{24,28},{26,30},{28,20... | collective-permute-start | bytes 798728 | tf_op jit(solution)/shard_map/ppermute | solution.py:184
  46.8 10.7 %collective-permute-start.23 = (bf16[64,2048]{1,0:T(8,128)(2,1)S(1)}, bf16[64,2048]{1,0:T(8,128)(2,1)S(1)}, u32[]{:S(2)}, u32[]{:S(2)}) collective-permute-start(bf16[64,2048]{1,0:T(8,128)(2,1)S(1)} %get-tuple-element.88), channel_id=1, source_target_pairs={{0,8},{2,10},{8,16},{10,18},{16,24},{18,26},{24,28},{26,30},{28,20... | collective-permute-start | bytes 786440 | tf_op jit(solution)/shard_map/ppermute | solution.py:217
  48.5 9.0 %collective-permute-start.24 = (bf16[64,2048]{1,0:T(8,128)(2,1)S(1)}, bf16[64,2048]{1,0:T(8,128)(2,1)S(1)}, u32[]{:S(2)}, u32[]{:S(2)}) collective-permute-start(bf16[64,2048]{1,0:T(8,128)(2,1)S(1)} %get-tuple-element.108), channel_id=1, source_target_pairs={{0,4},{2,6},{8,0},{10,2},{16,8},{18,10},{24,16},{26,18},{28,24},{3... | collective-permute-start | bytes 786440 | tf_op jit(solution)/shard_map/ppermute | solution.py:217
  52.4 9.7 %collective-permute-start.17 = (bf16[64,2048]{1,0:T(8,128)(2,1)S(1)}, bf16[64,2048]{1,0:T(8,128)(2,1)S(1)}, u32[]{:S(2)}, u32[]{:S(2)}) collective-permute-start(bf16[64,2048]{1,0:T(8,128)(2,1)S(1)} %get-tuple-element.91), channel_id=1, source_target_pairs={{0,4},{2,6},{8,0},{10,2},{16,8},{18,10},{24,16},{26,18},{28,24},{3... | collective-permute-start | bytes 786440 | tf_op jit(solution)/shard_map/ppermute | solution.py:217
  54.0 8.1 %collective-permute-start.18 = (bf16[64,2048]{1,0:T(8,128)(2,1)S(1)}, bf16[64,2048]{1,0:T(8,128)(2,1)S(1)}, u32[]{:S(2)}, u32[]{:S(2)}) collective-permute-start(bf16[64,2048]{1,0:T(8,128)(2,1)S(1)} %get-tuple-element.101), channel_id=1, source_target_pairs={{0,8},{2,10},{8,16},{10,18},{16,24},{18,26},{24,28},{26,30},{28,20... | collective-permute-start | bytes 786440 | tf_op jit(solution)/shard_map/ppermute | solution.py:217
  57.5 10.1 %collective-permute-start.26 = (bf16[64,2048]{1,0:T(8,128)(2,1)S(1)}, bf16[64,2048]{1,0:T(8,128)(2,1)S(1)}, u32[]{:S(2)}, u32[]{:S(2)}) collective-permute-start(bf16[64,2048]{1,0:T(8,128)(2,1)S(1)} %add_convert_fusion.6), channel_id=1, source_target_pairs={{0,4},{2,6},{8,0},{10,2},{16,8},{18,10},{24,16},{26,18},{28,24},{3... | collective-permute-start | bytes 786440 | tf_op jit(solution)/shard_map/ppermute | solution.py:217
  59.2 9.3 %collective-permute-start.25 = (bf16[64,2048]{1,0:T(8,128)(2,1)S(1)}, bf16[64,2048]{1,0:T(8,128)(2,1)S(1)}, u32[]{:S(2)}, u32[]{:S(2)}) collective-permute-start(bf16[64,2048]{1,0:T(8,128)(2,1)S(1)} %add_convert_fusion.7), channel_id=1, source_target_pairs={{0,8},{2,10},{8,16},{10,18},{16,24},{18,26},{24,28},{26,30},{28,20... | collective-permute-start | bytes 786440 | tf_op jit(solution)/shard_map/ppermute | solution.py:217
  62.1 12.0 %collective-permute-start.20 = (bf16[64,2048]{1,0:T(8,128)(2,1)S(1)}, bf16[64,2048]{1,0:T(8,128)(2,1)S(1)}, u32[]{:S(2)}, u32[]{:S(2)}) collective-permute-start(bf16[64,2048]{1,0:T(8,128)(2,1)S(1)} %add_convert_fusion.10), channel_id=1, source_target_pairs={{0,8},{2,10},{8,16},{10,18},{16,24},{18,26},{24,28},{26,30},{28,20... | collective-permute-start | bytes 786440 | tf_op jit(solution)/shard_map/ppermute | solution.py:217
  63.7 10.4 %collective-permute-start.19 = (bf16[64,2048]{1,0:T(8,128)(2,1)S(1)}, bf16[64,2048]{1,0:T(8,128)(2,1)S(1)}, u32[]{:S(2)}, u32[]{:S(2)}) collective-permute-start(bf16[64,2048]{1,0:T(8,128)(2,1)S(1)} %add_convert_fusion.11), channel_id=1, source_target_pairs={{0,4},{2,6},{8,0},{10,2},{16,8},{18,10},{24,16},{26,18},{28,24},{3... | collective-permute-start | bytes 786440 | tf_op jit(solution)/shard_map/ppermute | solution.py:217
  68.6 13.7 %collective-permute-start.28 = (bf16[64,2048]{1,0:T(8,128)(2,1)S(1)}, bf16[64,2048]{1,0:T(8,128)(2,1)S(1)}, u32[]{:S(2)}, u32[]{:S(2)}) collective-permute-start(bf16[64,2048]{1,0:T(8,128)(2,1)S(1)} %add_convert_fusion.4), channel_id=1, source_target_pairs={{0,4},{2,6},{8,0},{10,2},{16,8},{18,10},{24,16},{26,18},{28,24},{3... | collective-permute-start | bytes 786440 | tf_op jit(solution)/shard_map/ppermute | solution.py:217
  70.3 12.0 %collective-permute-start.27 = (bf16[64,2048]{1,0:T(8,128)(2,1)S(1)}, bf16[64,2048]{1,0:T(8,128)(2,1)S(1)}, u32[]{:S(2)}, u32[]{:S(2)}) collective-permute-start(bf16[64,2048]{1,0:T(8,128)(2,1)S(1)} %add_convert_fusion.5), channel_id=1, source_target_pairs={{0,8},{2,10},{8,16},{10,18},{16,24},{18,26},{24,28},{26,30},{28,20... | collective-permute-start | bytes 786440 | tf_op jit(solution)/shard_map/ppermute | solution.py:217
  74.2 9.1 %collective-permute-start.22 = (bf16[64,2048]{1,0:T(8,128)(2,1)S(1)}, bf16[64,2048]{1,0:T(8,128)(2,1)S(1)}, u32[]{:S(2)}, u32[]{:S(2)}) collective-permute-start(bf16[64,2048]{1,0:T(8,128)(2,1)S(1)} %add_convert_fusion.8), channel_id=1, source_target_pairs={{0,8},{2,10},{8,16},{10,18},{16,24},{18,26},{24,28},{26,30},{28,20... | collective-permute-start | bytes 786440 | tf_op jit(solution)/shard_map/ppermute | solution.py:217
  74.9 8.4 %collective-permute-start.21 = (bf16[64,2048]{1,0:T(8,128)(2,1)S(1)}, bf16[64,2048]{1,0:T(8,128)(2,1)S(1)}, u32[]{:S(2)}, u32[]{:S(2)}) collective-permute-start(bf16[64,2048]{1,0:T(8,128)(2,1)S(1)} %add_convert_fusion.9), channel_id=1, source_target_pairs={{0,4},{2,6},{8,0},{10,2},{16,8},{18,10},{24,16},{26,18},{28,24},{3... | collective-permute-start | bytes 786440 | tf_op jit(solution)/shard_map/ppermute | solution.py:217
  83.3 7.1 %collective-permute-start.29 = (bf16[64,2048]{1,0:T(8,128)(2,1)S(1)}, bf16[64,2048]{1,0:T(8,128)(2,1)S(1)}, u32[]{:S(2)}, u32[]{:S(2)}) collective-permute-start(bf16[64,2048]{1,0:T(8,128)(2,1)S(1)} %add_convert_fusion.3), channel_id=1, source_target_pairs={{0,4},{2,6},{8,0},{10,2},{16,8},{18,10},{24,16},{26,18},{28,24},{3... | collective-permute-start | bytes 786440 | tf_op jit(solution)/shard_map/ppermute | solution.py:217
  85.0 6.4 %collective-permute-start.30 = (bf16[64,2048]{1,0:T(8,128)(2,1)S(1)}, bf16[64,2048]{1,0:T(8,128)(2,1)S(1)}, u32[]{:S(2)}, u32[]{:S(2)}) collective-permute-start(bf16[64,2048]{1,0:T(8,128)(2,1)S(1)} %add_convert_fusion.1), channel_id=1, source_target_pairs={{0,8},{2,10},{8,16},{10,18},{16,24},{18,26},{24,28},{26,30},{28,20... | collective-permute-start | bytes 786440 | tf_op jit(solution)/shard_map/ppermute | solution.py:217

commit v7 on v6

--- a/solution.py
+++ b/solution.py
@@ -143,6 +143,25 @@
     )(*blocks, *own, *other)
 
 
+def finish_kernel(own_ref, ahead_ref, behind_ref, *refs):
+    total = own_ref[...] + ahead_ref[...].astype(jnp.float32) + behind_ref[...].astype(jnp.float32)
+    refs[-1][...] = total.astype(refs[-1].dtype)
+
+
+def finish(h, out, own, ahead, behind):
+    half, width = own.shape
+    near = pl.BlockSpec(memory_space=pltpu.VMEM)
+    return pl.pallas_call(
+        finish_kernel,
+        grid=(1,),
+        in_specs=[near] * 3 + ([] if out is None else [pl.BlockSpec(memory_space=pl.ANY)]),
+        out_specs=pl.BlockSpec((half, width), lambda i: (h, 0)),
+        out_shape=jax.ShapeDtypeStruct((2 * half, width), jnp.bfloat16),
+        input_output_aliases={} if out is None else {3: 0},
+        compiler_params=pltpu.CompilerParams(vmem_limit_bytes=6 * 2**20),
+    )(own, ahead, behind, *([] if out is None else [out]))
+
+
 def ring_order(chips):
     return list(range(0, chips, 2)) + list(range(1, chips, 2))[::-1]
 
@@ -223,11 +242,10 @@
             give(flows(1, s - 1), k_far)
         give(flows(0, s), *([back[f] for f in groups[1]] if s == 1 else []))
     compute([(0, 0, 0), (0, 1, 0)], pack([tokens], [tail], 0), worked[-1])
-    out = [
-        (done[0, h, 0] + back[0, h].astype(jnp.float32) + back[1, h].astype(jnp.float32)).astype(jnp.bfloat16)
-        for h in range(2)
-    ]
-    return jnp.concatenate(out, axis=0)
+    out = None
+    for h in range(2):
+        out = finish(h, out, done[0, h, 0], back[0, h], back[1, h])
+    return out
 
 
 def solution(mesh):

time: 92.6 us -> 92.5 us (level)
  Pallas kernels: 24.7 us -> 26.3 us
  other arithmetic: 2.35 us -> 1.38 us
    pallas_call x0 -> x2, Pallas kernels: none -> 1.56 us  [finish(): pl.pallas_call(finish_kernel, grid=(1,), in_specs=[near] * 3 + ([] if out...]
  transfers between devices with their start and end apart: 31 -> 31, of which waited for: 18 -> 19; matrix products, arithmetic and copies ran while one was open for 1% -> 1% of each run, Pallas kernels for 27% -> 28%
where the time goes in v7:
time: 92.5 us; the launch traced here: 92.2 us
  starting transfers between devices  30.8 us (33%)
  waiting for transfers between devices  27.9 us (30%)
  Pallas kernels  26.3 us (28%)
  local copies, waits for them, and re-layouts  5.68 us (6%)
  other arithmetic  1.38 us (1%)
    pallas_call x8, Pallas kernels, ffn(): pl.pallas_call(functools.partial(ffn_kernel, n_in, n_out, n_dev), in_spec...  23.7 us
    ppermute x14, waiting for transfers between devices, give(): back[d, h] = lax.ppermute(part, 'ep', perm[1 - d])  15.7 us
    ppermute x14, starting transfers between devices, give(): back[d, h] = lax.ppermute(part, 'ep', perm[1 - d])  15 us
    ppermute x10, starting transfers between devices, send(): held[d, h, s] = lax.ppermute(tie(held[d, h, s - 1], *deps), 'ep', perm[d])  10.2 us
    unnamed x12, local copies, waits for them, and re-layouts  5.68 us
    ppermute x10, waiting for transfers between devices, send(): held[d, h, s] = lax.ppermute(tie(held[d, h, s - 1], *deps), 'ep', perm[d])  4.87 us
    ppermute x2, waiting for transfers between devices, on_device(): tails = [lax.ppermute(tail, 'ep', perm[d]) for d in range(2)]  4.51 us
    ppermute x2, starting transfers between devices, on_device(): first = [lax.ppermute(tokens, 'ep', perm[d]) for d in range(2)]  3.03 us
  transfers between devices with their start and end apart: 31, of which 19 were waited for; matrix products, arithmetic and copies ran while one was open for 1% of the time, Pallas kernels for 28%

profile of v7, /device:TPU:0, one launch (start us, length us, event | category | flops | bytes accessed | tf_op | source)
XLA Modules:
  0.0 92.2 jit_solution(18155872859635064976)
XLA Ops:
  0.0 3.0 %collective-permute-start = (bf16[128,2048]{1,0:T(8,128)(2,1)}, bf16[128,2048]{1,0:T(8,128)(2,1)S(1)}, u32[]{:S(2)}, u32[]{:S(2)}) collective-permute-start(bf16[128,2048]{1,0:T(8,128)(2,1)} %refs_0_.2), channel_id=1, source_target_pairs={{0,8},{2,10},{8,16},{10,18},{16,24},{18,26},{24,28},{26,30},{28,20... | collective-permute-start | bytes 1572872 | tf_op jit(solution)/shard_map/ppermute | solution.py:186
  3.0 0.8 select_reduce_fusion.scores_ref
  3.8 0.1 shard_map.73.refs_1_
  3.9 2.0 %collective-permute-start.2 = (bf16[32,128]{1,0:T(8,128)(2,1)S(1)}, bf16[32,128]{1,0:T(8,128)(2,1)S(1)}, u32[]{:S(2)}, u32[]{:S(2)}) collective-permute-start(bf16[32,128]{1,0:T(8,128)(2,1)S(1)} %shard_map.73.refs_1_), channel_id=1, source_target_pairs={{0,8},{2,10},{8,16},{10,18},{16,24},{18,26},{24,28},{26,30},{28,20... | collective-permute-start | bytes 24584 | tf_op jit(solution)/shard_map/ppermute | solution.py:188
  5.9 1.9 %copy-done = bf16[1,2048,768]{2,1,0:T(8,128)(2,1)S(1)} copy-done((bf16[1,2048,768]{2,1,0:T(8,128)(2,1)S(1)}, bf16[1,2048,768]{2,1,0:T(8,128)(2,1)}, u32[]{:S(2)}) %copy-start) | copy-done | bytes 3145752
  7.8 1.9 %copy-done.1 = bf16[1,2048,768]{2,1,0:T(8,128)(2,1)S(1)} copy-done((bf16[1,2048,768]{2,1,0:T(8,128)(2,1)S(1)}, bf16[1,2048,768]{2,1,0:T(8,128)(2,1)}, u32[]{:S(2)}) %copy-start.1) | copy-done | bytes 3145752
  9.7 1.9 %copy-done.3 = bf16[1,768,2048]{2,1,0:T(8,128)(2,1)S(1)} copy-done((bf16[1,768,2048]{2,1,0:T(8,128)(2,1)S(1)}, bf16[1,768,2048]{2,1,0:T(8,128)(2,1)}, u32[]{:S(2)}) %copy-start.3) | copy-done | bytes 3145752
  11.6 0.7 shard_map.76
  12.3 3.0 %collective-permute-done.2.refs_2_ = bf16[32,128]{1,0:T(8,128)(2,1)S(1)} collective-permute-done((bf16[32,128]{1,0:T(8,128)(2,1)S(1)}, bf16[32,128]{1,0:T(8,128)(2,1)S(1)}, u32[]{:S(2)}, u32[]{:S(2)}) %collective-permute-start.2) | collective-permute-done | bytes 8224 | tf_op jit(solution)/shard_map/ppermute | solution.py:188
  15.2 1.5 %collective-permute-done.3.refs_3_ = bf16[32,128]{1,0:T(8,128)(2,1)S(1)} collective-permute-done((bf16[32,128]{1,0:T(8,128)(2,1)S(1)}, bf16[32,128]{1,0:T(8,128)(2,1)S(1)}, u32[]{:S(2)}, u32[]{:S(2)}) %collective-permute-start.3) | collective-permute-done | bytes 8224 | tf_op jit(solution)/shard_map/ppermute | solution.py:188
  16.8 0.5 collective-permute-start.9
  17.3 0.2 shard_map.75
  17.5 0.4 collective-permute-start.7
  17.9 1.7 %collective-permute-start.5 = (bf16[1040,128]{1,0:T(8,128)(2,1)S(1)}, bf16[1040,128]{1,0:T(8,128)(2,1)S(1)}, u32[]{:S(2)}, u32[]{:S(2)}) collective-permute-start(bf16[1040,128]{1,0:T(8,128)(2,1)S(1)} %get-tuple-element.95.refs_0_), channel_id=1, source_target_pairs={{0,8},{2,10},{8,16},{10,18},{16,24},{18,26},{24,28},{26,30},{28,20... | collective-permute-start | bytes 798728 | tf_op jit(solution)/shard_map/ppermute | solution.py:203
  19.6 2.9 %collective-permute-done.8.refs_6_ = bf16[1,2048,768]{2,1,0:T(8,128)(2,1)S(1)} collective-permute-done((bf16[1,2048,768]{2,1,0:T(8,128)(2,1)S(1)}, bf16[1,2048,768]{2,1,0:T(8,128)(2,1)S(1)}, u32[]{:S(2)}, u32[]{:S(2)}) %collective-permute-start.8) | collective-permute-done | bytes 3145760 | tf_op jit(solution)/shard_map/ppermute | solution.py:189
  22.5 0.3 collective-permute-start.13
  22.8 1.7 %collective-permute-start.15 = (bf16[1040,128]{1,0:T(8,128)(2,1)S(1)}, bf16[1040,128]{1,0:T(8,128)(2,1)S(1)}, u32[]{:S(2)}, u32[]{:S(2)}) collective-permute-start(bf16[1040,128]{1,0:T(8,128)(2,1)S(1)} %get-tuple-element.93.refs_1_), channel_id=1, source_target_pairs={{0,8},{2,10},{8,16},{10,18},{16,24},{18,26},{24,28},{26,30},{28,20... | collective-permute-start | bytes 798728 | tf_op jit(solution)/shard_map/ppermute | solution.py:203
  24.5 2.1 %collective-permute-done.7.refs_1_ = bf16[1040,128]{1,0:T(8,128)(2,1)S(1)} collective-permute-done((bf16[1040,128]{1,0:T(8,128)(2,1)S(1)}, bf16[1040,128]{1,0:T(8,128)(2,1)S(1)}, u32[]{:S(2)}, u32[]{:S(2)}) %collective-permute-start.7) | collective-permute-done | bytes 266272 | tf_op jit(solution)/shard_map/ppermute | solution.py:203
  26.6 0.3 collective-permute-start.11
  26.9 1.7 %collective-permute-start.6 = (bf16[1040,128]{1,0:T(8,128)(2,1)S(1)}, bf16[1040,128]{1,0:T(8,128)(2,1)S(1)}, u32[]{:S(2)}, u32[]{:S(2)}) collective-permute-start(bf16[1040,128]{1,0:T(8,128)(2,1)S(1)} %collective-permute-done.5.refs_0_), channel_id=1, source_target_pairs={{0,8},{2,10},{8,16},{10,18},{16,24},{18,26},{24,28},{26,30},{28,20... | collective-permute-start | bytes 798728 | tf_op jit(solution)/shard_map/ppermute | solution.py:203
  28.6 3.0 %shard_map.77 = (f32[64,2048]{1,0:T(8,128)S(1)}, f32[64,2048]{1,0:T(8,128)S(1)}) custom-call(bf16[1040,128]{1,0:T(8,128)(2,1)S(1)} %collective-permute-done.5.refs_0_, bf16[1040,128]{1,0:T(8,128)(2,1)S(1)} %collective-permute-done.7.refs_1_, bf16[1,2048,768]{2,1,0:T(8,128)(2,1)S(1)} %get-tuple-element.68.refs_2_, ...), custom_call_target="tpu_custom_call" | custom-call | flops 2415919104 | bytes 20447232 | tf_op jit(solution)/shard_map/pallas_call | solution.py:133
  31.6 0.7 collective-permute-done.13.refs_0_
  32.3 0.1 collective-permute-done.15.refs_1_
  32.4 1.6 %collective-permute-start.14 = (bf16[1040,128]{1,0:T(8,128)(2,1)S(1)}, bf16[1040,128]{1,0:T(8,128)(2,1)S(1)}, u32[]{:S(2)}, u32[]{:S(2)}) collective-permute-start(bf16[1040,128]{1,0:T(8,128)(2,1)S(1)} %collective-permute-done.13.refs_0_), channel_id=1, source_target_pairs={{0,4},{2,6},{8,0},{10,2},{16,8},{18,10},{24,16},{26,18},{28,24},{3... | collective-permute-start | bytes 798728 | tf_op jit(solution)/shard_map/ppermute | solution.py:203
  34.0 0.5 collective-permute-start.16
  34.4 3.0 %shard_map.78 = (f32[64,2048]{1,0:T(8,128)S(1)}, f32[64,2048]{1,0:T(8,128)S(1)}) custom-call(bf16[1040,128]{1,0:T(8,128)(2,1)S(1)} %collective-permute-done.13.refs_0_, bf16[1040,128]{1,0:T(8,128)(2,1)S(1)} %collective-permute-done.15.refs_1_, bf16[1,2048,768]{2,1,0:T(8,128)(2,1)S(1)} %get-tuple-element.68.refs_2_, ...), custom_call_target="tpu_custom_call" | custom-call | flops 2415919104 | bytes 20447232 | tf_op jit(solution)/shard_map/pallas_call | solution.py:133
  37.4 0.6 collective-permute-done.11.refs_1_
  38.0 0.1 collective-permute-done.6.refs_0_
  38.1 1.6 %collective-permute-start.12 = (bf16[1040,128]{1,0:T(8,128)(2,1)S(1)}, bf16[1040,128]{1,0:T(8,128)(2,1)S(1)}, u32[]{:S(2)}, u32[]{:S(2)}) collective-permute-start(bf16[1040,128]{1,0:T(8,128)(2,1)S(1)} %collective-permute-done.11.refs_1_), channel_id=1, source_target_pairs={{0,4},{2,6},{8,0},{10,2},{16,8},{18,10},{24,16},{26,18},{28,24},{3... | collective-permute-start | bytes 798728 | tf_op jit(solution)/shard_map/ppermute | solution.py:203
  39.7 0.5 collective-permute-start.10
  40.1 3.0 %shard_map.79 = (f32[64,2048]{1,0:T(8,128)S(1)}, f32[64,2048]{1,0:T(8,128)S(1)}) custom-call(bf16[1040,128]{1,0:T(8,128)(2,1)S(1)} %collective-permute-done.6.refs_0_, bf16[1040,128]{1,0:T(8,128)(2,1)S(1)} %collective-permute-done.11.refs_1_, bf16[1,2048,768]{2,1,0:T(8,128)(2,1)S(1)} %get-tuple-element.68.refs_2_, ...), custom_call_target="tpu_custom_call" | custom-call | flops 2415919104 | bytes 20447232 | tf_op jit(solution)/shard_map/pallas_call | solution.py:133
  43.1 0.6 collective-permute-done.14.refs_0_
  43.7 0.1 collective-permute-done.16.refs_1_
  43.8 3.0 %shard_map.80 = (bf16[64,2048]{1,0:T(8,128)(2,1)S(1)}, bf16[64,2048]{1,0:T(8,128)(2,1)S(1)}) custom-call(bf16[1040,128]{1,0:T(8,128)(2,1)S(1)} %collective-permute-done.14.refs_0_, bf16[1040,128]{1,0:T(8,128)(2,1)S(1)} %collective-permute-done.16.refs_1_, bf16[1,2048,768]{2,1,0:T(8,128)(2,1)S(1)} %get-tuple-element.68.refs_2_, ...), custom_call_target="tpu_custom_call" | custom-call | flops 2415919104 | bytes 20447232 | tf_op jit(solution)/shard_map/pallas_call | solution.py:133
  46.8 1.7 %collective-permute-start.17 = (bf16[64,2048]{1,0:T(8,128)(2,1)S(1)}, bf16[64,2048]{1,0:T(8,128)(2,1)S(1)}, u32[]{:S(2)}, u32[]{:S(2)}) collective-permute-start(bf16[64,2048]{1,0:T(8,128)(2,1)S(1)} %get-tuple-element.88), channel_id=1, source_target_pairs={{0,8},{2,10},{8,16},{10,18},{16,24},{18,26},{24,28},{26,30},{28,20... | collective-permute-start | bytes 786440 | tf_op jit(solution)/shard_map/ppermute | solution.py:236
  48.5 0.4 collective-permute-start.18
  48.9 0.5 collective-permute-done.10.refs_0_
  49.4 3.0 %shard_map.81 = (bf16[64,2048]{1,0:T(8,128)(2,1)S(1)}, bf16[64,2048]{1,0:T(8,128)(2,1)S(1)}) custom-call(bf16[1040,128]{1,0:T(8,128)(2,1)S(1)} %collective-permute-done.10.refs_0_, bf16[1040,128]{1,0:T(8,128)(2,1)S(1)} %collective-permute-done.12.refs_1_, bf16[1,2048,768]{2,1,0:T(8,128)(2,1)S(1)} %get-tuple-element.68.refs_2_, ...), custom_call_target="tpu_custom_call" | custom-call | flops 2415919104 | bytes 20447232 | tf_op jit(solution)/shard_map/pallas_call | solution.py:133
  52.4 1.6 %collective-permute-start.22 = (bf16[64,2048]{1,0:T(8,128)(2,1)S(1)}, bf16[64,2048]{1,0:T(8,128)(2,1)S(1)}, u32[]{:S(2)}, u32[]{:S(2)}) collective-permute-start(bf16[64,2048]{1,0:T(8,128)(2,1)S(1)} %get-tuple-element.91), channel_id=1, source_target_pairs={{0,4},{2,6},{8,0},{10,2},{16,8},{18,10},{24,16},{26,18},{28,24},{3... | collective-permute-start | bytes 786440 | tf_op jit(solution)/shard_map/ppermute | solution.py:236
  54.0 0.5 collective-permute-start.23
  54.5 3.0 %shard_map.82 = (f32[64,2048]{1,0:T(8,128)S(1)}, f32[64,2048]{1,0:T(8,128)S(1)}) custom-call(bf16[1040,128]{1,0:T(8,128)(2,1)S(1)} %get-tuple-element.92.refs_0_, bf16[1040,128]{1,0:T(8,128)(2,1)S(1)} %get-tuple-element.93.refs_1_, bf16[1,2048,768]{2,1,0:T(8,128)(2,1)S(1)} %get-tuple-element.68.refs_2_, bf16[1,2048,768]{2,1,0:T(8,128)(2,1)S(1)} %get-tuple-element.69.refs_3_, ...), custom_call_target="tpu_custom_call" | custom-call | flops 2415919104 | bytes 20447232 | tf_op jit(solution)/shard_map/pallas_call | solution.py:133
  57.5 1.6 %collective-permute-start.20 = (bf16[64,2048]{1,0:T(8,128)(2,1)S(1)}, bf16[64,2048]{1,0:T(8,128)(2,1)S(1)}, u32[]{:S(2)}, u32[]{:S(2)}) collective-permute-start(bf16[64,2048]{1,0:T(8,128)(2,1)S(1)} %add_convert_fusion.8), channel_id=1, source_target_pairs={{0,4},{2,6},{8,0},{10,2},{16,8},{18,10},{24,16},{26,18},{28,24},{3... | collective-permute-start | bytes 786440 | tf_op jit(solution)/shard_map/ppermute | solution.py:236
  59.2 0.5 collective-permute-start.19
  59.7 2.3 %collective-permute-done.22 = bf16[64,2048]{1,0:T(8,128)(2,1)S(1)} collective-permute-done((bf16[64,2048]{1,0:T(8,128)(2,1)S(1)}, bf16[64,2048]{1,0:T(8,128)(2,1)S(1)}, u32[]{:S(2)}, u32[]{:S(2)}) %collective-permute-start.22) | collective-permute-done | bytes 262176 | tf_op jit(solution)/shard_map/ppermute | solution.py:236
  62.1 1.5 %collective-permute-start.25 = (bf16[64,2048]{1,0:T(8,128)(2,1)S(1)}, bf16[64,2048]{1,0:T(8,128)(2,1)S(1)}, u32[]{:S(2)}, u32[]{:S(2)}) collective-permute-start(bf16[64,2048]{1,0:T(8,128)(2,1)S(1)} %add_convert_fusion.5), channel_id=1, source_target_pairs={{0,8},{2,10},{8,16},{10,18},{16,24},{18,26},{24,28},{26,30},{28,20... | collective-permute-start | bytes 786440 | tf_op jit(solution)/shard_map/ppermute | solution.py:236
  63.7 0.8 collective-permute-start.24
  64.6 3.1 %collective-permute-done.20 = bf16[64,2048]{1,0:T(8,128)(2,1)S(1)} collective-permute-done((bf16[64,2048]{1,0:T(8,128)(2,1)S(1)}, bf16[64,2048]{1,0:T(8,128)(2,1)S(1)}, u32[]{:S(2)}, u32[]{:S(2)}) %collective-permute-start.20) | collective-permute-done | bytes 262176 | tf_op jit(solution)/shard_map/ppermute | solution.py:236
  67.7 0.8 collective-permute-done.19
  68.6 0.7 collective-permute-start.28
  69.3 1.4 %collective-permute-start.21 = (bf16[64,2048]{1,0:T(8,128)(2,1)S(1)}, bf16[64,2048]{1,0:T(8,128)(2,1)S(1)}, u32[]{:S(2)}, u32[]{:S(2)}) collective-permute-start(bf16[64,2048]{1,0:T(8,128)(2,1)S(1)} %add_convert_fusion.7), channel_id=1, source_target_pairs={{0,4},{2,6},{8,0},{10,2},{16,8},{18,10},{24,16},{26,18},{28,24},{3... | collective-permute-start | bytes 786440 | tf_op jit(solution)/shard_map/ppermute | solution.py:236
  70.8 3.4 %collective-permute-done.25 = bf16[64,2048]{1,0:T(8,128)(2,1)S(1)} collective-permute-done((bf16[64,2048]{1,0:T(8,128)(2,1)S(1)}, bf16[64,2048]{1,0:T(8,128)(2,1)S(1)}, u32[]{:S(2)}, u32[]{:S(2)}) %collective-permute-start.25) | collective-permute-done | bytes 262176 | tf_op jit(solution)/shard_map/ppermute | solution.py:236
  74.2 0.7 collective-permute-start.27
  75.0 1.4 %collective-permute-start.26 = (bf16[64,2048]{1,0:T(8,128)(2,1)S(1)}, bf16[64,2048]{1,0:T(8,128)(2,1)S(1)}, u32[]{:S(2)}, u32[]{:S(2)}) collective-permute-start(bf16[64,2048]{1,0:T(8,128)(2,1)S(1)} %add_convert_fusion.4), channel_id=1, source_target_pairs={{0,4},{2,6},{8,0},{10,2},{16,8},{18,10},{24,16},{26,18},{28,24},{3... | collective-permute-start | bytes 786440 | tf_op jit(solution)/shard_map/ppermute | solution.py:236
  76.4 3.0 %shard_map.83 = (f32[64,2048]{1,0:T(8,128)S(1)}, f32[64,2048]{1,0:T(8,128)S(1)}) custom-call(bf16[1040,128]{1,0:T(8,128)(2,1)S(1)} %get-tuple-element.95.refs_0_, bf16[1040,128]{1,0:T(8,128)(2,1)S(1)} %get-tuple-element.96.refs_1_, bf16[1,2048,768]{2,1,0:T(8,128)(2,1)S(1)} %get-tuple-element.68.refs_2_, bf16[1,2048,768]{2,1,0:T(8,128)(2,1)S(1)} %get-tuple-element.69.refs_3_, ...), custom_call_target="tpu_custom_call" | custom-call | flops 2415919104 | bytes 20447232 | tf_op jit(solution)/shard_map/pallas_call | solution.py:133
  79.4 0.4 collective-permute-done.28.behind_ref
  79.8 3.5 %collective-permute-done.27 = bf16[64,2048]{1,0:T(8,128)(2,1)S(1)} collective-permute-done((bf16[64,2048]{1,0:T(8,128)(2,1)S(1)}, bf16[64,2048]{1,0:T(8,128)(2,1)S(1)}, u32[]{:S(2)}, u32[]{:S(2)}) %collective-permute-start.27) | collective-permute-done | bytes 262176 | tf_op jit(solution)/shard_map/ppermute | solution.py:236
  83.4 1.6 %collective-permute-start.30 = (bf16[64,2048]{1,0:T(8,128)(2,1)S(1)}, bf16[64,2048]{1,0:T(8,128)(2,1)S(1)}, u32[]{:S(2)}, u32[]{:S(2)}) collective-permute-start(bf16[64,2048]{1,0:T(8,128)(2,1)S(1)} %add_convert_fusion), channel_id=1, source_target_pairs={{0,4},{2,6},{8,0},{10,2},{16,8},{18,10},{24,16},{26,18},{28,24},{3... | collective-permute-start | bytes 786440 | tf_op jit(solution)/shard_map/ppermute | solution.py:236
  85.0 0.5 collective-permute-start.29
  85.6 0.1 shard_map.74
  85.6 3.0 %shard_map.84 = (f32[64,2048]{1,0:T(8,128)S(1)}, f32[64,2048]{1,0:T(8,128)S(1)}) custom-call(bf16[1040,128]{1,0:T(8,128)(2,1)S(1)} %get-tuple-element.98.refs_0_, bf16[1040,128]{1,0:T(8,128)(2,1)S(1)} %get-tuple-element.99.refs_1_, bf16[1,2048,768]{2,1,0:T(8,128)(2,1)S(1)} %get-tuple-element.68.refs_2_, bf16[1,2048,768]{2,1,0:T(8,128)(2,1)S(1)} %get-tuple-element.69.refs_3_, ...), custom_call_target="tpu_custom_call" | custom-call | flops 2415919104 | bytes 20447232 | tf_op jit(solution)/shard_map/pallas_call | solution.py:133
  88.6 1.8 %collective-permute-done.30.ahead_ref = bf16[64,2048]{1,0:T(8,128)(2,1)S(1)} collective-permute-done((bf16[64,2048]{1,0:T(8,128)(2,1)S(1)}, bf16[64,2048]{1,0:T(8,128)(2,1)S(1)}, u32[]{:S(2)}, u32[]{:S(2)}) %collective-permute-start.30) | collective-permute-done | bytes 262176 | tf_op jit(solution)/shard_map/ppermute | solution.py:236
  90.5 0.8 shard_map.85.refs_0_
  91.2 0.2 collective-permute-done.29.behind_ref
  91.5 0.8 shard_map.86
  (35 shorter events, 0.6 us)
Async XLA Ops:
  0.0 17.3 %collective-permute-start = (bf16[128,2048]{1,0:T(8,128)(2,1)}, bf16[128,2048]{1,0:T(8,128)(2,1)S(1)}, u32[]{:S(2)}, u32[]{:S(2)}) collective-permute-start(bf16[128,2048]{1,0:T(8,128)(2,1)} %refs_0_.2), channel_id=1, source_target_pairs={{0,8},{2,10},{8,16},{10,18},{16,24},{18,26},{24,28},{26,30},{28,20... | collective-permute-start | bytes 1572872 | tf_op jit(solution)/shard_map/ppermute | solution.py:186
  3.0 14.3 %collective-permute-start.1 = (bf16[128,2048]{1,0:T(8,128)(2,1)}, bf16[128,2048]{1,0:T(8,128)(2,1)S(1)}, u32[]{:S(2)}, u32[]{:S(2)}) collective-permute-start(bf16[128,2048]{1,0:T(8,128)(2,1)} %refs_0_.2), channel_id=1, source_target_pairs={{0,4},{2,6},{8,0},{10,2},{16,8},{18,10},{24,16},{26,18},{28,24},{3... | collective-permute-start | bytes 1572872 | tf_op jit(solution)/shard_map/ppermute | solution.py:186
  3.9 11.3 %collective-permute-start.2 = (bf16[32,128]{1,0:T(8,128)(2,1)S(1)}, bf16[32,128]{1,0:T(8,128)(2,1)S(1)}, u32[]{:S(2)}, u32[]{:S(2)}) collective-permute-start(bf16[32,128]{1,0:T(8,128)(2,1)S(1)} %shard_map.73.refs_1_), channel_id=1, source_target_pairs={{0,8},{2,10},{8,16},{10,18},{16,24},{18,26},{24,28},{26,30},{28,20... | collective-permute-start | bytes 24584 | tf_op jit(solution)/shard_map/ppermute | solution.py:188
  5.9 10.9 %collective-permute-start.3 = (bf16[32,128]{1,0:T(8,128)(2,1)S(1)}, bf16[32,128]{1,0:T(8,128)(2,1)S(1)}, u32[]{:S(2)}, u32[]{:S(2)}) collective-permute-start(bf16[32,128]{1,0:T(8,128)(2,1)S(1)} %shard_map.73.refs_1_), channel_id=1, source_target_pairs={{0,4},{2,6},{8,0},{10,2},{16,8},{18,10},{24,16},{26,18},{28,24},{3... | collective-permute-start | bytes 24584 | tf_op jit(solution)/shard_map/ppermute | solution.py:188
  5.9 11.6 %collective-permute-start.4 = (bf16[1,2048,768]{2,1,0:T(8,128)(2,1)}, bf16[1,2048,768]{2,1,0:T(8,128)(2,1)S(1)}, u32[]{:S(2)}, u32[]{:S(2)}) collective-permute-start(bf16[1,2048,768]{2,1,0:T(8,128)(2,1)} %refs_0_.3), channel_id=1, source_target_pairs={{0,2},{2,0},{4,6},{6,4},{8,10},{10,8},{12,14},{14,12},{16,18},{18,... | collective-permute-start | bytes 9437192 | tf_op jit(solution)/shard_map/ppermute | solution.py:189
  5.9 1.9 %copy-start = (bf16[1,2048,768]{2,1,0:T(8,128)(2,1)S(1)}, bf16[1,2048,768]{2,1,0:T(8,128)(2,1)}, u32[]{:S(2)}) copy-start(bf16[1,2048,768]{2,1,0:T(8,128)(2,1)} %refs_0_.3) | copy-start | bytes 9437188
  7.8 1.9 %copy-start.1 = (bf16[1,2048,768]{2,1,0:T(8,128)(2,1)S(1)}, bf16[1,2048,768]{2,1,0:T(8,128)(2,1)}, u32[]{:S(2)}) copy-start(bf16[1,2048,768]{2,1,0:T(8,128)(2,1)} %refs_1_.1) | copy-start | bytes 9437188
  9.7 1.9 %copy-start.3 = (bf16[1,768,2048]{2,1,0:T(8,128)(2,1)S(1)}, bf16[1,768,2048]{2,1,0:T(8,128)(2,1)}, u32[]{:S(2)}) copy-start(bf16[1,768,2048]{2,1,0:T(8,128)(2,1)} %refs_2_.1) | copy-start | bytes 9437188
  11.6 5.2 %copy-start.2 = (bf16[1,2048,768]{2,1,0:T(8,128)(2,1)S(1)}, bf16[1,2048,768]{2,1,0:T(8,128)(2,1)}, u32[]{:S(2)}) copy-start(bf16[1,2048,768]{2,1,0:T(8,128)(2,1)} %refs_1_.1) | copy-start | bytes 9437188
  11.6 5.2 %copy-start.4 = (bf16[1,768,2048]{2,1,0:T(8,128)(2,1)S(1)}, bf16[1,768,2048]{2,1,0:T(8,128)(2,1)}, u32[]{:S(2)}) copy-start(bf16[1,768,2048]{2,1,0:T(8,128)(2,1)} %refs_2_.1) | copy-start | bytes 9437188
  16.8 5.7 %collective-permute-start.8 = (bf16[1,2048,768]{2,1,0:T(8,128)(2,1)S(1)}, bf16[1,2048,768]{2,1,0:T(8,128)(2,1)S(1)}, u32[]{:S(2)}, u32[]{:S(2)}) collective-permute-start(bf16[1,2048,768]{2,1,0:T(8,128)(2,1)S(1)} %copy-done.2), channel_id=1, source_target_pairs={{0,2},{2,0},{4,6},{6,4},{8,10},{10,8},{12,14},{14,12},{16,18},{18,... | collective-permute-start | bytes 9437192 | tf_op jit(solution)/shard_map/ppermute | solution.py:189
  16.8 11.8 %collective-permute-start.9 = (bf16[1,768,2048]{2,1,0:T(8,128)(2,1)S(1)}, bf16[1,768,2048]{2,1,0:T(8,128)(2,1)S(1)}, u32[]{:S(2)}, u32[]{:S(2)}) collective-permute-start(bf16[1,768,2048]{2,1,0:T(8,128)(2,1)S(1)} %copy-done.4), channel_id=1, source_target_pairs={{0,2},{2,0},{4,6},{6,4},{8,10},{10,8},{12,14},{14,12},{16,18},{18,... | collective-permute-start | bytes 9437192 | tf_op jit(solution)/shard_map/ppermute | solution.py:189
  17.5 9.1 %collective-permute-start.7 = (bf16[1040,128]{1,0:T(8,128)(2,1)S(1)}, bf16[1040,128]{1,0:T(8,128)(2,1)S(1)}, u32[]{:S(2)}, u32[]{:S(2)}) collective-permute-start(bf16[1040,128]{1,0:T(8,128)(2,1)S(1)} %get-tuple-element.96.refs_1_), channel_id=1, source_target_pairs={{0,4},{2,6},{8,0},{10,2},{16,8},{18,10},{24,16},{26,18},{28,24},{3... | collective-permute-start | bytes 798728 | tf_op jit(solution)/shard_map/ppermute | solution.py:203
  17.9 9.0 %collective-permute-start.5 = (bf16[1040,128]{1,0:T(8,128)(2,1)S(1)}, bf16[1040,128]{1,0:T(8,128)(2,1)S(1)}, u32[]{:S(2)}, u32[]{:S(2)}) collective-permute-start(bf16[1040,128]{1,0:T(8,128)(2,1)S(1)} %get-tuple-element.95.refs_0_), channel_id=1, source_target_pairs={{0,8},{2,10},{8,16},{10,18},{16,24},{18,26},{24,28},{26,30},{28,20... | collective-permute-start | bytes 798728 | tf_op jit(solution)/shard_map/ppermute | solution.py:203
  22.5 9.9 %collective-permute-start.13 = (bf16[1040,128]{1,0:T(8,128)(2,1)S(1)}, bf16[1040,128]{1,0:T(8,128)(2,1)S(1)}, u32[]{:S(2)}, u32[]{:S(2)}) collective-permute-start(bf16[1040,128]{1,0:T(8,128)(2,1)S(1)} %get-tuple-element.92.refs_0_), channel_id=1, source_target_pairs={{0,4},{2,6},{8,0},{10,2},{16,8},{18,10},{24,16},{26,18},{28,24},{3... | collective-permute-start | bytes 798728 | tf_op jit(solution)/shard_map/ppermute | solution.py:203
  22.8 9.6 %collective-permute-start.15 = (bf16[1040,128]{1,0:T(8,128)(2,1)S(1)}, bf16[1040,128]{1,0:T(8,128)(2,1)S(1)}, u32[]{:S(2)}, u32[]{:S(2)}) collective-permute-start(bf16[1040,128]{1,0:T(8,128)(2,1)S(1)} %get-tuple-element.93.refs_1_), channel_id=1, source_target_pairs={{0,8},{2,10},{8,16},{10,18},{16,24},{18,26},{24,28},{26,30},{28,20... | collective-permute-start | bytes 798728 | tf_op jit(solution)/shard_map/ppermute | solution.py:203
  26.6 11.4 %collective-permute-start.11 = (bf16[1040,128]{1,0:T(8,128)(2,1)S(1)}, bf16[1040,128]{1,0:T(8,128)(2,1)S(1)}, u32[]{:S(2)}, u32[]{:S(2)}) collective-permute-start(bf16[1040,128]{1,0:T(8,128)(2,1)S(1)} %collective-permute-done.7.refs_1_), channel_id=1, source_target_pairs={{0,4},{2,6},{8,0},{10,2},{16,8},{18,10},{24,16},{26,18},{28,24},{3... | collective-permute-start | bytes 798728 | tf_op jit(solution)/shard_map/ppermute | solution.py:203
  26.9 11.2 %collective-permute-start.6 = (bf16[1040,128]{1,0:T(8,128)(2,1)S(1)}, bf16[1040,128]{1,0:T(8,128)(2,1)S(1)}, u32[]{:S(2)}, u32[]{:S(2)}) collective-permute-start(bf16[1040,128]{1,0:T(8,128)(2,1)S(1)} %collective-permute-done.5.refs_0_), channel_id=1, source_target_pairs={{0,8},{2,10},{8,16},{10,18},{16,24},{18,26},{24,28},{26,30},{28,20... | collective-permute-start | bytes 798728 | tf_op jit(solution)/shard_map/ppermute | solution.py:203
  32.4 11.3 %collective-permute-start.14 = (bf16[1040,128]{1,0:T(8,128)(2,1)S(1)}, bf16[1040,128]{1,0:T(8,128)(2,1)S(1)}, u32[]{:S(2)}, u32[]{:S(2)}) collective-permute-start(bf16[1040,128]{1,0:T(8,128)(2,1)S(1)} %collective-permute-done.13.refs_0_), channel_id=1, source_target_pairs={{0,4},{2,6},{8,0},{10,2},{16,8},{18,10},{24,16},{26,18},{28,24},{3... | collective-permute-start | bytes 798728 | tf_op jit(solution)/shard_map/ppermute | solution.py:203
  34.0 9.8 %collective-permute-start.16 = (bf16[1040,128]{1,0:T(8,128)(2,1)S(1)}, bf16[1040,128]{1,0:T(8,128)(2,1)S(1)}, u32[]{:S(2)}, u32[]{:S(2)}) collective-permute-start(bf16[1040,128]{1,0:T(8,128)(2,1)S(1)} %collective-permute-done.15.refs_1_), channel_id=1, source_target_pairs={{0,8},{2,10},{8,16},{10,18},{16,24},{18,26},{24,28},{26,30},{28,20... | collective-permute-start | bytes 798728 | tf_op jit(solution)/shard_map/ppermute | solution.py:203
  38.1 10.8 %collective-permute-start.12 = (bf16[1040,128]{1,0:T(8,128)(2,1)S(1)}, bf16[1040,128]{1,0:T(8,128)(2,1)S(1)}, u32[]{:S(2)}, u32[]{:S(2)}) collective-permute-start(bf16[1040,128]{1,0:T(8,128)(2,1)S(1)} %collective-permute-done.11.refs_1_), channel_id=1, source_target_pairs={{0,4},{2,6},{8,0},{10,2},{16,8},{18,10},{24,16},{26,18},{28,24},{3... | collective-permute-start | bytes 798728 | tf_op jit(solution)/shard_map/ppermute | solution.py:203
  39.7 9.7 %collective-permute-start.10 = (bf16[1040,128]{1,0:T(8,128)(2,1)S(1)}, bf16[1040,128]{1,0:T(8,128)(2,1)S(1)}, u32[]{:S(2)}, u32[]{:S(2)}) collective-permute-start(bf16[1040,128]{1,0:T(8,128)(2,1)S(1)} %collective-permute-done.6.refs_0_), channel_id=1, source_target_pairs={{0,8},{2,10},{8,16},{10,18},{16,24},{18,26},{24,28},{26,30},{28,20... | collective-permute-start | bytes 798728 | tf_op jit(solution)/shard_map/ppermute | solution.py:203
  46.8 10.7 %collective-permute-start.17 = (bf16[64,2048]{1,0:T(8,128)(2,1)S(1)}, bf16[64,2048]{1,0:T(8,128)(2,1)S(1)}, u32[]{:S(2)}, u32[]{:S(2)}) collective-permute-start(bf16[64,2048]{1,0:T(8,128)(2,1)S(1)} %get-tuple-element.88), channel_id=1, source_target_pairs={{0,8},{2,10},{8,16},{10,18},{16,24},{18,26},{24,28},{26,30},{28,20... | collective-permute-start | bytes 786440 | tf_op jit(solution)/shard_map/ppermute | solution.py:236
  48.5 9.0 %collective-permute-start.18 = (bf16[64,2048]{1,0:T(8,128)(2,1)S(1)}, bf16[64,2048]{1,0:T(8,128)(2,1)S(1)}, u32[]{:S(2)}, u32[]{:S(2)}) collective-permute-start(bf16[64,2048]{1,0:T(8,128)(2,1)S(1)} %get-tuple-element.101), channel_id=1, source_target_pairs={{0,4},{2,6},{8,0},{10,2},{16,8},{18,10},{24,16},{26,18},{28,24},{3... | collective-permute-start | bytes 786440 | tf_op jit(solution)/shard_map/ppermute | solution.py:236
  52.4 9.7 %collective-permute-start.22 = (bf16[64,2048]{1,0:T(8,128)(2,1)S(1)}, bf16[64,2048]{1,0:T(8,128)(2,1)S(1)}, u32[]{:S(2)}, u32[]{:S(2)}) collective-permute-start(bf16[64,2048]{1,0:T(8,128)(2,1)S(1)} %get-tuple-element.91), channel_id=1, source_target_pairs={{0,4},{2,6},{8,0},{10,2},{16,8},{18,10},{24,16},{26,18},{28,24},{3... | collective-permute-start | bytes 786440 | tf_op jit(solution)/shard_map/ppermute | solution.py:236
  54.0 8.0 %collective-permute-start.23 = (bf16[64,2048]{1,0:T(8,128)(2,1)S(1)}, bf16[64,2048]{1,0:T(8,128)(2,1)S(1)}, u32[]{:S(2)}, u32[]{:S(2)}) collective-permute-start(bf16[64,2048]{1,0:T(8,128)(2,1)S(1)} %get-tuple-element.107), channel_id=1, source_target_pairs={{0,8},{2,10},{8,16},{10,18},{16,24},{18,26},{24,28},{26,30},{28,20... | collective-permute-start | bytes 786440 | tf_op jit(solution)/shard_map/ppermute | solution.py:236
  57.5 10.2 %collective-permute-start.20 = (bf16[64,2048]{1,0:T(8,128)(2,1)S(1)}, bf16[64,2048]{1,0:T(8,128)(2,1)S(1)}, u32[]{:S(2)}, u32[]{:S(2)}) collective-permute-start(bf16[64,2048]{1,0:T(8,128)(2,1)S(1)} %add_convert_fusion.8), channel_id=1, source_target_pairs={{0,4},{2,6},{8,0},{10,2},{16,8},{18,10},{24,16},{26,18},{28,24},{3... | collective-permute-start | bytes 786440 | tf_op jit(solution)/shard_map/ppermute | solution.py:236
  59.2 9.3 %collective-permute-start.19 = (bf16[64,2048]{1,0:T(8,128)(2,1)S(1)}, bf16[64,2048]{1,0:T(8,128)(2,1)S(1)}, u32[]{:S(2)}, u32[]{:S(2)}) collective-permute-start(bf16[64,2048]{1,0:T(8,128)(2,1)S(1)} %add_convert_fusion.9), channel_id=1, source_target_pairs={{0,8},{2,10},{8,16},{10,18},{16,24},{18,26},{24,28},{26,30},{28,20... | collective-permute-start | bytes 786440 | tf_op jit(solution)/shard_map/ppermute | solution.py:236
  62.1 12.0 %collective-permute-start.25 = (bf16[64,2048]{1,0:T(8,128)(2,1)S(1)}, bf16[64,2048]{1,0:T(8,128)(2,1)S(1)}, u32[]{:S(2)}, u32[]{:S(2)}) collective-permute-start(bf16[64,2048]{1,0:T(8,128)(2,1)S(1)} %add_convert_fusion.5), channel_id=1, source_target_pairs={{0,8},{2,10},{8,16},{10,18},{16,24},{18,26},{24,28},{26,30},{28,20... | collective-permute-start | bytes 786440 | tf_op jit(solution)/shard_map/ppermute | solution.py:236
  63.7 10.4 %collective-permute-start.24 = (bf16[64,2048]{1,0:T(8,128)(2,1)S(1)}, bf16[64,2048]{1,0:T(8,128)(2,1)S(1)}, u32[]{:S(2)}, u32[]{:S(2)}) collective-permute-start(bf16[64,2048]{1,0:T(8,128)(2,1)S(1)} %add_convert_fusion.6), channel_id=1, source_target_pairs={{0,4},{2,6},{8,0},{10,2},{16,8},{18,10},{24,16},{26,18},{28,24},{3... | collective-permute-start | bytes 786440 | tf_op jit(solution)/shard_map/ppermute | solution.py:236
  68.6 11.2 %collective-permute-start.28 = (bf16[64,2048]{1,0:T(8,128)(2,1)S(1)}, bf16[64,2048]{1,0:T(8,128)(2,1)S(1)}, u32[]{:S(2)}, u32[]{:S(2)}) collective-permute-start(bf16[64,2048]{1,0:T(8,128)(2,1)S(1)} %add_convert_fusion.2), channel_id=1, source_target_pairs={{0,8},{2,10},{8,16},{10,18},{16,24},{18,26},{24,28},{26,30},{28,20... | collective-permute-start | bytes 786440 | tf_op jit(solution)/shard_map/ppermute | solution.py:236
  69.3 10.4 %collective-permute-start.21 = (bf16[64,2048]{1,0:T(8,128)(2,1)S(1)}, bf16[64,2048]{1,0:T(8,128)(2,1)S(1)}, u32[]{:S(2)}, u32[]{:S(2)}) collective-permute-start(bf16[64,2048]{1,0:T(8,128)(2,1)S(1)} %add_convert_fusion.7), channel_id=1, source_target_pairs={{0,4},{2,6},{8,0},{10,2},{16,8},{18,10},{24,16},{26,18},{28,24},{3... | collective-permute-start | bytes 786440 | tf_op jit(solution)/shard_map/ppermute | solution.py:236
  74.2 9.1 %collective-permute-start.27 = (bf16[64,2048]{1,0:T(8,128)(2,1)S(1)}, bf16[64,2048]{1,0:T(8,128)(2,1)S(1)}, u32[]{:S(2)}, u32[]{:S(2)}) collective-permute-start(bf16[64,2048]{1,0:T(8,128)(2,1)S(1)} %add_convert_fusion.3), channel_id=1, source_target_pairs={{0,8},{2,10},{8,16},{10,18},{16,24},{18,26},{24,28},{26,30},{28,20... | collective-permute-start | bytes 786440 | tf_op jit(solution)/shard_map/ppermute | solution.py:236
  75.0 10.6 %copy-start.5 = (bf16[128,2048]{1,0:T(8,128)(2,1)S(1)}, bf16[128,2048]{1,0:T(8,128)(2,1)}, u32[]{:S(2)}) copy-start(bf16[128,2048]{1,0:T(8,128)(2,1)} %refs_0_.2) | copy-start | bytes 1572868
  75.0 8.3 %collective-permute-start.26 = (bf16[64,2048]{1,0:T(8,128)(2,1)S(1)}, bf16[64,2048]{1,0:T(8,128)(2,1)S(1)}, u32[]{:S(2)}, u32[]{:S(2)}) collective-permute-start(bf16[64,2048]{1,0:T(8,128)(2,1)S(1)} %add_convert_fusion.4), channel_id=1, source_target_pairs={{0,4},{2,6},{8,0},{10,2},{16,8},{18,10},{24,16},{26,18},{28,24},{3... | collective-permute-start | bytes 786440 | tf_op jit(solution)/shard_map/ppermute | solution.py:236
  83.4 7.1 %collective-permute-start.30 = (bf16[64,2048]{1,0:T(8,128)(2,1)S(1)}, bf16[64,2048]{1,0:T(8,128)(2,1)S(1)}, u32[]{:S(2)}, u32[]{:S(2)}) collective-permute-start(bf16[64,2048]{1,0:T(8,128)(2,1)S(1)} %add_convert_fusion), channel_id=1, source_target_pairs={{0,4},{2,6},{8,0},{10,2},{16,8},{18,10},{24,16},{26,18},{28,24},{3... | collective-permute-start | bytes 786440 | tf_op jit(solution)/shard_map/ppermute | solution.py:236
  85.0 6.4 %collective-permute-start.29 = (bf16[64,2048]{1,0:T(8,128)(2,1)S(1)}, bf16[64,2048]{1,0:T(8,128)(2,1)S(1)}, u32[]{:S(2)}, u32[]{:S(2)}) collective-permute-start(bf16[64,2048]{1,0:T(8,128)(2,1)S(1)} %add_convert_fusion.1), channel_id=1, source_target_pairs={{0,8},{2,10},{8,16},{10,18},{16,24},{18,26},{24,28},{26,30},{28,20... | collective-permute-start | bytes 786440 | tf_op jit(solution)/shard_map/ppermute | solution.py:236
